TPU v7x, 32 devices: a whole 2x2x4 slice. The times are simulated.
32 devices in a mesh: seq: 8 (over z, x), tp: 4 (over y, core).
Axes of the slice: x: 2, y: 2, z: 4, core: 2. Of those that a mesh axis runs over, the one named last changes fastest.
Arguments:
- tokens: bfloat16 [16, 1024, 768], P(None, 'seq'), may hold values from -6 to 6
- rand_blocks: int32 [16, 16, 12, 3], P(None, None, 'tp'), may hold values from 0 to 15, as said below
- query_weight: bfloat16 [768, 768], P(None, 'tp'), may hold values from -0.21875 to 0.21875
- query_bias: float32 [768], P('tp'), may hold values from -3 to 3
- key_weight: bfloat16 [768, 768], P(None, 'tp'), may hold values from -0.21875 to 0.21875
- value_weight: bfloat16 [768, 768], P(None, 'tp'), may hold values from -0.21875 to 0.21875
- value_bias: float32 [768], P('tp'), may hold values from -1.2 to 1.2
- output_weight: bfloat16 [768, 768], P('tp'), may hold values from -0.875 to 0.875
- output_bias: float32 [768], replicated, may hold values from -1.8 to 1.8
- attn_gain: float32 [768], replicated, may hold values from 0.25 to 1.75
- attn_shift: float32 [768], replicated, may hold values from -1.8 to 1.8
- up_weight: bfloat16 [768, 3072], P(None, 'tp'), may hold values from -0.21875 to 0.21875
- up_bias: float32 [3072], P('tp'), may hold values from -3 to 3
- down_weight: bfloat16 [3072, 768], P('tp'), may hold values from -0.109375 to 0.109375
- down_bias: float32 [768], replicated, may hold values from -1.8 to 1.8
- ffn_gain: float32 [768], replicated, may hold values from 0.25 to 1.75
- ffn_shift: float32 [768], replicated, may hold values from -1.8 to 1.8
- cotangent: bfloat16 [16, 1024, 768], P(None, 'seq'), may hold values from -6 to 6
Outputs:
- layer_output: bfloat16 [16, 1024, 768], P(None, 'seq')
- input_grad: float32 [16, 1024, 768], P(None, 'seq')
- grad_qweight: float32 [768, 768], P(None, 'tp')
- grad_qbias: float32 [768], P('tp')
- grad_kweight: float32 [768, 768], P(None, 'tp')
- grad_vweight: float32 [768, 768], P(None, 'tp')
- grad_vbias: float32 [768], P('tp')
- grad_oweight: float32 [768, 768], P('tp')
- grad_obias: float32 [768], replicated
- grad_attngain: float32 [768], replicated
- grad_attnshift: float32 [768], replicated
- grad_upweight: float32 [768, 3072], P(None, 'tp')
- grad_upbias: float32 [3072], P('tp')
- grad_downweight: float32 [3072, 768], P('tp')
- grad_downbias: float32 [768], replicated
- grad_ffngain: float32 [768], replicated
- grad_ffnshift: float32 [768], replicated
Inputs may be any that keep to these rules, and one draw needn't show every extreme that they name: `rand_blocks`: entries name blocks of the same sequence; the entries of query blocks 0 and 15 are not read. Group the entries by head group (heads g * 3 to (g + 1) * 3 - 1) and by query run (query blocks p * 2 to (p + 1) * 2 - 1, all sequences): in each such group at most 72 entries name blocks of any one key run (blocks o * 2 to (o + 1) * 2 - 1), and one key run is named exactly 72 times by every group.
All inputs are finite; a program needn't handle non-finite values.
Results may differ from a plain program's by a relative error of at most 0.015.
Values may be sent and summed in bfloat16 or wider, within the bound.
A program may use at most 384 MiB of HBM per device.

v0:
```python
import jax
import jax.numpy as jnp
from jax import lax
from jax.sharding import PartitionSpec as P

HD = 64
BLOCK = 64


norm_eps = 1e-06
masked_score = -1e30
highest_precision = lax.Precision.HIGHEST


def with_halo(shard, sides, width):
    for axis, dim in sides:
        size, length = (lax.axis_size(axis), shard.shape[dim])
        up = [(i, (i + 1) % size) for i in range(size - 1)]
        down = [(j, i) for i, j in up]
        last = lax.slice_in_dim(shard, length - width, length, axis=dim)
        first = lax.slice_in_dim(shard, 0, width, axis=dim)
        before = lax.ppermute(last, axis, up)
        after = lax.ppermute(first, axis, down)
        shard = jnp.concatenate([before, shard, after], axis=dim)
    return shard


def joined(shard, axis, combine):
    everything = jax.tree.map(lambda part: lax.all_gather(part, axis), shard)
    first = jax.tree.map(lambda part: part[0], everything)

    def hop(k, so_far):
        return combine(so_far, jax.tree.map(lambda part: part[k], everything))

    return lax.fori_loop(1, lax.axis_size(axis), hop, first)


def layer_norm(resid, gain, shift):
    centre = resid - jnp.mean(resid, -1, keepdims=True)
    spread = jnp.mean(centre * centre, -1, keepdims=True)
    return centre * lax.rsqrt(spread + norm_eps) * gain + shift


def gelu_exact(values):
    return jax.nn.gelu(values, approximate=False)


def plain_dot(left, right):
    return jnp.dot(left, right, preferred_element_type=jnp.float32)


def rows_dot(left, right):
    return lax.dot_general(
        left, right, (((0,), (0,)), ((), ())), preferred_element_type=jnp.float32
    )


def back_dot(left, right):
    return lax.dot_general(
        left, right, (((1,), (1,)), ((), ())), preferred_element_type=jnp.float32
    )


def softmax_row_probs(scores):
    top_score = jnp.max(scores, -1, keepdims=True)
    expo = jnp.exp(scores - top_score)
    return expo / jnp.sum(expo, -1, keepdims=True)


def head_sum_fwd(pieces):
    return lax.psum(pieces, "tp")


def head_sum_back(pieces):
    return lax.psum(pieces, "tp")


def merge_rows(first, second):
    top_score = jnp.maximum(first[0], second[0])
    scale_one = jnp.exp(first[0] - top_score)
    scale_two = jnp.exp(second[0] - top_score)
    return (
        top_score,
        first[1] * scale_one + second[1] * scale_two,
        first[2] * scale_one[..., None] + second[2] * scale_two[..., None],
    )


def tile_plan(rand_blocks, my_index, n_dev, per_dev, seqs, heads):
    count = seqs * per_dev * heads * 3
    capacity = max(2, 2 * count // n_dev)
    requests = (
        rand_blocks.reshape(seqs, n_dev, per_dev, heads, 3)
        .transpose(1, 0, 2, 3, 4)
        .reshape(n_dev, count)
    )
    is_mine = requests // per_dev == my_index
    ranking = jnp.cumsum(is_mine.astype(jnp.int32), 1) - 1
    slot_ids = jnp.arange(capacity, dtype=jnp.int32)
    select = is_mine[:, None, :] & (ranking[:, None, :] == slot_ids[None, :, None])
    filled = jnp.any(select, 2)
    position = jnp.arange(count, dtype=jnp.int32)
    seq_of = position // (per_dev * heads * 3)
    head_of = position // 3 % heads
    tile_of = (seq_of[None, :] * per_dev + requests % per_dev) * heads + head_of[None, :]
    send_index = jnp.sum(jnp.where(select, tile_of[:, None, :], 0), 2)
    own_requests = lax.dynamic_slice_in_dim(rand_blocks, my_index * per_dev, per_dev, 1).reshape(
        count
    )
    own_owner = own_requests // per_dev
    onehot = (own_owner[:, None] == jnp.arange(n_dev, dtype=jnp.int32)[None, :]).astype(jnp.int32)
    own_rank = jnp.sum((jnp.cumsum(onehot, 0) - 1) * onehot, 1)
    recv_index = own_owner * capacity + own_rank
    return (capacity, send_index, filled, recv_index)


def pick_tiles(incoming, recv_index, seqs, per_dev, heads, block, hsize):
    stacked = incoming.reshape(-1, block, 2 * hsize)
    return jnp.take(stacked, recv_index, 0).reshape(seqs, per_dev, heads, 3, block, 2 * hsize)


def assemble(end_part, window_part, tile_part, seqs, per_dev, heads, block, hsize):
    ends_wide = jnp.broadcast_to(end_part[:, None], (seqs, per_dev, heads, 2 * block, hsize))
    return jnp.concatenate(
        [ends_wide, window_part, tile_part.reshape(seqs, per_dev, heads, 3 * block, hsize)], 3
    )


def per_device(
    tokens,
    rand_blocks,
    query_weight,
    query_bias,
    key_weight,
    value_weight,
    value_bias,
    output_weight,
    output_bias,
    attn_gain,
    attn_shift,
    up_weight,
    up_bias,
    down_weight,
    down_bias,
    ffn_gain,
    ffn_shift,
    cotangent,
):
    seqs, rows, width = tokens.shape
    block = BLOCK
    hsize = HD
    per_dev = rows // block
    n_dev = lax.axis_size("seq")
    my_index = lax.axis_index("seq")
    n_blocks = per_dev * n_dev
    heads = query_weight.shape[1] // hsize
    hidden = heads * hsize
    n_tok = seqs * rows
    is_first = my_index == 0
    is_last = my_index == n_dev - 1
    flat = tokens.reshape(n_tok, width)
    query_low = (plain_dot(flat, query_weight) + query_bias).astype(jnp.bfloat16)
    key_low = plain_dot(flat, key_weight).astype(jnp.bfloat16)
    value_low = (plain_dot(flat, value_weight) + value_bias).astype(jnp.bfloat16)
    keyval = jnp.concatenate([key_low, value_low], 1).reshape(seqs, rows, 2 * hidden)
    extended = with_halo(keyval, (("seq", 1),), block)
    windows = jnp.stack(
        [extended[:, offset * block : (offset + 3) * block] for offset in range(per_dev)], 1
    )
    windows = windows.reshape(seqs, per_dev, 3 * block, 2, heads, hsize)
    win_key = windows[:, :, :, 0].transpose(0, 1, 3, 2, 4)
    win_value = windows[:, :, :, 1].transpose(0, 1, 3, 2, 4)
    triple = jnp.concatenate([query_low.reshape(seqs, rows, hidden), keyval], 2).astype(jnp.float32)
    own_ends = jnp.stack(
        [
            jnp.where(is_first, triple[:, :block], 0.0),
            jnp.where(is_last, triple[:, rows - block :], 0.0),
        ],
        1,
    )
    ends = lax.psum(own_ends.astype(jnp.bfloat16), "seq").reshape(seqs, 2, block, 3, heads, hsize)
    end_query = ends[:, :, :, 0].transpose(0, 3, 1, 2, 4).reshape(seqs, heads, 2 * block, hsize)
    end_key = ends[:, :, :, 1].transpose(0, 3, 1, 2, 4).reshape(seqs, heads, 2 * block, hsize)
    end_value = ends[:, :, :, 2].transpose(0, 3, 1, 2, 4).reshape(seqs, heads, 2 * block, hsize)
    capacity, send_index, filled, recv_index = tile_plan(
        rand_blocks, my_index, n_dev, per_dev, seqs, heads
    )
    table = (
        keyval.reshape(seqs, per_dev, block, 2, heads, hsize)
        .transpose(0, 1, 4, 2, 3, 5)
        .reshape(seqs * per_dev * heads, block, 2 * hsize)
    )
    outgoing = jnp.take(table, send_index.reshape(-1), 0).reshape(n_dev, capacity, block, 2 * hsize)
    outgoing = jnp.where(filled[:, :, None, None], outgoing, jnp.zeros((), jnp.bfloat16))
    incoming = lax.all_to_all(outgoing, "seq", split_axis=0, concat_axis=0, tiled=True)
    tiles = pick_tiles(incoming, recv_index, seqs, per_dev, heads, block, hsize)
    q_blocks = query_low.reshape(seqs, per_dev, block, heads, hsize).transpose(0, 1, 3, 2, 4)
    keys_all = assemble(end_key, win_key, tiles[..., :hsize], seqs, per_dev, heads, block, hsize)
    values_all = assemble(
        end_value, win_value, tiles[..., hsize:], seqs, per_dev, heads, block, hsize
    )
    block_ids = my_index * per_dev + jnp.arange(per_dev, dtype=jnp.int32)
    slot_ids = jnp.arange(8 * block, dtype=jnp.int32) // block
    dropped = (slot_ids == 2)[None, :] & (block_ids == 1)[:, None] | (slot_ids == 4)[None, :] & (
        block_ids == n_blocks - 2
    )[:, None]
    unscaled_scores = (
        jnp.einsum("sbhqd,sbhkd->sbhqk", q_blocks, keys_all, preferred_element_type=jnp.float32)
        * 0.125
    )
    unscaled_scores = jnp.where(dropped[None, :, None, None, :], masked_score, unscaled_scores)
    weights = softmax_row_probs(unscaled_scores)
    sparse_attention = jnp.einsum(
        "sbhqk,sbhkd->sbhqd",
        weights,
        values_all.astype(jnp.float32),
        precision=highest_precision,
        preferred_element_type=jnp.float32,
    )
    key_local = key_low.reshape(seqs, rows, heads, hsize).transpose(0, 2, 1, 3)
    value_local = value_low.reshape(seqs, rows, heads, hsize).transpose(0, 2, 1, 3)
    end_raw = (
        jnp.einsum("shqd,shkd->shqk", end_query, key_local, preferred_element_type=jnp.float32)
        * 0.125
    )
    end_top = jnp.max(end_raw, -1)
    end_expo = jnp.exp(end_raw - end_top[..., None])
    end_total = jnp.sum(end_expo, -1)
    end_acc = jnp.einsum(
        "shqk,shkd->shqd",
        end_expo,
        value_local.astype(jnp.float32),
        precision=highest_precision,
        preferred_element_type=jnp.float32,
    )
    merged_top, merged_total, merged_acc = joined((end_top, end_total, end_acc), "seq", merge_rows)
    end_out = merged_acc / merged_total[..., None]
    end_lse = merged_top + jnp.log(merged_total)
    end_split = end_out.reshape(seqs, heads, 2, block, hsize)
    first_rows = block_ids == 0
    last_rows = block_ids == n_blocks - 1
    attn = jnp.where(
        first_rows[None, :, None, None, None], end_split[:, None, :, 0], sparse_attention
    )
    attn = jnp.where(last_rows[None, :, None, None, None], end_split[:, None, :, 1], attn)
    attn_low = attn.transpose(0, 1, 3, 2, 4).reshape(n_tok, hidden).astype(jnp.bfloat16)
    branch = head_sum_fwd(plain_dot(attn_low, output_weight)) + output_bias
    resid = flat.astype(jnp.float32) + branch
    normed = layer_norm(resid, attn_gain, attn_shift)
    normed_low = normed.astype(jnp.bfloat16)
    pre_act = plain_dot(normed_low, up_weight) + up_bias
    act_low = gelu_exact(pre_act).astype(jnp.bfloat16)
    ffn = head_sum_fwd(plain_dot(act_low, down_weight)) + down_bias
    resid_two = normed + ffn
    layer_output = (
        layer_norm(resid_two, ffn_gain, ffn_shift).astype(jnp.bfloat16).reshape(seqs, rows, width)
    )
    cot_flat = cotangent.reshape(n_tok, width).astype(jnp.float32)
    norm_two, pull_two = jax.vjp(layer_norm, resid_two, ffn_gain, ffn_shift)
    grad_resid2, grad_ffngain, grad_ffnshift = pull_two(cot_flat)
    grad_ffn = grad_resid2.astype(jnp.bfloat16)
    grad_downbias = jnp.sum(grad_ffn.astype(jnp.float32), 0)
    grad_downweight = rows_dot(act_low, grad_ffn)
    grad_act = back_dot(grad_ffn, down_weight)
    gelu_out, pull_gelu = jax.vjp(gelu_exact, pre_act)
    grad_pre = pull_gelu(grad_act)[0].astype(jnp.bfloat16)
    grad_upbias = jnp.sum(grad_pre.astype(jnp.float32), 0)
    grad_upweight = rows_dot(normed_low, grad_pre)
    grad_normed = grad_resid2 + head_sum_back(back_dot(grad_pre, up_weight))
    norm_one, pull_one = jax.vjp(layer_norm, resid, attn_gain, attn_shift)
    grad_resid, grad_attngain, grad_attnshift = pull_one(grad_normed)
    grad_branch = grad_resid.astype(jnp.bfloat16)
    grad_obias = jnp.sum(grad_branch.astype(jnp.float32), 0)
    grad_oweight = rows_dot(attn_low, grad_branch)
    grad_attn = back_dot(grad_branch, output_weight).astype(jnp.bfloat16)
    grad_heads = grad_attn.reshape(seqs, per_dev, block, heads, hsize).transpose(0, 1, 3, 2, 4)
    global_mask = (first_rows | last_rows)[None, :, None, None, None]
    grad_sparse = jnp.where(global_mask, jnp.zeros((), jnp.bfloat16), grad_heads)
    own_dout = jnp.stack(
        [
            jnp.where(is_first, grad_heads[:, 0].astype(jnp.float32), 0.0),
            jnp.where(is_last, grad_heads[:, per_dev - 1].astype(jnp.float32), 0.0),
        ],
        2,
    ).reshape(seqs, heads, 2 * block, hsize)
    own_delta = jnp.sum(own_dout * end_out, -1)
    end_dout, end_delta = lax.psum((own_dout, own_delta), "seq")
    end_dlow = end_dout.astype(jnp.bfloat16)
    end_prob = jnp.exp(end_raw - end_lse[..., None])
    end_dprob = jnp.einsum(
        "shqd,shkd->shqk", end_dlow, value_local, preferred_element_type=jnp.float32
    )
    end_dscore = (end_prob * (end_dprob - end_delta[..., None]) * 0.125).astype(jnp.bfloat16)
    end_dquery_part = jnp.einsum(
        "shqk,shkd->shqd", end_dscore, key_local, preferred_element_type=jnp.float32
    )
    local_dkey = jnp.einsum(
        "shqk,shqd->shkd", end_dscore, end_query, preferred_element_type=jnp.float32
    )
    local_dvalue = jnp.einsum(
        "shqk,shqd->shkd",
        end_prob,
        end_dout,
        precision=highest_precision,
        preferred_element_type=jnp.float32,
    )
    again = lax.all_to_all(outgoing, "seq", split_axis=0, concat_axis=0, tiled=True)
    back_tiles = pick_tiles(again, recv_index, seqs, per_dev, heads, block, hsize)
    keys_back = assemble(
        end_key, win_key, back_tiles[..., :hsize], seqs, per_dev, heads, block, hsize
    )
    values_back = assemble(
        end_value, win_value, back_tiles[..., hsize:], seqs, per_dev, heads, block, hsize
    )
    grad_prob = jnp.einsum(
        "sbhqd,sbhkd->sbhqk", grad_sparse, values_back, preferred_element_type=jnp.float32
    )
    row_delta = jnp.sum(weights * grad_prob, -1, keepdims=True)
    grad_score = (weights * (grad_prob - row_delta) * 0.125).astype(jnp.bfloat16)
    grad_qblocks = jnp.einsum(
        "sbhqk,sbhkd->sbhqd", grad_score, keys_back, preferred_element_type=jnp.float32
    )
    grad_keysall = jnp.einsum(
        "sbhqk,sbhqd->sbhkd", grad_score, q_blocks, preferred_element_type=jnp.float32
    )
    grad_valsall = jnp.einsum(
        "sbhqk,sbhqd->sbhkd",
        weights,
        grad_sparse.astype(jnp.float32),
        precision=highest_precision,
        preferred_element_type=jnp.float32,
    )
    end_dkey = jnp.sum(grad_keysall[:, :, :, : 2 * block], 1)
    end_dvalue = jnp.sum(grad_valsall[:, :, :, : 2 * block], 1)
    win_grad = jnp.stack(
        [
            grad_keysall[:, :, :, 2 * block : 5 * block].transpose(0, 1, 3, 2, 4),
            grad_valsall[:, :, :, 2 * block : 5 * block].transpose(0, 1, 3, 2, 4),
        ],
        3,
    ).reshape(seqs, per_dev, 3 * block, 2 * hidden)
    rand_grad = (
        jnp.concatenate(
            [
                grad_keysall[:, :, :, 5 * block :].reshape(seqs, per_dev, heads, 3, block, hsize),
                grad_valsall[:, :, :, 5 * block :].reshape(seqs, per_dev, heads, 3, block, hsize),
            ],
            5,
        )
        .reshape(-1, block, 2 * hsize)
        .astype(jnp.bfloat16)
    )
    ext_grad = jnp.zeros((seqs, rows + 2 * block, 2 * hidden), jnp.float32)
    for offset in range(per_dev):
        ext_grad = ext_grad.at[:, offset * block : (offset + 3) * block].add(win_grad[:, offset])
    rims = jnp.concatenate([ext_grad[:, :block], ext_grad[:, rows + block :]], 1)
    returned_rims = with_halo(rims.astype(jnp.bfloat16), (("seq", 1),), block).astype(rims.dtype)
    middle_zero = jnp.zeros((seqs, rows - 2 * block, 2 * hidden), jnp.float32)
    kv_grad = ext_grad[:, block : rows + block] + jnp.concatenate(
        [returned_rims[:, :block], middle_zero, returned_rims[:, 3 * block :]], 1
    )
    sent_back = (
        jnp.zeros((n_dev * capacity, block, 2 * hsize), jnp.bfloat16)
        .at[recv_index]
        .set(rand_grad)
        .reshape(n_dev, capacity, block, 2 * hsize)
    )
    arrived = lax.all_to_all(sent_back, "seq", split_axis=0, concat_axis=0, tiled=True)
    arrived = jnp.where(filled[:, :, None, None], arrived.astype(jnp.float32), 0.0)
    table_grad = (
        jnp.zeros((seqs * per_dev * heads, block, 2 * hsize), jnp.float32)
        .at[send_index.reshape(-1)]
        .add(arrived.reshape(-1, block, 2 * hsize))
    )
    kv_grad = kv_grad + table_grad.reshape(seqs, per_dev, heads, block, 2, hsize).transpose(
        0, 1, 3, 4, 2, 5
    ).reshape(seqs, rows, 2 * hidden)
    kv_grad = kv_grad + jnp.stack(
        [local_dkey.transpose(0, 2, 1, 3), local_dvalue.transpose(0, 2, 1, 3)], 2
    ).reshape(seqs, rows, 2 * hidden)
    end_dquery, end_dkey_all, end_dvalue_all = (
        lax.psum(end_dquery_part.astype(jnp.bfloat16), "seq").astype(jnp.float32),
        lax.psum(end_dkey.astype(jnp.bfloat16), "seq").astype(jnp.float32),
        lax.psum(end_dvalue.astype(jnp.bfloat16), "seq").astype(jnp.float32),
    )
    end_kv = jnp.stack(
        [end_dkey_all.transpose(0, 2, 1, 3), end_dvalue_all.transpose(0, 2, 1, 3)], 2
    ).reshape(seqs, 2 * block, 2 * hidden)
    kv_grad = kv_grad + jnp.concatenate(
        [
            jnp.where(is_first, end_kv[:, :block], 0.0),
            middle_zero,
            jnp.where(is_last, end_kv[:, block:], 0.0),
        ],
        1,
    )
    end_q = end_dquery.transpose(0, 2, 1, 3).reshape(seqs, 2 * block, hidden)
    query_zero = jnp.zeros((seqs, rows - 2 * block, hidden), jnp.float32)
    grad_query = grad_qblocks.transpose(0, 1, 3, 2, 4).reshape(seqs, rows, hidden)
    grad_query = grad_query + jnp.concatenate(
        [
            jnp.where(is_first, end_q[:, :block], 0.0),
            query_zero,
            jnp.where(is_last, end_q[:, block:], 0.0),
        ],
        1,
    )
    query_glow = grad_query.reshape(n_tok, hidden).astype(jnp.bfloat16)
    kv_glow = kv_grad.reshape(n_tok, 2 * hidden).astype(jnp.bfloat16)
    key_glow = kv_glow[:, :hidden]
    value_glow = kv_glow[:, hidden:]
    grad_qbias = jnp.sum(query_glow.astype(jnp.float32), 0)
    grad_vbias = jnp.sum(value_glow.astype(jnp.float32), 0)
    grad_qweight = rows_dot(flat, query_glow)
    grad_kweight = rows_dot(flat, key_glow)
    grad_vweight = rows_dot(flat, value_glow)
    into_tokens = (
        back_dot(query_glow, query_weight)
        + back_dot(key_glow, key_weight)
        + back_dot(value_glow, value_weight)
    )
    input_grad = (grad_resid + head_sum_back(into_tokens)).reshape(seqs, rows, width)
    totals = lax.psum(
        (
            grad_qweight,
            grad_qbias,
            grad_kweight,
            grad_vweight,
            grad_vbias,
            grad_oweight,
            grad_obias,
            grad_attngain,
            grad_attnshift,
            grad_upweight,
            grad_upbias,
            grad_downweight,
            grad_downbias,
            grad_ffngain,
            grad_ffnshift,
        ),
        "seq",
    )
    return (
        layer_output,
        input_grad,
        totals[0],
        totals[1],
        totals[2],
        totals[3],
        totals[4],
        totals[5],
        totals[6],
        totals[7],
        totals[8],
        totals[9],
        totals[10],
        totals[11],
        totals[12],
        totals[13],
        totals[14],
    )


def solution(mesh):
    placed = (
        P(None, "seq", None),
        P(None, None, "tp", None),
        P(None, "tp"),
        P("tp"),
        P(None, "tp"),
        P(None, "tp"),
        P("tp"),
        P("tp", None),
        P(),
        P(),
        P(),
        P(None, "tp"),
        P("tp"),
        P("tp", None),
        P(),
        P(),
        P(),
        P(None, "seq", None),
    )
    return jax.shard_map(
        per_device,
        mesh=mesh,
        in_specs=placed,
        out_specs=(
            P(None, "seq", None),
            P(None, "seq", None),
            P(None, "tp"),
            P("tp"),
            P(None, "tp"),
            P(None, "tp"),
            P("tp"),
            P("tp", None),
            P(),
            P(),
            P(),
            P(None, "tp"),
            P("tp"),
            P("tp", None),
            P(),
            P(),
            P(),
        ),
        check_vma=False,
    )
```

profile of v0, /device:TPU:0, one launch (start us, length us, event | category | flops | bytes accessed | tf_op | source)
XLA Modules:
  0.0 2475.2 jit_solution(13134395559490497797)
XLA Ops:
  36.0 167.7 %all-reduce.15.cloned.1.call-done = bf16[16,2,64,3,3,64]{2,1,5,4,0,3:T(2,128)(2,1)} async-done(((bf16[16,2,64,3,3,64]{2,1,5,4,0,3:T(2,128)(2,1)}), bf16[16,2,64,3,3,64]{2,1,5,4,0,3:T(2,128)(2,1)}) %all-reduce.15.cloned.1.call-update) | async-done | bytes 2359312 | tf_op jit(solution)/shard_map/psum | solution.py:181
  245.8 18.5 gather_fusion
  311.9 92.9 %collective-permute-done = bf16[16,64,384]{2,1,0:T(8,128)(2,1)} collective-permute-done((bf16[16,64,384]{2,1,0:T(8,128)(2,1)}, bf16[16,64,384]{2,1,0:T(8,128)(2,1)}, u32[]{:S(2)}, u32[]{:S(2)}) %collective-permute-start) | collective-permute-done | bytes 786464 | tf_op jit(solution)/shard_map/ppermute | solution.py:22
  433.7 227.2 %all-gather.1 = f32[128,3,128]{2,0,1:T(8,128)S(1)} all-gather(f32[16,3,128]{2,0,1:T(8,128)S(1)} %copy.338), channel_id=3, replica_groups=mesh['seq'=8,'tp'=4] {'seq'}, dimensions={0}, use_global_device_ids=true | all-gather | bytes 221184 | tf_op jit(solution)/shard_map/all_gather | solution.py:29
  662.2 30.8 %all-gather = f32[128,3,128]{2,0,1:T(8,128)S(1)} all-gather(f32[16,3,128]{2,0,1:T(8,128)} %copy.337), channel_id=2, replica_groups=mesh['seq'=8,'tp'=4] {'seq'}, dimensions={0}, use_global_device_ids=true | all-gather | bytes 221184 | tf_op jit(solution)/shard_map/all_gather | solution.py:29
  744.5 74.6 %while.21 = (s32[]{:T(128)}, f32[16,3,128]{2,1,0:T(4,128)S(1)}, f32[16,3,128]{2,1,0:T(4,128)S(1)}, f32[16,3,128,64]{3,2,1,0:T(8,128)}, f32[8,16,3,128]{3,1,0,2:T...) while((s32[]{:T(128)}, f32[16,3,128]{2,1,0:T(4,128)S(1)}, ...), condition=%wide.region_4.5_spmd, body=%wide.region_3.4_spmd.sunk | while | flops 1216517 | bytes 11354255 | solution.py:35
  843.2 14.2 fusion.38
  867.5 116.9 %all-reduce.17.cloned.1.call-done = f32[2048,768]{1,0:T(8,128)} async-done(((f32[2048,768]{1,0:T(8,128)}), f32[2048,768]{1,0:T(8,128)}) %all-reduce.17.cloned.1.call-update) | async-done | bytes 6291472 | tf_op jit(solution)/shard_map/psum | solution.py:71
  991.7 18.3 multiply_convert_fusion.1
  1016.2 119.9 %all-reduce.19.cloned.1.call-done = f32[2048,768]{1,0:T(8,128)} async-done(((f32[2048,768]{1,0:T(8,128)}), f32[2048,768]{1,0:T(8,128)}) %all-reduce.19.cloned.1.call-update) | async-done | bytes 6291472 | tf_op jit(solution)/shard_map/psum | solution.py:71
  1166.3 118.9 %all-reduce.21.cloned.1.call-done = f32[2048,768]{1,0:T(8,128)} async-done(((f32[2048,768]{1,0:T(8,128)}), f32[2048,768]{1,0:T(8,128)}) %all-reduce.21.cloned.1.call-update) | async-done | bytes 6291472 | tf_op jit(solution)/shard_map/psum | solution.py:75
  1313.9 11.9 fusion.84
  1339.6 47.6 %fusion.25 = f32[16,2,3,512,64]{3,4,2,1,0:T(8,128)} fusion(f32[16,2,3,64,512]{4,3,2,1,0:T(8,128)} %fusion.42, bf16[16,2,64,3,64]{2,1,0,4,3:T(2,128)(2,1)} %reshape.720, f32[16,2,3,64,512]{4,3,2,1,0:T(8,128)} %copy-done.21, f32[16,2,3,64]{3,2,1,0:T(4,128)S(1)} %copy-done.70, f32[16,2,3,64]{3,2,1,0:T(4,128)S(1)} %copy-done.69, pred[2,512]{1,0:T(4,128)(4,1)S(1)} %and_or_fusion), kind=kOutput, calls=%fused_computation.81 | convolution fusion | flops 443554304 | bytes 38585344 | tf_op jit(solution)/shard_map/sbhqk,sbhqd->sbhkd/dot_general | solution.py:323
  1414.1 38.9 %scatter_fusion = bf16[576,64,128]{2,1,0:T(8,128)(2,1)} fusion(bf16[576,64,128]{2,1,0:T(8,128)(2,1)} %broadcast_in_dim.252, s32[288]{0:T(512)S(1)} %fusion.110, bf16[288,64,128]{2,1,0:T(8,128)(2,1)} %pad_maximum_fusion.4), kind=kCustom, calls=%fused_computation.2 | custom fusion | bytes 14156928 | tf_op jit(solution)/shard_map/scatter | solution.py:365
  1484.5 11.6 pad_maximum_fusion
  1507.3 200.8 %psum.180 = f32[16,3,128]{2,1,0:T(4,128)S(1)} all-reduce(f32[16,3,128]{2,1,0:T(4,128)S(1)} %multiply_reduce_fusion.6), channel_id=1, replica_groups=mesh['seq'=8,'tp'=4] {'seq'}, use_global_device_ids=true, to_apply=%region_28.30 | all-reduce | flops 6144 | bytes 49152 | tf_op jit(solution)/shard_map/psum | solution.py:287
  1774.3 24.5 collective-permute-done.2
  1818.4 44.6 %all-reduce.29.cloned.1.call-done = (bf16[16,128,192]{1,2,0:T(8,128)(2,1)}, bf16[16,128,1,3,64]{1,4,3,2,0:T(8,128)(2,1)}, bf16[16,128,1,3,64]{1,4,3,2,0:T(8,128)(2,1)}) async-done(((bf16[16,128,192]{1,2,0:T(8,128)(2,1)}, bf16[16,128,1,3,64]{1,4,3,2,0:T(8,128)(2,1)}, bf16[16,128,1,3,64]{1,4,3,2,0:T(8,128)(2,1)}), (bf16[16,128,192]{1,2,0:T(8,128)(2,1)}, bf16[16,128,1,3,64]{1,4,3,2,0:T(8,128)(2,1)}, ...) | async-done | bytes 2359312 | tf_op jit(solution)/shard_map/psum | solution.py:382
  1877.5 47.3 %convert_reduce_fusion.4 = (f32[3,64]{1,0:T(4,128)S(1)}, bf16[16,2,64,3,64]{4,2,3,1,0:T(8,128)(2,1)}, f32[16,2,64,3,64]{4,2,3,1,0:T(8,128)}) fusion(f32[16,2,64,3,64]{4,2,3,1,0:T(8,128)} %copy.392, bf16[16,2,3,192,64]{3,4,2,1,0:T(8,128)(2,1)} %copy.365, bf16[16,2,3,192,64]{3,4,2,1,0:T(8,128)(2,1)} %get-tuple-element.339, ...), kind=kOutput, calls=%fused_computation.110 | convolution fusion | flops 464001344 | bytes 35440384 | tf_op jit(solution)/shard_map/sbhqk,sbhkd->sbhqd/dot_general | solution.py:320
  1958.7 90.0 %scatter_fusion.1 = f32[96,64,128]{2,1,0:T(8,128)} fusion(f32[96,64,128]{2,1,0:T(8,128)} %broadcast_in_dim.251, s32[576]{0:T(1024)S(1)} %copy-done.74, f32[576,64,128]{2,1,0:T(8,128)} %bitcast.302), kind=kCustom, calls=%fused_computation.3 | custom fusion | flops 4718592 | bytes 56625408 | tf_op jit(solution)/shard_map/scatter-add | solution.py:373
  2055.8 12.1 copy.387
  2129.2 35.8 %all-reduce.3 = (f32[192]{0:T(256)}, f32[192]{0:T(256)}, f32[768]{0:T(1024)}, f32[768]{0:T(1024)}, f32[768]{0:T(1024)}, /*index=5*/f32[768]{0:T(1024)}, f32[768]{0:T(1024)}, f32[768]{0:T(1024)}, f32[768]{0:T(1024)}) all-reduce(f32[192]{0:T(256)S(1)} %reduce_sum.258, ...), channel_id=1, replica_groups=mesh['seq'=8,'tp'=4] {'seq'}, use_global_device_ids=true, to_apply=%region_39.41 | all-reduce | flops 5760 | bytes 46080 | tf_op jit(solution)/shard_map/psum | solution.py:423
  2165.0 48.0 %all-reduce.25.cloned.1.call-done = f32[2048,768]{1,0:T(8,128)} async-done(((f32[2048,768]{1,0:T(8,128)}), f32[2048,768]{1,0:T(8,128)}) %all-reduce.25.cloned.1.call-update) | async-done | bytes 6291472 | tf_op jit(solution)/shard_map/psum | solution.py:75
  2221.0 236.7 %all-reduce.27.cloned.1.call-done = (f32[768,192]{0,1:T(8,128)}, f32[768,192]{0,1:T(8,128)}, f32[768,192]{0,1:T(8,128)}, f32[192,768]{1,0:T(8,128)}, f32[768,768]{1,0:T(8,128)}, /*index=5*/f32[768,768]{1,0:T(8,128)}) async-done(((f32[768,192]{0,1:T(8,128)}, f32[768,192]{0,1:T(8,128)}, f32[768,192]{0,1:T(8,128)}, f32[192,768]{1,0:T(8,128)}, f32[768,768]{1,0:T(8,128)}, /*index=5*/f32[768,768]{1,0:T(8,128)}), ...) | async-done | bytes 7077904 | tf_op jit(solution)/shard_map/psum | solution.py:423
  (477 shorter events, 684.6 us)
Async XLA Ops:
  7.2 984.5 %copy-start = (bf16[768,768]{1,0:T(8,128)(2,1)S(1)}, bf16[768,768]{1,0:T(8,128)(2,1)}, u32[]{:S(2)}) copy-start(bf16[768,768]{1,0:T(8,128)(2,1)} %param.37) | copy-start | bytes 3538948
  7.2 196.4 %all-reduce.15.cloned.1.call-start = ((), (), s32[]{:S(2)}) async-start(), calls=%async_computation.2 | async-start | bytes 9437184 | tf_op jit(solution)/shard_map/psum | solution.py:181
  31.1 709.6 %all-gather.5.cloned.1.call-start = ((), (), s32[]{:S(2)}) async-start(), calls=%async_computation.8 | async-start | bytes 14155776 | tf_op jit(solution)/shard_map/all_gather | solution.py:29
  34.4 181.4 %copy-start.26 = (bf16[24,8,16,128]{3,2,1,0:T(8,128)(2,1)}, bf16[24,8,16,128]{3,2,1,0:T(8,128)(2,1)S(1)}, u32[]{:S(2)}) copy-start(bf16[24,8,16,128]{3,2,1,0:T(8,128)(2,1)S(1)} %copy.415) | copy-start | bytes 2359300
  36.0 180.6 %copy-start.30 = (bf16[24,8,16,128]{3,2,1,0:T(8,128)(2,1)}, bf16[24,8,16,128]{3,2,1,0:T(8,128)(2,1)S(1)}, u32[]{:S(2)}) copy-start(bf16[24,8,16,128]{3,2,1,0:T(8,128)(2,1)S(1)} %copy.416) | copy-start | bytes 2359300
  245.8 18.5 copy-start.73
  274.2 420.2 %all-to-all-start = ((bf16[8,72,64,128]{3,2,1,0:T(8,128)(2,1)}), bf16[8,72,64,128]{3,2,1,0:T(8,128)(2,1)}, u32[]{:S(2)}, u32[]{:S(2)}) async-start(bf16[8,72,64,128]{3,2,1,0:T(8,128)(2,1)} %select_select_fusion), calls=%async_computation | async-start | bytes 18874368 | tf_op jit(solution)/shard_map/all_to_all | solution.py:195
  279.4 27.0 %copy-start.39 = (bf16[2048,192]{0,1:T(8,128)(2,1)S(1)}, bf16[2048,192]{0,1:T(8,128)(2,1)}, u32[]{:S(2)}) copy-start(bf16[2048,192]{0,1:T(8,128)(2,1)} %copy-done.38) | copy-start | bytes 2359300
  279.4 705.1 %all-reduce.17.cloned.1.call-start = ((), (), s32[]{:S(2)}) async-start(), calls=%async_computation.3 | async-start | bytes 12582912 | tf_op jit(solution)/shard_map/psum | solution.py:71
  284.5 126.9 %collective-permute-start.1 = (bf16[16,64,384]{2,1,0:T(8,128)(2,1)}, bf16[16,64,384]{2,1,0:T(8,128)(2,1)}, u32[]{:S(2)}, u32[]{:S(2)}) collective-permute-start(bf16[16,64,384]{2,1,0:T(8,128)(2,1)} %copy.410), channel_id=1, source_target_pairs={{4,0},{8,4},{12,8},{16,12},{20,16},{24,20},{28,24},{5,1},{9,5},{13... | collective-permute-start | bytes 2359304 | tf_op jit(solution)/shard_map/ppermute | solution.py:23
  288.5 116.3 %collective-permute-start = (bf16[16,64,384]{2,1,0:T(8,128)(2,1)}, bf16[16,64,384]{2,1,0:T(8,128)(2,1)}, u32[]{:S(2)}, u32[]{:S(2)}) collective-permute-start(bf16[16,64,384]{2,1,0:T(8,128)(2,1)} %copy.409), channel_id=1, source_target_pairs={{0,4},{4,8},{8,12},{12,16},{16,20},{20,24},{24,28},{1,5},{5,9},{9,... | collective-permute-start | bytes 2359304 | tf_op jit(solution)/shard_map/ppermute | solution.py:22
  867.5 117.0 %copy-start.89 = (f32[768]{0:T(1024)S(1)}, f32[768]{0:T(1024)}, u32[]{:S(2)}) copy-start(f32[768]{0:T(1024)} %param.34) | copy-start | bytes 9220
  867.5 268.6 %all-reduce.19.cloned.1.call-start = ((), (), s32[]{:S(2)}) async-start(), calls=%async_computation.4 | async-start | bytes 12582912 | tf_op jit(solution)/shard_map/psum | solution.py:71
  991.7 20.0 copy-start.91
  1016.1 120.0 %copy-start.90 = (f32[768]{0:T(1024)S(1)}, f32[768]{0:T(1024)}, u32[]{:S(2)}) copy-start(f32[768]{0:T(1024)} %param.40) | copy-start | bytes 9220
  1016.1 269.1 %all-reduce.21.cloned.1.call-start = ((), (), s32[]{:S(2)}) async-start(), calls=%async_computation.5 | async-start | bytes 12582912 | tf_op jit(solution)/shard_map/psum | solution.py:75
  1453.0 493.1 %all-to-all-start.1 = ((bf16[8,72,64,128]{3,2,1,0:T(8,128)(2,1)}), bf16[8,72,64,128]{3,2,1,0:T(8,128)(2,1)}, u32[]{:S(2)}, u32[]{:S(2)}) async-start(bf16[8,72,64,128]{3,2,1,0:T(8,128)(2,1)} %bitcast.303), calls=%async_computation.1 | async-start | bytes 18874368 | tf_op jit(solution)/shard_map/all_to_all | solution.py:368
  1471.2 261.0 %all-reduce.23.cloned.1.call-start = ((), (), s32[]{:S(2)}) async-start(), calls=%async_computation.6 | async-start | bytes 3145728 | tf_op jit(solution)/shard_map/psum | solution.py:287
  1471.8 391.2 %all-reduce.29.cloned.1.call-start = ((), (), s32[]{:S(2)}) async-start(), calls=%async_computation.10 | async-start | bytes 4718592 | tf_op jit(solution)/shard_map/psum | solution.py:382
  1738.5 474.5 %all-reduce.25.cloned.1.call-start = ((), (), s32[]{:S(2)}) async-start(), calls=%async_computation.7 | async-start | bytes 12582912 | tf_op jit(solution)/shard_map/psum | solution.py:75
  1751.1 21.6 collective-permute-start.3
  1758.1 40.6 %collective-permute-start.2 = (bf16[16,64,384]{2,1,0:T(8,128)(2,1)}, bf16[16,64,384]{2,1,0:T(8,128)(2,1)S(1)}, u32[]{:S(2)}, u32[]{:S(2)}) collective-permute-start(bf16[16,64,384]{2,1,0:T(8,128)(2,1)} %copy.380), channel_id=1, source_target_pairs={{0,4},{4,8},{8,12},{12,16},{16,20},{20,24},{24,28},{1,5},{5,9},{9,... | collective-permute-start | bytes 2359304 | tf_op jit(solution)/shard_map/ppermute | solution.py:22
  2094.3 363.3 %all-reduce.27.cloned.1.call-start = ((), (), s32[]{:S(2)}) async-start(), calls=%async_computation.9 | async-start | bytes 14155776 | tf_op jit(solution)/shard_map/psum | solution.py:423
  2126.1 86.9 %copy-start.67 = (f32[2048]{0:T(1024)S(1)}, f32[2048]{0:T(1024)}, u32[]{:S(2)}) copy-start(f32[2048]{0:T(1024)} %copy-done.66) | copy-start | bytes 24580
  (97 other events, 481.3 us)
Sparse Core Ops, SparseCore 0:
  31.2 172.3 all-reduce.14
  221.5 351.3 all-gather.4
  867.6 116.8 all-reduce.16
  1016.2 119.7 all-reduce.18
  1165.4 119.7 all-reduce.20
  1475.8 256.3 all-reduce.22
  1738.6 124.3 all-reduce.28
  2094.4 118.5 all-reduce.24
  2220.0 237.5 all-reduce.26
where the time goes:
time: 2490 us; the launch traced here: 2480 us
  waiting for transfers between devices  992 us (40%)
  blocking collectives  495 us (20%)
  local copies, waits for them, and re-layouts  426 us (17%)
  other arithmetic  293 us (12%)
  matrix products  230 us (9%)
    all_gather x2, blocking collectives, joined(): everything = jax.tree.map(lambda part: lax.all_gather(part, axis), shard)  258 us
    psum x2, waiting for transfers between devices, head_sum_fwd(): return lax.psum(pieces, 'tp')  237 us
    psum x1, waiting for transfers between devices, per_device(): lax.psum((grad_qweight, grad_qbias, grad_kweight, grad_vweight, grad_vbia...  237 us
    psum x1, blocking collectives, per_device(): end_dout, end_delta = lax.psum((own_dout, own_delta), 'seq')  201 us
    psum x1, waiting for transfers between devices, per_device(): lax.psum(own_ends.astype(jnp.bfloat16), 'seq')  168 us
    psum x2, waiting for transfers between devices, head_sum_back(): return lax.psum(pieces, 'tp')  167 us
    ppermute x2, waiting for transfers between devices, with_halo(): before = lax.ppermute(last, axis, up)  117 us
    scatter-add x1, other arithmetic, per_device(): table_grad = jnp.zeros((seqs * per_dev * heads, block, 2 * hsize), jnp.fl...  90 us
  transfers between devices with their start and end apart: 15, of which 11 were waited for; matrix products, arithmetic and copies ran while one was open for 15% of the time, Pallas kernels for 0%

commit v1 on v0

--- a/solution.py
+++ b/solution.py
@@ -2,6 +2,8 @@
 import jax.numpy as jnp
 from jax import lax
 from jax.sharding import PartitionSpec as P
+from jax.experimental import pallas as pl
+from jax.experimental.pallas import tpu as pltpu
 
 HD = 64
 BLOCK = 64
@@ -126,7 +128,7 @@
     )
 
 
-def per_device(
+def split_sequences(
     tokens,
     rand_blocks,
     query_weight,
@@ -461,6 +463,399 @@
     )
 
 
+HALF_ROOT = 0.7071067811865476
+PDF_SCALE = 0.3989422804014327
+
+
+def attend_kernel(q_ref, ko_ref, kx_ref, vo_ref, vx_ref, bo_ref, bx_ref, o_ref, lse_ref):
+    span = q_ref.shape[0]
+    blocks = span // BLOCK
+    lane = lax.broadcasted_iota(jnp.int32, (1, 2 * HD), 1) // HD
+    vo_t = vo_ref[...].T
+    vx_t = vx_ref[...].T
+    outs = []
+    for h in range(2):
+        qh = (jnp.where(lane == h, q_ref[...], 0.0) * 0.125).astype(jnp.bfloat16)
+
+        def scores(k_ref, b_ref):
+            raw = back_dot(k_ref[...], qh).reshape(blocks, BLOCK, span)
+            return (raw + b_ref[h][:, None, :]).reshape(span, span)
+
+        so = scores(ko_ref, bo_ref)
+        sx = scores(kx_ref, bx_ref)
+        top = jnp.maximum(jnp.max(so, 0, keepdims=True), jnp.max(sx, 0, keepdims=True))
+        po = jnp.exp(so - top)
+        px = jnp.exp(sx - top)
+        total = jnp.sum(po, 0, keepdims=True) + jnp.sum(px, 0, keepdims=True)
+        rows = slice(h * HD, (h + 1) * HD)
+        acc = plain_dot(vo_t[rows], po.astype(jnp.bfloat16))
+        acc = acc + plain_dot(vx_t[rows], px.astype(jnp.bfloat16))
+        outs.append(acc / total)
+        lse_ref[0, h : h + 1, :] = top + jnp.log(total)
+    o_ref[...] = jnp.concatenate(outs, 0).T.astype(jnp.bfloat16)
+
+
+def attend_back_kernel(
+    q_ref, ko_ref, kx_ref, vo_ref, vx_ref, bo_ref, bx_ref, lse_ref, o_ref, g_ref,
+    dq_ref, dko_ref, dkx_ref, dvo_ref, dvx_ref,
+):
+    span = q_ref.shape[0]
+    blocks = span // BLOCK
+    lane = lax.broadcasted_iota(jnp.int32, (1, 2 * HD), 1) // HD
+    weighted = (o_ref[...].astype(jnp.float32) * g_ref[...].astype(jnp.float32)).T
+    parts = ((ko_ref, vo_ref, bo_ref), (kx_ref, vx_ref, bx_ref))
+    k_ts = [k_ref[...].T for k_ref, _, _ in parts]
+    dks = [None, None]
+    dvs = [None, None]
+    dq_ts = []
+    for h in range(2):
+        mine = lane == h
+        rows = slice(h * HD, (h + 1) * HD)
+        qh = (jnp.where(mine, q_ref[...], 0.0) * 0.125).astype(jnp.bfloat16)
+        gh = jnp.where(mine, g_ref[...], 0.0).astype(jnp.bfloat16)
+        delta = jnp.sum(weighted[rows], 0, keepdims=True)
+        lse = lse_ref[0, h : h + 1, :]
+        dq_t = None
+        for at, (k_ref, v_ref, b_ref) in enumerate(parts):
+            raw = back_dot(k_ref[...], qh).reshape(blocks, BLOCK, span)
+            raw = (raw + b_ref[h][:, None, :]).reshape(span, span)
+            prob = jnp.exp(raw - lse)
+            dprob = back_dot(v_ref[...], gh)
+            dscore = (prob * (dprob - delta)).astype(jnp.bfloat16)
+            dv = plain_dot(prob.astype(jnp.bfloat16), gh)
+            dk = plain_dot(dscore, qh)
+            dvs[at] = dv if dvs[at] is None else dvs[at] + dv
+            dks[at] = dk if dks[at] is None else dks[at] + dk
+            piece = plain_dot(k_ts[at][rows], dscore)
+            dq_t = piece if dq_t is None else dq_t + piece
+        dq_ts.append(dq_t * 0.125)
+    dq_ref[...] = jnp.concatenate(dq_ts, 0).T.astype(dq_ref.dtype)
+    for ref, value in ((dko_ref, dks[0]), (dkx_ref, dks[1]), (dvo_ref, dvs[0]), (dvx_ref, dvs[1])):
+        ref[...] = value.astype(ref.dtype)
+
+
+def pair_specs(span, blocks):
+    tile = pl.BlockSpec((span, 2 * HD), lambda i: (0, i))
+    bias = pl.BlockSpec((2, blocks, span), lambda i: (i, 0, 0))
+    lse = pl.BlockSpec((1, 2, span), lambda i: (i, 0, 0))
+    return tile, bias, lse
+
+
+def attend(q, ko, kx, vo, vx, bo, bx):
+    span, width = q.shape
+    heads = width // HD
+    tile, bias, lse = pair_specs(span, span // BLOCK)
+    return pl.pallas_call(
+        attend_kernel,
+        grid=(heads // 2,),
+        in_specs=[tile] * 5 + [bias] * 2,
+        out_specs=[tile, lse],
+        out_shape=[
+            jax.ShapeDtypeStruct((span, width), jnp.bfloat16),
+            jax.ShapeDtypeStruct((heads // 2, 2, span), jnp.float32),
+        ],
+        compiler_params=pltpu.CompilerParams(vmem_limit_bytes=48 * 2**20),
+        cost_estimate=pl.CostEstimate(
+            flops=heads * span * span * 2 * 2 * 2 * HD * 4,
+            bytes_accessed=span * width * 12,
+            transcendentals=heads * span * span * 2,
+        ),
+    )(q, ko, kx, vo, vx, bo, bx)
+
+
+def attend_back(q, ko, kx, vo, vx, bo, bx, lse_all, o, g):
+    span, width = q.shape
+    heads = width // HD
+    tile, bias, lse = pair_specs(span, span // BLOCK)
+    low = jax.ShapeDtypeStruct((span, width), jnp.bfloat16)
+    full = jax.ShapeDtypeStruct((span, width), jnp.float32)
+    return pl.pallas_call(
+        attend_back_kernel,
+        grid=(heads // 2,),
+        in_specs=[tile] * 5 + [bias] * 2 + [lse] + [tile] * 2,
+        out_specs=[tile] * 5,
+        out_shape=[low, full, low, full, low],
+        compiler_params=pltpu.CompilerParams(vmem_limit_bytes=48 * 2**20),
+        cost_estimate=pl.CostEstimate(
+            flops=heads * span * span * 2 * 2 * 5 * HD * 4,
+            bytes_accessed=span * width * 30,
+            transcendentals=heads * span * span * 2,
+        ),
+    )(q, ko, kx, vo, vx, bo, bx, lse_all, o, g)
+
+
+def swap(piece, bits):
+    size = lax.axis_size("tp")
+    return lax.ppermute(piece, "tp", [(i, i ^ bits) for i in range(size)])
+
+
+def gathered_over_tp(own):
+    far = swap(own, 2)
+    return own, swap(own, 1), far, swap(far, 1)
+
+
+def by_core(parts, core):
+    swapped = (parts[1], parts[0], parts[3], parts[2])
+    return [jnp.where(core == 0, a, b) for a, b in zip(parts, swapped)]
+
+
+def seq_exchange(pieces, sign):
+    size = lax.axis_size("seq")
+    return [pieces[0]] + [
+        lax.ppermute(pieces[k], "seq", [(i, (i + sign * k) % size) for i in range(size)])
+        for k in range(1, size)
+    ]
+
+
+def norm_parts(resid):
+    centre = resid - jnp.mean(resid, -1, keepdims=True)
+    inverse = lax.rsqrt(jnp.mean(centre * centre, -1, keepdims=True) + norm_eps)
+    return centre * inverse, inverse
+
+
+def norm_back(grad, unit, inverse, gain):
+    scaled = grad * gain
+    pull = scaled - jnp.mean(scaled, -1, keepdims=True)
+    pull = pull - unit * jnp.mean(scaled * unit, -1, keepdims=True)
+    return pull * inverse, jnp.sum(grad * unit, 0), jnp.sum(grad, 0)
+
+
+def key_bias(ids, query_ids, key_ids, n_blocks):
+    b = query_ids[None, None, :]
+    k = key_ids[None, :, None]
+    one = lambda flag: flag.astype(jnp.int32)
+    count = (
+        one(k == 0)
+        + one(k == n_blocks - 1)
+        + one((k == b - 1) & (b != 1))
+        + one(k == b)
+        + one((k == b + 1) & (b != n_blocks - 2))
+    )
+    for at in range(3):
+        count = count + one(ids[:, None, :, at] == k)
+    whole = (b == 0) | (b == n_blocks - 1)
+    count = jnp.where(whole, 1, count).astype(jnp.float32)
+    bias = jnp.where(count > 0, jnp.log(jnp.maximum(count, 1.0)), masked_score)
+    return jnp.repeat(bias, BLOCK, axis=2)
+
+
+def whole_sequences(
+    tokens,
+    rand_blocks,
+    query_weight,
+    query_bias,
+    key_weight,
+    value_weight,
+    value_bias,
+    output_weight,
+    output_bias,
+    attn_gain,
+    attn_shift,
+    up_weight,
+    up_bias,
+    down_weight,
+    down_bias,
+    ffn_gain,
+    ffn_shift,
+    cotangent,
+):
+    seqs, rows, width = tokens.shape
+    n_dev = lax.axis_size("seq")
+    me = lax.axis_index("seq")
+    t = lax.axis_index("tp")
+    side, core = t // 2, t % 2
+    n_blocks = rows // BLOCK * n_dev
+    hidden = query_weight.shape[1]
+    units = up_weight.shape[1]
+    span = n_dev * BLOCK
+
+    def to_owner(array):
+        cut = array.reshape(n_dev, 2, 2, BLOCK, width)
+        cut = lax.dynamic_index_in_dim(cut, side, 1, False)
+        cut = lax.dynamic_index_in_dim(cut, core, 1, False)
+        pieces = [
+            lax.dynamic_index_in_dim(cut, (me + k) % n_dev, 0, False) for k in range(n_dev)
+        ]
+        return jnp.concatenate(seq_exchange(pieces, 1), 0)
+
+    x = to_owner(tokens)
+    qkv_own = jnp.concatenate([query_weight.T, key_weight.T, value_weight.T], 0)
+    qkv_w = by_core(gathered_over_tp(qkv_own), core)
+    cot = to_owner(cotangent)
+
+    flat_rand = rand_blocks.reshape(seqs, -1).astype(jnp.float32)
+    small_own = jnp.concatenate([query_bias, value_bias, up_bias])
+
+    def small_for(bits):
+        sid = 2 * me + (t ^ bits) // 2
+        row = lax.dynamic_index_in_dim(flat_rand, sid, 0, False)
+        return jnp.concatenate([row, small_own])
+
+    smalls = [small_for(0)] + [swap(small_for(bits), bits) for bits in (1, 2, 3)]
+    smalls = by_core(smalls, core)
+    n_rand = flat_rand.shape[1]
+    ids = jnp.stack([s[:n_rand] for s in smalls]).astype(jnp.int32)
+    heads_dev = hidden // HD
+    ids = ids.reshape(4, n_dev, 2, heads_dev, 3)
+    ids = lax.dynamic_index_in_dim(ids, core, 2, False)
+    source = (me - jnp.arange(n_dev, dtype=jnp.int32)) % n_dev
+    ids = jnp.take(ids, source, 1).transpose(0, 2, 1, 3).reshape(4 * heads_dev, n_dev, 3)
+    q_bias = jnp.concatenate([s[n_rand : n_rand + hidden] for s in smalls])
+    v_bias = jnp.concatenate([s[n_rand + hidden : n_rand + 2 * hidden] for s in smalls])
+    u_bias = jnp.concatenate([s[n_rand + 2 * hidden :] for s in smalls])
+    own_ids = 2 * source + core
+    bias_own = key_bias(ids, own_ids, own_ids, n_blocks)
+    bias_far = key_bias(ids, own_ids, 2 * source + 1 - core, n_blocks)
+
+    wq = jnp.concatenate([w[:hidden] for w in qkv_w], 0)
+    wk = jnp.concatenate([w[hidden : 2 * hidden] for w in qkv_w], 0)
+    wv = jnp.concatenate([w[2 * hidden :] for w in qkv_w], 0)
+    k_own = back_dot(x, wk).astype(jnp.bfloat16)
+    v_own = (back_dot(x, wv) + v_bias).astype(jnp.bfloat16)
+    k_far, v_far = swap(k_own, 1), swap(v_own, 1)
+    q = (back_dot(x, wq) + q_bias).astype(jnp.bfloat16)
+
+    wo = jnp.concatenate(by_core(gathered_over_tp(output_weight), core), 0)
+    w_up = jnp.concatenate(by_core(gathered_over_tp(up_weight), core), 1)
+    w_down = jnp.concatenate(by_core(gathered_over_tp(down_weight), core), 0)
+
+    attn_low, lse = attend(q, k_own, k_far, v_own, v_far, bias_own, bias_far)
+    branch = plain_dot(attn_low, wo) + output_bias
+    unit_one, inverse_one = norm_parts(x.astype(jnp.float32) + branch)
+    normed = unit_one * attn_gain + attn_shift
+    normed_low = normed.astype(jnp.bfloat16)
+    pre_act = plain_dot(normed_low, w_up) + u_bias
+    cdf = 0.5 * (1.0 + lax.erf(pre_act * HALF_ROOT))
+    act_low = (pre_act * cdf).astype(jnp.bfloat16)
+    slope = (cdf + pre_act * (PDF_SCALE * jnp.exp(-0.5 * pre_act * pre_act))).astype(jnp.bfloat16)
+    ffn = plain_dot(act_low, w_down) + down_bias
+    unit_two, inverse_two = norm_parts(normed + ffn)
+    out_low = (unit_two * ffn_gain + ffn_shift).astype(jnp.bfloat16)
+
+    g_resid2, grad_ffngain, grad_ffnshift = norm_back(
+        cot.astype(jnp.float32), unit_two, inverse_two, ffn_gain
+    )
+    g_ffn = g_resid2.astype(jnp.bfloat16)
+    grad_downbias = jnp.sum(g_ffn.astype(jnp.float32), 0)
+    grad_down = rows_dot(act_low, g_ffn)
+    g_pre = (back_dot(g_ffn, w_down) * slope.astype(jnp.float32)).astype(jnp.bfloat16)
+    grad_upbias = jnp.sum(g_pre.astype(jnp.float32), 0)
+    grad_up = [
+        rows_dot(normed_low, g_pre[:, r * units : (r + 1) * units]) for r in range(4)
+    ]
+
+    def reduced(parts):
+        parts = by_core(parts, core)
+        near = swap(jnp.concatenate([parts[1], parts[3]], 0).astype(jnp.bfloat16), 1)
+        height = parts[0].shape[0]
+        mine = parts[0] + near[:height].astype(jnp.float32)
+        other = parts[2] + near[height:].astype(jnp.float32)
+        mine = mine + swap(other.astype(jnp.bfloat16), 2).astype(jnp.float32)
+        return lax.psum(mine.astype(jnp.bfloat16), "seq").astype(jnp.float32)
+
+    ffn_total = reduced(
+        [
+            jnp.concatenate([grad_down[r * units : (r + 1) * units], grad_up[r]], 0)
+            for r in range(4)
+        ]
+    )
+    g_normed = g_resid2 + back_dot(g_pre, w_up)
+    g_resid, grad_attngain, grad_attnshift = norm_back(g_normed, unit_one, inverse_one, attn_gain)
+    g_branch = g_resid.astype(jnp.bfloat16)
+    grad_obias = jnp.sum(g_branch.astype(jnp.float32), 0)
+    grad_o = rows_dot(attn_low, g_branch)
+    g_attn = back_dot(g_branch, wo).astype(jnp.bfloat16)
+
+    dq, dk_own, dk_far, dv_own, dv_far = attend_back(
+        q, k_own, k_far, v_own, v_far, bias_own, bias_far, lse, attn_low, g_attn
+    )
+    dk = (dk_own + swap(dk_far, 1).astype(jnp.float32)).astype(jnp.bfloat16)
+    dv = (dv_own + swap(dv_far, 1).astype(jnp.float32)).astype(jnp.bfloat16)
+    grad_qbias = jnp.sum(dq.astype(jnp.float32), 0)
+    grad_vbias = jnp.sum(dv.astype(jnp.float32), 0)
+    grad_q = rows_dot(dq, x)
+    grad_k = rows_dot(dk, x)
+    grad_v = rows_dot(dv, x)
+    input_grad = g_resid + plain_dot(dq, wq) + plain_dot(dk, wk) + plain_dot(dv, wv)
+    attn_total = reduced(
+        [
+            jnp.concatenate([m[r * hidden : (r + 1) * hidden] for m in (grad_o, grad_q, grad_k, grad_v)], 0)
+            for r in range(4)
+        ]
+    )
+
+    def absolute(vector):
+        parts = vector.reshape(4, -1)
+        return jnp.take(parts, jnp.arange(4) ^ (2 * side), 0).reshape(-1)
+
+    small_total = lax.psum(
+        jnp.concatenate(
+            [
+                absolute(grad_qbias),
+                absolute(grad_vbias),
+                absolute(grad_upbias),
+                grad_obias,
+                grad_attngain,
+                grad_attnshift,
+                grad_downbias,
+                grad_ffngain,
+                grad_ffnshift,
+            ]
+        ),
+        ("seq", "tp"),
+    )
+
+    def share(start, size):
+        whole = small_total[start : start + 4 * size].reshape(4, size)
+        return lax.dynamic_index_in_dim(whole, t, 0, False)
+
+    tail = 8 * hidden + 4 * units
+    rep = [small_total[tail + i * width : tail + (i + 1) * width] for i in range(6)]
+
+    def from_owner(array):
+        pieces = [array[k * BLOCK : (k + 1) * BLOCK] for k in range(n_dev)]
+        got = jnp.stack(seq_exchange(pieces, -1))
+        got = lax.dynamic_slice_in_dim(
+            jnp.concatenate([got, got], 0), (n_dev - me) % n_dev, n_dev, 0
+        )
+        r0, r1, r2, r3 = gathered_over_tp(got)
+        near = jnp.where(core == 0, jnp.stack([r0, r1], 1), jnp.stack([r1, r0], 1))
+        far = jnp.where(core == 0, jnp.stack([r2, r3], 1), jnp.stack([r3, r2], 1))
+        both = jnp.where(side == 0, jnp.stack([near, far], 1), jnp.stack([far, near], 1))
+        return both.reshape(seqs, rows, width)
+
+    layer_output = from_owner(out_low)
+    input_out = from_owner(input_grad.astype(jnp.bfloat16)).astype(jnp.float32)
+    g_o, g_q, g_k, g_v = (attn_total[i * hidden : (i + 1) * hidden] for i in range(4))
+    return (
+        layer_output,
+        input_out,
+        g_q.T,
+        share(0, hidden),
+        g_k.T,
+        g_v.T,
+        share(4 * hidden, hidden),
+        g_o,
+        rep[0],
+        rep[1],
+        rep[2],
+        ffn_total[units:],
+        share(8 * hidden, units),
+        ffn_total[:units],
+        rep[3],
+        rep[4],
+        rep[5],
+    )
+
+
+def per_device(tokens, *rest):
+    seqs, rows, _ = tokens.shape
+    n_dev = lax.axis_size("seq")
+    if lax.axis_size("tp") == 4 and seqs == 2 * n_dev and rows == 2 * BLOCK:
+        return whole_sequences(tokens, *rest)
+    return split_sequences(tokens, *rest)
+
+
 def solution(mesh):
     placed = (
         P(None, "seq", None),

time: 2490 us -> 611 us (0.25)
  waiting for transfers between devices: 992 us -> 254 us
  blocking collectives: 495 us -> 54 us
  local copies, waits for them, and re-layouts: 426 us -> 73.5 us
  other arithmetic: 293 us -> 50.8 us
  matrix products: 230 us -> 58.9 us
  starting transfers between devices: 24.5 us -> 61.2 us
  Pallas kernels: 0 us -> 34.2 us
    psum x8 -> x1, waiting for transfers between devices: 864 us -> 68.4 us  [reduced(): return lax.psum(mine.astype(jnp.bfloat16), 'seq').astype(jnp.float32)]
    all_gather x2 -> x0, blocking collectives: 258 us -> none  [joined(): everything = jax.tree.map(lambda part: lax.all_gather(part, axis), shard)]
    psum x2 -> x1, blocking collectives: 237 us -> 54 us  [whole_sequences(): lax.psum(jnp.concatenate([absolute(grad_qbias), absolute(grad_vbias), abs...]
    dot_general x12 -> x0, matrix products: 153 us -> none  [the longest x1 47.6 us: per_device(): jnp.einsum('sbhqk,sbhqd->sbhkd', grad_score, q_blocks, preferred_element_...]
    scatter-add x1 -> x0, other arithmetic: 90 us -> none  [per_device(): table_grad = jnp.zeros((seqs * per_dev * heads, block, 2 * hsize), jnp.fl...]
    reshape x18 -> x9, local copies, waits for them, and re-layouts: 64.9 us -> 1.42 us  [the longest x3 0.85 us: absolute(): parts = vector.reshape(4, -1)]
    add x18 -> x3, other arithmetic: 59.9 us -> 0.1 us  [key_bias(): one(k == 0) + one(k == n_blocks - 1) + one((k == b - 1) & (b != 1))]
    ppermute x4 -> x57, waiting for transfers between devices: 127 us -> 186 us  [the longest x29 94.4 us: swap(): return lax.ppermute(piece, 'tp', [(i, i ^ bits) for i in range(size)])]
  transfers between devices with their start and end apart: 15 -> 58, of which waited for: 11 -> 26; matrix products, arithmetic and copies ran while one was open for 15% -> 17% of each run, Pallas kernels for 0% -> 0%
where the time goes in v1:
time: 611 us; the launch traced here: 603 us
  waiting for transfers between devices  254 us (42%)
  local copies, waits for them, and re-layouts  73.5 us (12%)
  starting transfers between devices  61.2 us (10%)
  matrix products  58.9 us (10%)
  blocking collectives  54 us (9%)
  other arithmetic  50.8 us (8%)
  Pallas kernels  34.2 us (6%)
  between operations  16.5 us (3%)
    ppermute x29, waiting for transfers between devices, swap(): return lax.ppermute(piece, 'tp', [(i, i ^ bits) for i in range(size)])  94.4 us
    ppermute x28, waiting for transfers between devices, seq_exchange(): lax.ppermute(pieces[k], 'seq', [(i, (i + sign * k) % size) for i in range...  91.6 us
    psum x1, waiting for transfers between devices, reduced(): return lax.psum(mine.astype(jnp.bfloat16), 'seq').astype(jnp.float32)  68.4 us
    psum x1, blocking collectives, whole_sequences(): lax.psum(jnp.concatenate([absolute(grad_qbias), absolute(grad_vbias), abs...  54 us
    ppermute x28, starting transfers between devices, seq_exchange(): lax.ppermute(pieces[k], 'seq', [(i, (i + sign * k) % size) for i in range...  44.7 us
    unnamed x309, local copies, waits for them, and re-layouts  31.4 us
    dot_general x9, matrix products, rows_dot(): lax.dot_general(left, right, (((0,), (0,)), ((), ())), preferred_element_...  21.9 us
    dot_general x6, matrix products, back_dot(): lax.dot_general(left, right, (((1,), (1,)), ((), ())), preferred_element_...  21.1 us
  transfers between devices with their start and end apart: 58, of which 26 were waited for; matrix products, arithmetic and copies ran while one was open for 17% of the time, Pallas kernels for 0%

profile of v1, /device:TPU:0, one launch (start us, length us, event | category | flops | bytes accessed | tf_op | source)
XLA Modules:
  0.0 603.5 jit_solution(6669957559842867364)
XLA Ops:
  34.6 5.3 collective-permute-done.1
  40.0 6.6 %collective-permute-done.2 = bf16[64,768]{1,0:T(8,128)(2,1)S(1)} collective-permute-done((bf16[64,768]{1,0:T(8,128)(2,1)}, bf16[64,768]{1,0:T(8,128)(2,1)S(1)}, u32[]{:S(2)}, u32[]{:S(2)}) %collective-permute-start.2) | collective-permute-done | bytes 98336 | tf_op jit(solution)/shard_map/ppermute | solution.py:605
  46.6 6.4 %collective-permute-done.3 = bf16[64,768]{1,0:T(8,128)(2,1)S(1)} collective-permute-done((bf16[64,768]{1,0:T(8,128)(2,1)}, bf16[64,768]{1,0:T(8,128)(2,1)S(1)}, u32[]{:S(2)}, u32[]{:S(2)}) %collective-permute-start.3) | collective-permute-done | bytes 98336 | tf_op jit(solution)/shard_map/ppermute | solution.py:605
  53.1 5.6 collective-permute-done.4
  71.3 7.9 %collective-permute-done.34 = bf16[64,768]{1,0:T(8,128)(2,1)S(1)} collective-permute-done((bf16[64,768]{1,0:T(8,128)(2,1)}, bf16[64,768]{1,0:T(8,128)(2,1)S(1)}, u32[]{:S(2)}, u32[]{:S(2)}) %collective-permute-start.34) | collective-permute-done | bytes 98336 | tf_op jit(solution)/shard_map/ppermute | solution.py:605
  79.2 6.6 %collective-permute-done.35 = bf16[64,768]{1,0:T(8,128)(2,1)S(1)} collective-permute-done((bf16[64,768]{1,0:T(8,128)(2,1)}, bf16[64,768]{1,0:T(8,128)(2,1)S(1)}, u32[]{:S(2)}, u32[]{:S(2)}) %collective-permute-start.35) | collective-permute-done | bytes 98336 | tf_op jit(solution)/shard_map/ppermute | solution.py:605
  85.8 6.6 %collective-permute-done.36 = bf16[64,768]{1,0:T(8,128)(2,1)S(1)} collective-permute-done((bf16[64,768]{1,0:T(8,128)(2,1)}, bf16[64,768]{1,0:T(8,128)(2,1)S(1)}, u32[]{:S(2)}, u32[]{:S(2)}) %collective-permute-start.36) | collective-permute-done | bytes 98336 | tf_op jit(solution)/shard_map/ppermute | solution.py:605
  92.5 6.0 collective-permute-done.37
  123.2 21.0 %collective-permute-done.19 = bf16[768,768]{1,0:T(8,128)(2,1)S(1)} collective-permute-done((bf16[768,768]{1,0:T(8,128)(2,1)}, bf16[768,768]{1,0:T(8,128)(2,1)S(1)}, u32[]{:S(2)}, u32[]{:S(2)}) %collective-permute-start.19) | collective-permute-done | bytes 1179680 | tf_op jit(solution)/shard_map/ppermute | solution.py:589
  144.2 24.9 %collective-permute-done.22 = bf16[768,768]{1,0:T(8,128)(2,1)S(1)} collective-permute-done((bf16[768,768]{1,0:T(8,128)(2,1)}, bf16[768,768]{1,0:T(8,128)(2,1)S(1)}, u32[]{:S(2)}, u32[]{:S(2)}) %collective-permute-start.22) | collective-permute-done | bytes 1179680 | tf_op jit(solution)/shard_map/ppermute | solution.py:589
  180.9 13.6 %shard_map.305 = (bf16[512,768]{1,0:T(8,128)(2,1)S(1)}, f32[6,2,512]{2,1,0:T(2,128)S(1)}) custom-call(bf16[512,768]{1,0:T(8,128)(2,1)S(1)} %add_convert_fusion.9.q_ref, bf16[512,768]{1,0:T(8,128)(2,1)S(1)} %convolution_convert_fusion.1.ko_ref, bf16[512,768]{1,0:T(8,128)(2,1)S(1)} %collective-permute-done.13.kx_ref, ...), custom_call_target="tpu_custom_call" | custom-call | flops 6442450944 | bytes 4718592 | tf_op jit(solution)/shard_map/pallas_call | solution.py:548
  197.5 7.1 %multiply_convert_fusion.1 = (bf16[512,3072]{1,0:T(8,128)(2,1)S(1)}, f32[512,3072]{1,0:T(8,128)}) fusion(f32[3072]{0:T(1024)S(1)} %pad_maximum_fusion.31, bf16[512,768]{1,0:T(8,128)(2,1)S(1)} %fusion.13, bf16[768,768]{1,0:T(8,128)(2,1)S(1)} %copy-done.68, bf16[768,768]{1,0:T(8,128)(2,1)S(1)} %copy-done.67, bf16[768,768]{1,0:T(8,128)(2,1)S(1)} %get-tuple-element.100, ...), kind=kOutput, calls=%fused_computation.12 | convolution fusion | flops 2444230656 | bytes 14954496 | tf_op jit(solution)/shard_map/dot_general | solution.py:51
  210.8 9.7 %convert_reduce_fusion = (f32[3072]{0:T(1024)S(1)}, bf16[512,3072]{1,0:T(8,128)(2,1)S(1)}) fusion(f32[512,3072]{1,0:T(8,128)} %get-tuple-element.175, f32[3072]{0:T(1024)S(1)} %pad_maximum_fusion.31, bf16[768,768]{1,0:T(8,128)(2,1)} %get-tuple-element.98, bf16[768,768]{1,0:T(8,128)(2,1)} %copy-done.69, bf16[768,768]{1,0:T(8,128)(2,1)} %get-tuple-element.96, ...), kind=kOutput, calls=%fused_computation.10 | convolution fusion | flops 2458776576 | bytes 15753216 | tf_op jit(solution)/shard_map/dot_general | solution.py:61
  220.5 7.3 %multiply_reduce_fusion = (f32[768]{0:T(1024)}, f32[512]{0:T(512)S(1)}, f32[512]{0:T(512)S(1)}, f32[768]{0:T(1024)}, f32[512,768]{1,0:T(8,128)S(1)}) fusion(f32[512,768]{1,0:T(8,128)S(1)} %get-tuple-element.173, f32[512]{0:T(512)S(1)} %add_rsqrt_fusion.1, f32[512]{0:T(512)S(1)} %broadcast_multiply_fusion.5, f32[768]{0:T(1024)S(1)} %copy-done.109, ...), kind=kOutput, calls=%fused_computation.52 | convolution fusion | flops 2438723072 | bytes 12600320 | tf_op jit(solution)/shard_map/dot_general | solution.py:61
  232.9 20.6 %shard_map.306 = (bf16[512,768]{1,0:T(8,128)(2,1)S(1)}, f32[512,768]{1,0:T(8,128)}, bf16[512,768]{1,0:T(8,128)(2,1)S(1)}, f32[512,768]{1,0:T(8,128)}, bf16[512,768]{1,0:T(8,128)(2,1)S(1)}) custom-call(bf16[512,768]{1,0:T(8,128)(2,1)S(1)} %add_convert_fusion.9.q_ref, bf16[512,768]{1,0:T(8,128)(2,1)S(1)} %convolution_convert_fusion.1.ko_ref, ...), custom_call_target="tpu_custom_call" | custom-call | flops 16106127360 | bytes 11796480 | tf_op jit(solution)/shard_map/pallas_call | solution.py:572
  267.2 5.3 fusion.52
  274.9 4.7 collective-permute-start.28
  287.1 4.5 fusion.57
  344.3 4.3 collective-permute-start.43
  376.2 6.4 %collective-permute-done.48 = bf16[64,768]{1,0:T(8,128)(2,1)S(1)} collective-permute-done((bf16[64,768]{1,0:T(8,128)(2,1)S(1)}, bf16[64,768]{1,0:T(8,128)(2,1)S(1)}, u32[]{:S(2)}, u32[]{:S(2)}) %collective-permute-start.48) | collective-permute-done | bytes 98336 | tf_op jit(solution)/shard_map/ppermute | solution.py:605
  382.9 6.9 %collective-permute-done.49 = bf16[64,768]{1,0:T(8,128)(2,1)S(1)} collective-permute-done((bf16[64,768]{1,0:T(8,128)(2,1)S(1)}, bf16[64,768]{1,0:T(8,128)(2,1)S(1)}, u32[]{:S(2)}, u32[]{:S(2)}) %collective-permute-start.49) | collective-permute-done | bytes 98336 | tf_op jit(solution)/shard_map/ppermute | solution.py:605
  391.9 48.4 %collective-permute-done.54 = bf16[768,768]{1,0:T(8,128)(2,1)S(1)} collective-permute-done((bf16[768,768]{1,0:T(8,128)(2,1)S(1)}, bf16[768,768]{1,0:T(8,128)(2,1)S(1)}, u32[]{:S(2)}, u32[]{:S(2)}) %collective-permute-start.54) | collective-permute-done | bytes 1179680 | tf_op jit(solution)/shard_map/ppermute | solution.py:589
  450.1 54.0 %psum.22 = f32[9216]{0:T(1024)S(1)} all-reduce(f32[9216]{0:T(1024)S(1)} %constant_dynamic-update-slice_fusion.49), channel_id=1, replica_groups=mesh['seq'=8,'tp'=4] {'seq','tp'}, use_global_device_ids=true, to_apply=%region_18.20 | all-reduce | flops 9216 | bytes 73728 | tf_op jit(solution)/shard_map/psum | solution.py:791
  520.9 68.4 %all-reduce.3.cloned.1.call-done = (bf16[768,768]{1,0:T(8,128)(2,1)}, bf16[1536,768]{1,0:T(8,128)(2,1)}) async-done(((bf16[768,768]{1,0:T(8,128)(2,1)}, bf16[1536,768]{1,0:T(8,128)(2,1)}), (bf16[768,768]{1,0:T(8,128)(2,1)}, bf16[1536,768]{1,0:T(8,128)(2,1)})) %all-reduce.3.cloned.1.call-update) | async-done | bytes 3538960 | tf_op jit(solution)/shard_map/psum | solution.py:754
  (569 shorter events, 228.7 us)
Async XLA Ops:
  7.2 582.0 %all-reduce.3.cloned.1.call-start = ((), (), s32[]{:S(2)}) async-start(), calls=%async_computation | async-start | bytes 7077888 | tf_op jit(solution)/shard_map/psum | solution.py:754
  7.2 108.0 %collective-permute-start.15 = (bf16[192,768]{1,0:T(8,128)(2,1)}, bf16[192,768]{1,0:T(8,128)(2,1)}, u32[]{:S(2)}, u32[]{:S(2)}) collective-permute-start(bf16[192,768]{1,0:T(8,128)(2,1)} %param.27), channel_id=1, source_target_pairs={{0,1},{1,0},{2,3},{3,2},{4,5},{5,4},{6,7},{7,6},{8,9},{9,8},{10,11... | collective-permute-start | bytes 884744 | tf_op jit(solution)/shard_map/ppermute | solution.py:589
  7.8 92.2 %collective-permute-start.16 = (bf16[192,768]{1,0:T(8,128)(2,1)}, bf16[192,768]{1,0:T(8,128)(2,1)}, u32[]{:S(2)}, u32[]{:S(2)}) collective-permute-start(bf16[192,768]{1,0:T(8,128)(2,1)} %param.27), channel_id=1, source_target_pairs={{0,2},{1,3},{2,0},{3,1},{4,6},{5,7},{6,4},{7,5},{8,10},{9,11},{10,... | collective-permute-start | bytes 884744 | tf_op jit(solution)/shard_map/ppermute | solution.py:589
  23.6 93.7 %collective-permute-start.8 = (bf16[576,768]{1,0:T(8,128)(2,1)}, bf16[576,768]{1,0:T(8,128)(2,1)}, u32[]{:S(2)}, u32[]{:S(2)}) collective-permute-start(bf16[576,768]{1,0:T(8,128)(2,1)} %pad_maximum_fusion.16), channel_id=1, source_target_pairs={{0,2},{1,3},{2,0},{3,1},{4,6},{5,7},{6,4},{7,5},{8,10},{9,11},{10,... | collective-permute-start | bytes 2654216 | tf_op jit(solution)/shard_map/ppermute | solution.py:589
  25.0 96.0 %collective-permute-start.7 = (bf16[576,768]{1,0:T(8,128)(2,1)}, bf16[576,768]{1,0:T(8,128)(2,1)}, u32[]{:S(2)}, u32[]{:S(2)}) collective-permute-start(bf16[576,768]{1,0:T(8,128)(2,1)} %pad_maximum_fusion.16), channel_id=1, source_target_pairs={{0,1},{1,0},{2,3},{3,2},{4,5},{5,4},{6,7},{7,6},{8,9},{9,8},{10,11... | collective-permute-start | bytes 2654216 | tf_op jit(solution)/shard_map/ppermute | solution.py:589
  115.2 53.9 %collective-permute-start.18 = (bf16[768,768]{1,0:T(8,128)(2,1)}, bf16[768,768]{1,0:T(8,128)(2,1)S(1)}, u32[]{:S(2)}, u32[]{:S(2)}) collective-permute-start(bf16[768,768]{1,0:T(8,128)(2,1)} %param.31), channel_id=1, source_target_pairs={{0,1},{1,0},{2,3},{3,2},{4,5},{5,4},{6,7},{7,6},{8,9},{9,8},{10,11... | collective-permute-start | bytes 3538952 | tf_op jit(solution)/shard_map/ppermute | solution.py:589
  115.2 29.0 %collective-permute-start.19 = (bf16[768,768]{1,0:T(8,128)(2,1)}, bf16[768,768]{1,0:T(8,128)(2,1)S(1)}, u32[]{:S(2)}, u32[]{:S(2)}) collective-permute-start(bf16[768,768]{1,0:T(8,128)(2,1)} %param.31), channel_id=1, source_target_pairs={{0,2},{1,3},{2,0},{3,1},{4,6},{5,7},{6,4},{7,5},{8,10},{9,11},{10,... | collective-permute-start | bytes 3538952 | tf_op jit(solution)/shard_map/ppermute | solution.py:589
  116.8 52.3 %collective-permute-start.22 = (bf16[768,768]{1,0:T(8,128)(2,1)}, bf16[768,768]{1,0:T(8,128)(2,1)S(1)}, u32[]{:S(2)}, u32[]{:S(2)}) collective-permute-start(bf16[768,768]{1,0:T(8,128)(2,1)} %param.33), channel_id=1, source_target_pairs={{0,2},{1,3},{2,0},{3,1},{4,6},{5,7},{6,4},{7,5},{8,10},{9,11},{10,... | collective-permute-start | bytes 3538952 | tf_op jit(solution)/shard_map/ppermute | solution.py:589
  117.3 53.3 %collective-permute-start.21 = (bf16[768,768]{1,0:T(8,128)(2,1)}, bf16[768,768]{1,0:T(8,128)(2,1)S(1)}, u32[]{:S(2)}, u32[]{:S(2)}) collective-permute-start(bf16[768,768]{1,0:T(8,128)(2,1)} %param.33), channel_id=1, source_target_pairs={{0,1},{1,0},{2,3},{3,2},{4,5},{5,4},{6,7},{7,6},{8,9},{9,8},{10,11... | collective-permute-start | bytes 3538952 | tf_op jit(solution)/shard_map/ppermute | solution.py:589
  121.0 52.4 %collective-permute-start.9 = (bf16[576,768]{1,0:T(8,128)(2,1)}, bf16[576,768]{1,0:T(8,128)(2,1)S(1)}, u32[]{:S(2)}, u32[]{:S(2)}) collective-permute-start(bf16[576,768]{1,0:T(8,128)(2,1)} %collective-permute-done.8), channel_id=1, source_target_pairs={{0,1},{1,0},{2,3},{3,2},{4,5},{5,4},{6,7},{7,6},{8,9},{9,8},{10,11... | collective-permute-start | bytes 2654216 | tf_op jit(solution)/shard_map/ppermute | solution.py:589
  144.2 33.9 %collective-permute-start.20 = (bf16[768,768]{1,0:T(8,128)(2,1)S(1)}, bf16[768,768]{1,0:T(8,128)(2,1)S(1)}, u32[]{:S(2)}, u32[]{:S(2)}) collective-permute-start(bf16[768,768]{1,0:T(8,128)(2,1)S(1)} %collective-permute-done.19), channel_id=1, source_target_pairs={{0,1},{1,0},{2,3},{3,2},{4,5},{5,4},{6,7},{7,6},{8,9},{9,8},{10,11... | collective-permute-start | bytes 3538952 | tf_op jit(solution)/shard_map/ppermute | solution.py:589
  273.4 42.9 %collective-permute-start.30 = (bf16[64,768]{1,0:T(8,128)(2,1)S(1)}, bf16[64,768]{1,0:T(8,128)(2,1)S(1)}, u32[]{:S(2)}, u32[]{:S(2)}) collective-permute-start(bf16[64,768]{1,0:T(8,128)(2,1)S(1)} %get-tuple-element.127), channel_id=1, source_target_pairs={{0,4},{4,8},{8,12},{12,16},{16,20},{20,24},{24,28},{28,0},{1,5},{5... | collective-permute-start | bytes 294920 | tf_op jit(solution)/shard_map/ppermute | solution.py:605
  274.9 40.8 %collective-permute-start.29 = (bf16[64,768]{1,0:T(8,128)(2,1)S(1)}, bf16[64,768]{1,0:T(8,128)(2,1)S(1)}, u32[]{:S(2)}, u32[]{:S(2)}) collective-permute-start(bf16[64,768]{1,0:T(8,128)(2,1)S(1)} %get-tuple-element.128), channel_id=1, source_target_pairs={{0,8},{4,12},{8,16},{12,20},{16,24},{20,28},{24,0},{28,4},{1,9},{5... | collective-permute-start | bytes 294920 | tf_op jit(solution)/shard_map/ppermute | solution.py:605
  274.9 40.1 %collective-permute-start.28 = (bf16[64,768]{1,0:T(8,128)(2,1)S(1)}, bf16[64,768]{1,0:T(8,128)(2,1)S(1)}, u32[]{:S(2)}, u32[]{:S(2)}) collective-permute-start(bf16[64,768]{1,0:T(8,128)(2,1)S(1)} %get-tuple-element.129), channel_id=1, source_target_pairs={{0,12},{4,16},{8,20},{12,24},{16,28},{20,0},{24,4},{28,8},{1,13},{... | collective-permute-start | bytes 294920 | tf_op jit(solution)/shard_map/ppermute | solution.py:605
  279.6 34.2 %collective-permute-start.27 = (bf16[64,768]{1,0:T(8,128)(2,1)S(1)}, bf16[64,768]{1,0:T(8,128)(2,1)S(1)}, u32[]{:S(2)}, u32[]{:S(2)}) collective-permute-start(bf16[64,768]{1,0:T(8,128)(2,1)S(1)} %get-tuple-element.130), channel_id=1, source_target_pairs={{0,16},{4,20},{8,24},{12,28},{16,0},{20,4},{24,8},{28,12},{1,17},{... | collective-permute-start | bytes 294920 | tf_op jit(solution)/shard_map/ppermute | solution.py:605
  279.6 23.4 %collective-permute-start.24 = (bf16[64,768]{1,0:T(8,128)(2,1)S(1)}, bf16[64,768]{1,0:T(8,128)(2,1)S(1)}, u32[]{:S(2)}, u32[]{:S(2)}) collective-permute-start(bf16[64,768]{1,0:T(8,128)(2,1)S(1)} %get-tuple-element.133), channel_id=1, source_target_pairs={{0,28},{4,0},{8,4},{12,8},{16,12},{20,16},{24,20},{28,24},{1,29},{... | collective-permute-start | bytes 294920 | tf_op jit(solution)/shard_map/ppermute | solution.py:605
  315.0 42.5 %collective-permute-start.55 = (bf16[3072,768]{1,0:T(8,128)(2,1)}, bf16[3072,768]{1,0:T(8,128)(2,1)}, u32[]{:S(2)}, u32[]{:S(2)}) collective-permute-start(bf16[3072,768]{1,0:T(8,128)(2,1)} %pad_maximum_fusion.6), channel_id=1, source_target_pairs={{0,1},{1,0},{2,3},{3,2},{4,5},{5,4},{6,7},{7,6},{8,9},{9,8},{10,11... | collective-permute-start | bytes 14155784 | tf_op jit(solution)/shard_map/ppermute | solution.py:589
  325.2 181.9 %collective-permute-start.31 = (bf16[8,64,768]{2,1,0:T(8,128)(2,1)}, bf16[8,64,768]{2,1,0:T(8,128)(2,1)}, u32[]{:S(2)}, u32[]{:S(2)}) collective-permute-start(bf16[8,64,768]{2,1,0:T(8,128)(2,1)} %constant_dynamic-slice_fusion.4), channel_id=1, source_target_pairs={{0,1},{1,0},{2,3},{3,2},{4,5},{5,4},{6,7},{7,6},{8,9},{9,8},{10,11... | collective-permute-start | bytes 2359304 | tf_op jit(solution)/shard_map/ppermute | solution.py:589
  325.7 124.3 %collective-permute-start.32 = (bf16[8,64,768]{2,1,0:T(8,128)(2,1)}, bf16[8,64,768]{2,1,0:T(8,128)(2,1)}, u32[]{:S(2)}, u32[]{:S(2)}) collective-permute-start(bf16[8,64,768]{2,1,0:T(8,128)(2,1)} %constant_dynamic-slice_fusion.4), channel_id=1, source_target_pairs={{0,2},{1,3},{2,0},{3,1},{4,6},{5,7},{6,4},{7,5},{8,10},{9,11},{10,... | collective-permute-start | bytes 2359304 | tf_op jit(solution)/shard_map/ppermute | solution.py:589
  338.8 27.7 %collective-permute-start.53 = (bf16[1536,768]{1,0:T(8,128)(2,1)}, bf16[1536,768]{1,0:T(8,128)(2,1)}, u32[]{:S(2)}, u32[]{:S(2)}) collective-permute-start(bf16[1536,768]{1,0:T(8,128)(2,1)} %pad_maximum_fusion.11), channel_id=1, source_target_pairs={{0,1},{1,0},{2,3},{3,2},{4,5},{5,4},{6,7},{7,6},{8,9},{9,8},{10,11... | collective-permute-start | bytes 7077896 | tf_op jit(solution)/shard_map/ppermute | solution.py:589
  366.0 77.4 %collective-permute-start.56 = (bf16[1536,768]{1,0:T(8,128)(2,1)S(1)}, bf16[1536,768]{1,0:T(8,128)(2,1)S(1)}, u32[]{:S(2)}, u32[]{:S(2)}) collective-permute-start(bf16[1536,768]{1,0:T(8,128)(2,1)S(1)} %add_convert_fusion.1), channel_id=1, source_target_pairs={{0,2},{1,3},{2,0},{3,1},{4,6},{5,7},{6,4},{7,5},{8,10},{9,11},{10,... | collective-permute-start | bytes 7077896 | tf_op jit(solution)/shard_map/ppermute | solution.py:589
  372.6 67.7 %collective-permute-start.54 = (bf16[768,768]{1,0:T(8,128)(2,1)S(1)}, bf16[768,768]{1,0:T(8,128)(2,1)S(1)}, u32[]{:S(2)}, u32[]{:S(2)}) collective-permute-start(bf16[768,768]{1,0:T(8,128)(2,1)S(1)} %add_convert_fusion.3), channel_id=1, source_target_pairs={{0,2},{1,3},{2,0},{3,1},{4,6},{5,7},{6,4},{7,5},{8,10},{9,11},{10,... | collective-permute-start | bytes 3538952 | tf_op jit(solution)/shard_map/ppermute | solution.py:589
  449.4 57.2 %collective-permute-start.51 = (bf16[8,64,768]{2,1,0:T(8,128)(2,1)S(1)}, bf16[8,64,768]{2,1,0:T(8,128)(2,1)}, u32[]{:S(2)}, u32[]{:S(2)}) collective-permute-start(bf16[8,64,768]{2,1,0:T(8,128)(2,1)S(1)} %constant_dynamic-slice_fusion.3), channel_id=1, source_target_pairs={{0,2},{1,3},{2,0},{3,1},{4,6},{5,7},{6,4},{7,5},{8,10},{9,11},{10,... | collective-permute-start | bytes 2359304 | tf_op jit(solution)/shard_map/ppermute | solution.py:589
  450.0 58.8 %collective-permute-start.33 = (bf16[8,64,768]{2,1,0:T(8,128)(2,1)}, bf16[8,64,768]{2,1,0:T(8,128)(2,1)}, u32[]{:S(2)}, u32[]{:S(2)}) collective-permute-start(bf16[8,64,768]{2,1,0:T(8,128)(2,1)} %collective-permute-done.32), channel_id=1, source_target_pairs={{0,1},{1,0},{2,3},{3,2},{4,5},{5,4},{6,7},{7,6},{8,9},{9,8},{10,11... | collective-permute-start | bytes 2359304 | tf_op jit(solution)/shard_map/ppermute | solution.py:589
  (163 other events, 2231.0 us)
Sparse Core Ops, SparseCore 0:
  448.0 141.2 all-reduce.2

commit v2 on v0

--- a/solution.py
+++ b/solution.py
@@ -1,7 +1,11 @@
+from functools import partial
+
 import jax
 import jax.numpy as jnp
 from jax import lax
 from jax.sharding import PartitionSpec as P
+from jax.experimental import pallas as pl
+from jax.experimental.pallas import tpu as pltpu
 
 HD = 64
 BLOCK = 64
@@ -126,7 +130,7 @@
     )
 
 
-def per_device(
+def split_sequences(
     tokens,
     rand_blocks,
     query_weight,
@@ -461,6 +465,937 @@
     )
 
 
+HALF_ROOT = 0.7071067811865476
+PDF_SCALE = 0.3989422804014327
+
+
+MESH = pl.DeviceIdType.MESH
+
+
+def place():
+    me, t = lax.axis_index("seq"), lax.axis_index("tp")
+    side, core = lax.div(t, 2), lax.rem(t, 2)
+    return me, t, side, core
+
+
+def tp_peer(side, core, bits):
+    there = 1 - side if bits & 2 else side
+    return there * 2 + (1 - core if bits & 1 else core)
+
+
+def greet(peers):
+    barrier = pltpu.get_barrier_semaphore()
+    for peer in peers:
+        pl.semaphore_signal(barrier, inc=1, device_id=peer, device_id_type=MESH)
+    pl.semaphore_wait(barrier, len(peers))
+
+
+def remote(src, dst, sends, recvs, at, peer):
+    return pltpu.make_async_remote_copy(
+        src_ref=src,
+        dst_ref=dst,
+        send_sem=sends.at[at],
+        recv_sem=recvs.at[at],
+        device_id=peer,
+        device_id_type=MESH,
+    )
+
+
+def enter_kernel(
+    n_dev, tok, rand, wq, wk, wv, pack,
+    x, q, ko, vo, kf, vf, wt_out, packs, ids,
+    wt, rand_v, ids_for, tok_send, tok_recv, w_send, w_recv, s_send, s_recv, kv_send, kv_recv, local,
+):
+    me, t, side, core = place()
+    half = lax.rem(me, 2)
+    beside = (me + 1 - 2 * half, t)
+    near, across = (me, tp_peer(side, core, 1)), (me, tp_peer(side, core, 2))
+    hidden = wq.shape[1]
+    part = hidden // 2
+    greet(
+        [(lax.rem(me + k, n_dev), t) for k in range(1, n_dev)]
+        + [(me, tp_peer(side, core, bits)) for bits in (1, 2, 3)]
+    )
+    own_tok = pltpu.make_async_copy(
+        tok.at[2 * me + side, pl.ds(core * BLOCK, BLOCK), :], x.at[pl.ds(0, BLOCK), :], local.at[0]
+    )
+    own_rand = pltpu.make_async_copy(rand.at[pl.ds(2 * me, 2)], rand_v, local.at[1])
+    own_rand.start()
+    own_tok.start()
+    moves = []
+    for k in range(1, n_dev):
+        to = lax.rem(me + k, n_dev)
+        move = remote(
+            tok.at[2 * to + side, pl.ds(core * BLOCK, BLOCK), :],
+            x.at[pl.ds(k * BLOCK, BLOCK), :],
+            tok_send, tok_recv, k - 1, (to, t),
+        )
+        move.start()
+        moves.append(move)
+
+    def rows(h):
+        return pl.ds(h * part, part)
+
+    weights = {}
+    for m, w in ((1, wk), (2, wv), (0, wq)):
+        wt[m, core] = w[...].T
+        to_y = remote(
+            wt.at[m, core, rows(half)], wt.at[m, 2 + core, rows(half)], w_send, w_recv, (m, 0), across
+        )
+        to_core = remote(wt.at[m, core], wt.at[m, core], w_send, w_recv, (m, 1), near)
+        to_y.start()
+        to_core.start()
+        weights[m] = [to_y, to_core]
+
+    packs[core] = pack[...]
+    own_rand.wait()
+    lane = lax.broadcasted_iota(jnp.int32, (1, n_dev * BLOCK), 1)
+    for y in range(2):
+        for c in range(2):
+            tiles = [
+                rand_v[y, 2 * lax.rem(me - i + n_dev, n_dev) + c] for i in range(n_dev)
+            ]
+            for h in range(tiles[0].shape[0]):
+                for r in range(3):
+                    row = jnp.broadcast_to(tiles[0][h : h + 1, r : r + 1], lane.shape)
+                    for i in range(1, n_dev):
+                        row = jnp.where(lane // BLOCK == i, tiles[i][h : h + 1, r : r + 1], row)
+                    ids_for[2 * y + c, h, r : r + 1, :] = row
+    heads = ids_for.shape[1]
+    ids[pl.ds(core * heads, heads)] = ids_for[t]
+    for bits in (1, 2, 3):
+        slot = (bits & 2) + core
+        to = tp_peer(side, core, bits)
+        for n, (src, dst) in enumerate(
+            ((pack, packs.at[slot]), (ids_for.at[to], ids.at[pl.ds(slot * heads, heads)]))
+        ):
+            move = remote(src, dst, s_send, s_recv, (bits - 1, n), (me, to))
+            move.start()
+            moves.append(move)
+
+    for m in (1, 2, 0):
+        weights[m][0].wait_recv()
+        held = wt.at[m, 2 + core, rows(half)]
+        for n, peer in ((2, beside), (3, near)):
+            move = remote(held, held, w_send, w_recv, (m, n), peer)
+            move.start()
+            weights[m].append(move)
+    for m in (1, 2, 0):
+        weights[m][2].wait_recv()
+        held = wt.at[m, 2 + core, rows(1 - half)]
+        move = remote(held, held, w_send, w_recv, (m, 4), near)
+        move.start()
+        weights[m].append(move)
+    for move in moves:
+        move.wait_recv()
+    own_tok.wait()
+
+    def bias_of(start):
+        return jnp.concatenate([packs[j, :, start : start + hidden] for j in range(4)], 1)
+
+    def project(m):
+        for n in (1, 3, 4):
+            weights[m][n].wait_recv()
+        return back_dot(x[...], wt[m].reshape(4 * hidden, x.shape[1]))
+
+    sends = []
+    ko[...] = project(1).astype(jnp.bfloat16)
+    sends.append(remote(ko, kf, kv_send, kv_recv, 0, near))
+    sends[0].start()
+    pad = pack.shape[1] - 2 * hidden
+    vo[...] = (project(2) + bias_of(256)).astype(jnp.bfloat16)
+    sends.append(remote(vo, vf, kv_send, kv_recv, 1, near))
+    sends[1].start()
+    q[...] = (project(0) + bias_of(0)).astype(jnp.bfloat16)
+    keep = pltpu.make_async_copy(wt, wt_out, local.at[2])
+    keep.start()
+    for move in sends:
+        move.wait_recv()
+    for move in moves + sends + [move for m in range(3) for move in weights[m]]:
+        move.wait_send()
+    keep.wait()
+
+
+def enter(tokens, rand_blocks, wq, wk, wv, pack, n_dev):
+    width = tokens.shape[2]
+    span = n_dev * BLOCK
+    hidden = wq.shape[1]
+    heads = hidden // HD
+    vmem = pl.BlockSpec(memory_space=pltpu.VMEM)
+    hbm = pl.BlockSpec(memory_space=pl.ANY)
+    low = jax.ShapeDtypeStruct((span, width), jnp.bfloat16)
+    wt = (3, 4, hidden, width)
+    dma = pltpu.SemaphoreType.DMA
+    return pl.pallas_call(
+        partial(enter_kernel, n_dev),
+        in_specs=[hbm, hbm, vmem, vmem, vmem, vmem],
+        out_specs=[vmem] * 6 + [hbm, vmem, vmem],
+        out_shape=[low] * 6
+        + [
+            jax.ShapeDtypeStruct(wt, jnp.bfloat16),
+            jax.ShapeDtypeStruct((4,) + pack.shape, jnp.float32),
+            jax.ShapeDtypeStruct((4 * heads, 3, span), jnp.int32),
+        ],
+        scratch_shapes=[
+            pltpu.VMEM(wt, jnp.bfloat16),
+            pltpu.VMEM((2,) + rand_blocks.shape[1:], jnp.int32),
+            pltpu.VMEM((4, heads, 3, span), jnp.int32),
+            dma((n_dev - 1,)),
+            dma((n_dev - 1,)),
+            dma((3, 5)),
+            dma((3, 5)),
+            dma((3, 2)),
+            dma((3, 2)),
+            dma((2,)),
+            dma((2,)),
+            dma((3,)),
+        ],
+        compiler_params=pltpu.CompilerParams(
+            collective_id=0, has_side_effects=True, vmem_limit_bytes=48 * 2**20
+        ),
+    )(tokens, rand_blocks, wq, wk, wv, pack)
+
+
+def list_bias(ids_ref, h, key_shift, me, core, n_dev, span):
+    n_blocks = 2 * n_dev
+    row = lax.broadcasted_iota(jnp.int32, (n_dev, span), 0)
+    lane = lax.broadcasted_iota(jnp.int32, (n_dev, span), 1)
+    wrap = lambda i: lax.rem(me - i + n_dev, n_dev)
+    k = 2 * wrap(row) + (1 - core if key_shift else core)
+    b = 2 * wrap(lane // BLOCK) + core
+    one = lambda flag: jnp.where(flag, 1.0, 0.0)
+    count = (
+        one(k == 0)
+        + one(k == n_blocks - 1)
+        + one((k == b - 1) & (b != 1))
+        + one(k == b)
+        + one((k == b + 1) & (b != n_blocks - 2))
+    )
+    for r in range(3):
+        count = count + one(ids_ref[h, r : r + 1, :] == k)
+    count = jnp.where((b == 0) | (b == n_blocks - 1), 1.0, count)
+    return jnp.where(count > 0.5, jnp.log(jnp.maximum(count, 1.0)), masked_score)
+
+
+def attend_gather_kernel(
+    n_dev, q_ref, ko_ref, kx_ref, vo_ref, vx_ref, ids_ref, cot, wo, up, down,
+    o_ref, lse_ref, cot_out, wo_out, up_out, down_out,
+    c_send, c_recv, w_send, w_recv, local,
+):
+    me, t, side, core = place()
+    step = pl.program_id(0)
+    last = pl.num_programs(0) - 1
+    half = lax.rem(me, 2)
+    beside = (me + 1 - 2 * half, t)
+    near, across = (me, tp_peer(side, core, 1)), (me, tp_peer(side, core, 2))
+    tall = wo.shape[0]
+    units = down.shape[0]
+    part = units // 4
+
+    def cot_moves():
+        return [
+            remote(
+                cot.at[2 * lax.rem(me + k, n_dev) + side, pl.ds(core * BLOCK, BLOCK), :],
+                cot_out.at[pl.ds(k * BLOCK, BLOCK), :],
+                c_send, c_recv, k - 1, (lax.rem(me + k, n_dev), t),
+            )
+            for k in range(1, n_dev)
+        ]
+
+    def local_moves():
+        pairs = (
+            (cot.at[2 * me + side, pl.ds(core * BLOCK, BLOCK), :], cot_out.at[pl.ds(0, BLOCK), :]),
+            (wo, slot(0, core)),
+            (up, slot(1, core)),
+            (down, slot(2, core)),
+        )
+        return [pltpu.make_async_copy(a, b, local.at[n]) for n, (a, b) in enumerate(pairs)]
+
+    def slot(m, j, start=None):
+        if m == 0:
+            return wo_out.at[pl.ds(j * tall, tall), :]
+        rows = pl.ds(0, units) if start is None else pl.ds(start, part)
+        if m == 1:
+            return up_out.at[rows, pl.ds(j * units, units)]
+        if start is None:
+            return down_out.at[pl.ds(j * units, units), :]
+        return down_out.at[pl.ds(j * units + start, part), :]
+
+    pieces = [(0, None)] + [(m, n) for m in (1, 2) for n in (0, 1)]
+
+    def start_of(n, h):
+        return None if n is None else (2 * h + n) * part
+
+    def own(m, start):
+        ref = (wo, up, down)[m]
+        return ref if start is None else ref.at[pl.ds(start, part), :]
+
+    def over_y(at):
+        m, n = pieces[at]
+        s = start_of(n, half)
+        return remote(own(m, s), slot(m, 2 + core, s), w_send, w_recv, (at, 0), across)
+
+    def over_x(at, h):
+        m, n = pieces[at]
+        held = slot(m, 2 + core, start_of(n, h))
+        return remote(held, held, w_send, w_recv, (at, 1), beside)
+
+    def to_near(at, h, sem):
+        m, n = pieces[at]
+        held = slot(m, 2 + core, start_of(n, h))
+        return remote(held, held, w_send, w_recv, (at, sem), near)
+
+    def own_near(m):
+        return remote((wo, up, down)[m], slot(m, core), w_send, w_recv, (m, 4), near)
+
+    @pl.when(step == 0)
+    def _():
+        greet(
+            [(lax.rem(me + k, n_dev), t) for k in range(1, n_dev)] + [near, across]
+        )
+        for at in range(len(pieces)):
+            over_y(at).start()
+        for move in cot_moves():
+            move.start()
+        for m in range(3):
+            own_near(m).start()
+        for move in local_moves():
+            move.start()
+
+    attend_pair(n_dev, q_ref, ko_ref, kx_ref, vo_ref, vx_ref, ids_ref, o_ref, lse_ref, me, core)
+
+    def pass_on(at):
+        over_y(at).wait_recv()
+        to_near(at, half, 2).start()
+        if at:
+            over_x(at, half).start()
+
+    def pass_side(at):
+        over_x(at, half).wait_recv()
+        to_near(at, 1 - half, 3).start()
+
+    @pl.when(step == last - 2)
+    def _():
+        pass_on(0)
+
+    @pl.when(step == last)
+    def _():
+        n = len(pieces)
+        for at in range(1, n):
+            pass_on(at)
+            if at > 1:
+                pass_side(at - 1)
+        pass_side(n - 1)
+        for move in local_moves():
+            move.wait()
+        for move in cot_moves():
+            move.wait()
+        for m in range(3):
+            own_near(m).wait()
+        for at in range(n):
+            over_y(at).wait_send()
+            to_near(at, half, 2).wait()
+            if at:
+                over_x(at, half).wait_send()
+                to_near(at, 1 - half, 3).wait()
+
+
+def attend_pair(n_dev, q_ref, ko_ref, kx_ref, vo_ref, vx_ref, ids_ref, o_ref, lse_ref, me, core):
+    span = q_ref.shape[0]
+    blocks = span // BLOCK
+    lane = lax.broadcasted_iota(jnp.int32, (1, 2 * HD), 1) // HD
+    vo_t = vo_ref[...].T
+    vx_t = vx_ref[...].T
+    outs = []
+    for h in range(2):
+        qh = (jnp.where(lane == h, q_ref[...], 0.0) * 0.125).astype(jnp.bfloat16)
+
+        def scores(k_ref, far):
+            bias = list_bias(ids_ref, h, far, me, core, n_dev, span)
+            raw = back_dot(k_ref[...], qh).reshape(blocks, BLOCK, span)
+            return (raw + bias[:, None, :]).reshape(span, span)
+
+        so = scores(ko_ref, False)
+        sx = scores(kx_ref, True)
+        top = jnp.maximum(jnp.max(so, 0, keepdims=True), jnp.max(sx, 0, keepdims=True))
+        po = jnp.exp(so - top)
+        px = jnp.exp(sx - top)
+        total = jnp.sum(po, 0, keepdims=True) + jnp.sum(px, 0, keepdims=True)
+        rows = slice(h * HD, (h + 1) * HD)
+        acc = plain_dot(vo_t[rows], po.astype(jnp.bfloat16))
+        acc = acc + plain_dot(vx_t[rows], px.astype(jnp.bfloat16))
+        outs.append(acc / total)
+        lse_ref[0, h : h + 1, :] = top + jnp.log(total)
+    o_ref[...] = jnp.concatenate(outs, 0).T.astype(jnp.bfloat16)
+
+
+def attend_gather(q, ko, kx, vo, vx, ids, cot, wo, up, down, n_dev):
+    span, width = q.shape
+    heads = width // HD
+    units = down.shape[0]
+    tile = pl.BlockSpec((span, 2 * HD), lambda i: (0, i))
+    ids_spec = pl.BlockSpec((2, 3, span), lambda i: (i, 0, 0))
+    lse = pl.BlockSpec((1, 2, span), lambda i: (i, 0, 0))
+    hbm = pl.BlockSpec(memory_space=pl.ANY)
+    dma = pltpu.SemaphoreType.DMA
+    low = lambda *shape: jax.ShapeDtypeStruct(shape, jnp.bfloat16)
+    return pl.pallas_call(
+        partial(attend_gather_kernel, n_dev),
+        grid=(heads // 2,),
+        in_specs=[tile] * 5 + [ids_spec] + [hbm] * 4,
+        out_specs=[tile, lse] + [hbm] * 4,
+        out_shape=[
+            low(span, width),
+            jax.ShapeDtypeStruct((heads // 2, 2, span), jnp.float32),
+            low(span, width),
+            low(4 * wo.shape[0], width),
+            low(width, 4 * units),
+            low(4 * units, width),
+        ],
+        scratch_shapes=[
+            dma((n_dev - 1,)),
+            dma((n_dev - 1,)),
+            dma((5, 5)),
+            dma((5, 5)),
+            dma((4,)),
+        ],
+        compiler_params=pltpu.CompilerParams(
+            collective_id=1, has_side_effects=True, vmem_limit_bytes=48 * 2**20
+        ),
+    )(q, ko, kx, vo, vx, ids, cot, wo, up, down)
+
+
+def attend_back_kernel(
+    n_dev, q_ref, ko_ref, kx_ref, vo_ref, vx_ref, ids_ref, lse_ref, o_ref, g_ref,
+    dq_ref, dko_ref, dkx_ref, dvo_ref, dvx_ref,
+):
+    span = q_ref.shape[0]
+    blocks = span // BLOCK
+    lane = lax.broadcasted_iota(jnp.int32, (1, 2 * HD), 1) // HD
+    weighted = (o_ref[...].astype(jnp.float32) * g_ref[...].astype(jnp.float32)).T
+    me, _, _, core = place()
+    parts = ((ko_ref, vo_ref), (kx_ref, vx_ref))
+    k_ts = [k_ref[...].T for k_ref, _ in parts]
+    dks = [None, None]
+    dvs = [None, None]
+    dq_ts = []
+    for h in range(2):
+        mine = lane == h
+        rows = slice(h * HD, (h + 1) * HD)
+        qh = (jnp.where(mine, q_ref[...], 0.0) * 0.125).astype(jnp.bfloat16)
+        gh = jnp.where(mine, g_ref[...], 0.0).astype(jnp.bfloat16)
+        delta = jnp.sum(weighted[rows], 0, keepdims=True)
+        lse = lse_ref[0, h : h + 1, :]
+        dq_t = None
+        for at, (k_ref, v_ref) in enumerate(parts):
+            bias = list_bias(ids_ref, h, at == 1, me, core, n_dev, span)
+            raw = back_dot(k_ref[...], qh).reshape(blocks, BLOCK, span)
+            raw = (raw + bias[:, None, :]).reshape(span, span)
+            prob = jnp.exp(raw - lse)
+            dprob = back_dot(v_ref[...], gh)
+            dscore = (prob * (dprob - delta)).astype(jnp.bfloat16)
+            dv = plain_dot(prob.astype(jnp.bfloat16), gh)
+            dk = plain_dot(dscore, qh)
+            dvs[at] = dv if dvs[at] is None else dvs[at] + dv
+            dks[at] = dk if dks[at] is None else dks[at] + dk
+            piece = plain_dot(k_ts[at][rows], dscore)
+            dq_t = piece if dq_t is None else dq_t + piece
+        dq_ts.append(dq_t * 0.125)
+    dq_ref[...] = jnp.concatenate(dq_ts, 0).T.astype(dq_ref.dtype)
+    for ref, value in ((dko_ref, dks[0]), (dkx_ref, dks[1]), (dvo_ref, dvs[0]), (dvx_ref, dvs[1])):
+        ref[...] = value.astype(ref.dtype)
+
+
+def pair_specs(span):
+    tile = pl.BlockSpec((span, 2 * HD), lambda i: (0, i))
+    ids = pl.BlockSpec((2, 3, span), lambda i: (i, 0, 0))
+    lse = pl.BlockSpec((1, 2, span), lambda i: (i, 0, 0))
+    return tile, ids, lse
+
+
+def attend_back(q, ko, kx, vo, vx, ids, lse_all, o, g, n_dev):
+    span, width = q.shape
+    heads = width // HD
+    tile, ids_spec, lse = pair_specs(span)
+    low = jax.ShapeDtypeStruct((span, width), jnp.bfloat16)
+    full = jax.ShapeDtypeStruct((span, width), jnp.float32)
+    return pl.pallas_call(
+        partial(attend_back_kernel, n_dev),
+        grid=(heads // 2,),
+        in_specs=[tile] * 5 + [ids_spec] + [lse] + [tile] * 2,
+        out_specs=[tile] * 5,
+        out_shape=[low, full, low, full, low],
+        compiler_params=pltpu.CompilerParams(vmem_limit_bytes=48 * 2**20),
+        cost_estimate=pl.CostEstimate(
+            flops=heads * span * span * 2 * 2 * 5 * HD * 4,
+            bytes_accessed=span * width * 30,
+            transcendentals=heads * span * span * 2,
+        ),
+    )(q, ko, kx, vo, vx, ids, lse_all, o, g)
+
+
+def flip(index, bit):
+    value = lax.rem(lax.div(index, bit), 2)
+    return index + bit - 2 * bit * value, value
+
+
+class Reduction:
+    def __init__(self, sources, spots, bufs, sems):
+        self.sources = sources
+        self.me, self.t, self.side, self.core = spots
+        self.load, self.b0, self.ys, self.b1, self.acc, self.halves, self.got, self.f = bufs
+        self.send, self.recv, self.send0, self.recv0, self.local = sems
+        self.near = (self.me, tp_peer(self.side, self.core, 1))
+        self.across = (self.me, tp_peer(self.side, self.core, 2))
+        self.mates = []
+        self.bits = []
+        for bit in (1, 2, 4):
+            mate, value = flip(self.me, bit)
+            self.mates.append((mate, self.t))
+            self.bits.append(value)
+
+    def rows(self, depth):
+        start, size = 0, self.f.shape[1]
+        other = 0
+        for level in range(depth):
+            size //= 2
+            other = start + (1 - self.bits[level]) * size
+            start = start + self.bits[level] * size
+        return start, other, size
+
+    def parts(self, ch, block):
+        at = 0
+        for ref in self.sources[ch](block):
+            yield ref, pl.ds(at, ref.shape[0])
+            at += ref.shape[0]
+
+    def first(self, ch):
+        at = [(y, *part) for y in range(2) for part in self.parts(ch, 2 * y + 1 - self.core)]
+        return [
+            remote(ref, self.b0.at[ch, y, rows, :], self.send0, self.recv0, (ch, n), self.near)
+            for n, (y, ref, rows) in enumerate(at)
+        ]
+
+    def loads(self, ch):
+        at = [(y, *part) for y in range(2) for part in self.parts(ch, 2 * y + self.core)]
+        return [
+            pltpu.make_async_copy(ref, self.load.at[ch, y, rows, :], self.local.at[ch, n])
+            for n, (y, ref, rows) in enumerate(at)
+        ]
+
+    def over_y(self, ch):
+        return remote(self.ys.at[ch], self.b1.at[ch], self.send, self.recv, (ch, 0), self.across)
+
+    def halving(self, ch, level):
+        size = self.rows(level + 1)[2]
+        return remote(
+            self.halves.at[ch, pl.ds(size, size), :],
+            self.got.at[ch, pl.ds(size, size), :],
+            self.send, self.recv, (ch, 1 + level), self.mates[level],
+        )
+
+    def gather(self, ch, level):
+        start, _, size = self.rows(level + 1)
+        held = self.f.at[ch, pl.ds(pl.multiple_of(start, 16), size), :]
+        return remote(held, held, self.send, self.recv, (ch, 4 + level), self.mates[level])
+
+    def stage(self, ch, s):
+        full = jnp.float32
+        if s == 0:
+            for move in self.first(ch) + self.loads(ch):
+                move.start()
+        elif s == 1:
+            for move in self.loads(ch):
+                move.wait()
+            for move in self.first(ch):
+                move.wait_recv()
+            self.ys[ch] = (self.load[ch, 1].astype(full) + self.b0[ch, 1].astype(full)).astype(jnp.bfloat16)
+            self.over_y(ch).start()
+            self.acc[ch] = self.load[ch, 0].astype(full) + self.b0[ch, 0].astype(full)
+        elif s <= 4:
+            level = s - 2
+            start, _, size = self.rows(level)
+            if s == 2:
+                self.over_y(ch).wait_recv()
+                came = self.b1[ch]
+            else:
+                self.halving(ch, level - 1).wait_recv()
+                came = self.got[ch, pl.ds(size, size), :]
+            here = pl.ds(pl.multiple_of(start, 16), size)
+            self.acc[ch, here, :] = self.acc[ch, here, :] + came.astype(full)
+            _, other, small = self.rows(level + 1)
+            there = pl.ds(pl.multiple_of(other, 16), small)
+            self.halves[ch, pl.ds(small, small), :] = self.acc[ch, there, :].astype(jnp.bfloat16)
+            self.halving(ch, level).start()
+        elif s == 5:
+            start, _, size = self.rows(3)
+            self.halving(ch, 2).wait_recv()
+            here = pl.ds(pl.multiple_of(start, 16), size)
+            total = self.acc[ch, here, :] + self.got[ch, pl.ds(size, size), :].astype(full)
+            self.f[ch, here, :] = total.astype(jnp.bfloat16)
+            self.gather(ch, 2).start()
+        elif s <= 7:
+            self.gather(ch, 8 - s).wait_recv()
+            self.gather(ch, 7 - s).start()
+        else:
+            self.gather(ch, 0).wait_recv()
+
+    def finish(self, ch):
+        for move in self.first(ch):
+            move.wait_send()
+        self.over_y(ch).wait_send()
+        for level in range(3):
+            self.halving(ch, level).wait_send()
+            self.gather(ch, level).wait_send()
+
+
+class Return:
+    def __init__(self, at, n_dev, src, dst, spots, sems):
+        self.at, self.n_dev, self.src, self.dst = at, n_dev, src, dst
+        self.me, self.t, self.side, self.core = spots
+        self.send, self.recv, self.local = sems
+        self.near = (self.me, tp_peer(self.side, self.core, 1))
+        self.across = (self.me, tp_peer(self.side, self.core, 2))
+
+    def block(self, s, side):
+        return self.dst.at[s, side, pl.ds(self.core * BLOCK, BLOCK), :]
+
+    def keep(self):
+        return pltpu.make_async_copy(
+            self.src.at[pl.ds(0, BLOCK), :], self.block(self.me, self.side), self.local.at[self.at]
+        )
+
+    def out(self, k):
+        to = lax.rem(self.me - k + self.n_dev, self.n_dev)
+        return remote(
+            self.src.at[pl.ds(k * BLOCK, BLOCK), :], self.block(self.me, self.side),
+            self.send, self.recv, (self.at, k - 1), (to, self.t),
+        )
+
+    def pass_on(self, n):
+        side = 1 - self.side if n == 2 else self.side
+        held = self.dst.at[:, side, pl.ds(self.core * BLOCK, BLOCK), :]
+        peer = self.across if n == 0 else self.near
+        return remote(held, held, self.send, self.recv, (self.at, self.n_dev - 1 + n), peer)
+
+    def stage(self, s):
+        if s == 0:
+            self.keep().start()
+            for k in range(1, self.n_dev):
+                self.out(k).start()
+        elif s == 1:
+            self.keep().wait()
+            for k in range(1, self.n_dev):
+                self.out(k).wait_recv()
+            self.pass_on(0).start()
+            self.pass_on(1).start()
+        elif s == 2:
+            self.pass_on(0).wait_recv()
+            self.pass_on(2).start()
+        else:
+            for k in range(1, self.n_dev):
+                self.out(k).wait_send()
+            self.pass_on(0).wait_send()
+            self.pass_on(1).wait()
+            self.pass_on(2).wait()
+
+
+class SmallSum:
+    def __init__(self, src, out, came, spots, sems):
+        self.src, self.out, self.came = src, out, came
+        me, t, side, core = spots
+        self.send, self.recv = sems
+        self.peers = [(me, tp_peer(side, core, 1)), (me, tp_peer(side, core, 2))]
+        self.peers += [(flip(me, bit)[0], t) for bit in (1, 2, 4)]
+
+    def move(self, n):
+        held = self.out.at[n]
+        return remote(held, self.came.at[n], self.send, self.recv, n, self.peers[n])
+
+    def stage(self, n):
+        if n == 0:
+            self.out[0] = self.src[...]
+        else:
+            self.move(n - 1).wait_recv()
+            self.out[n] = self.out[n - 1] + self.came[n - 1]
+        if n < len(self.peers):
+            self.move(n).start()
+
+    def finish(self):
+        for n in range(len(self.peers)):
+            self.move(n).wait_send()
+
+
+def all_peers(n_dev, me, t, side, core):
+    return [(lax.rem(me + k, n_dev), t) for k in range(1, n_dev)] + [
+        (me, tp_peer(side, core, bits)) for bits in (1, 2)
+    ]
+
+
+def blocks_of(ref, height, start, size):
+    return lambda block: [ref.at[pl.ds(block * height + start, size), :]]
+
+
+def columns_of(ref, wide, start, size):
+    return lambda block: [ref.at[pl.ds(start, size), pl.ds(block * wide, wide)]]
+
+
+def pair_of(one, two, height):
+    return lambda block: [
+        one.at[pl.ds(block * height, height), :], two.at[pl.ds(block * height, height), :]
+    ]
+
+
+def leave_kernel(
+    n_dev, gd, gu, go, gq, gk, gv, low, ig, small,
+    f, out, iout, total,
+    load, b0, ys, b1, acc, halves, got, came,
+    send, recv, send0, recv0, local, r_send, r_recv, r_local, s_send, s_recv,
+):
+    spots = place()
+    units, hidden = gd.shape[0] // 4, go.shape[0] // 4
+    rows = f.shape[1]
+    sources = [blocks_of(gd, units, i * rows, rows) for i in range(units // rows)]
+    sources += [columns_of(gu, units, i * rows, rows) for i in range(gu.shape[0] // rows)]
+    sources += [pair_of(go, gq, hidden), pair_of(gk, gv, hidden)]
+    red = Reduction(
+        sources, spots, (load, b0, ys, b1, acc, halves, got, f), (send, recv, send0, recv0, local)
+    )
+    backs = [
+        Return(n, n_dev, src, dst, spots, (r_send, r_recv, r_local))
+        for n, (src, dst) in enumerate(((low, out), (ig, iout)))
+    ]
+    tiny = SmallSum(small, total, came, spots, (s_send, s_recv))
+    greet(all_peers(n_dev, *spots))
+    count = len(sources)
+    for ch in range(count):
+        red.stage(ch, 0)
+    tiny.stage(0)
+    for back in backs:
+        back.stage(0)
+    for ch in range(count):
+        red.stage(ch, 1)
+    for tick in range(count + 6):
+        for ch in range(count):
+            if 2 <= tick - ch + 2 <= 8:
+                red.stage(ch, tick - ch + 2)
+        if tick < 5:
+            tiny.stage(tick + 1)
+        if 2 <= tick < 5:
+            for back in backs:
+                back.stage(tick - 1)
+    for ch in range(count):
+        red.finish(ch)
+    tiny.finish()
+
+
+def leave(gd, gu, go, gq, gk, gv, low, ig, small, n_dev):
+    width = low.shape[1]
+    rows = 2 * (go.shape[0] // 4)
+    count = (gd.shape[0] // 4 + gu.shape[0]) // rows + 2
+    vmem = pl.BlockSpec(memory_space=pltpu.VMEM)
+    hbm = pl.BlockSpec(memory_space=pl.ANY)
+    dma = pltpu.SemaphoreType.DMA
+    landed = jax.ShapeDtypeStruct((n_dev, 2, 2 * BLOCK, width), jnp.bfloat16)
+    low_buf = lambda *shape: pltpu.VMEM(shape + (width,), jnp.bfloat16)
+    return pl.pallas_call(
+        partial(leave_kernel, n_dev),
+        in_specs=[hbm] * 8 + [vmem],
+        out_specs=[vmem, hbm, hbm, vmem],
+        out_shape=[
+            jax.ShapeDtypeStruct((count, rows, width), jnp.bfloat16),
+            landed,
+            landed,
+            jax.ShapeDtypeStruct((6,) + small.shape, jnp.float32),
+        ],
+        scratch_shapes=[
+            low_buf(count, 2, rows),
+            low_buf(count, 2, rows),
+            low_buf(count, rows),
+            low_buf(count, rows),
+            pltpu.VMEM((count, rows, width), jnp.float32),
+            low_buf(count, rows),
+            low_buf(count, rows),
+            pltpu.VMEM((5,) + small.shape, jnp.float32),
+            dma((count, 7)),
+            dma((count, 7)),
+            dma((count, 4)),
+            dma((count, 4)),
+            dma((count, 4)),
+            dma((2, n_dev + 2)),
+            dma((2, n_dev + 2)),
+            dma((2,)),
+            dma((5,)),
+            dma((5,)),
+        ],
+        compiler_params=pltpu.CompilerParams(
+            collective_id=2, has_side_effects=True, vmem_limit_bytes=58 * 2**20
+        ),
+    )(gd, gu, go, gq, gk, gv, low, ig, small)
+
+
+def swap(piece, bits):
+    size = lax.axis_size("tp")
+    return lax.ppermute(piece, "tp", [(i, i ^ bits) for i in range(size)])
+
+
+def norm_parts(resid):
+    centre = resid - jnp.mean(resid, -1, keepdims=True)
+    inverse = lax.rsqrt(jnp.mean(centre * centre, -1, keepdims=True) + norm_eps)
+    return centre * inverse, inverse
+
+
+def norm_back(grad, unit, inverse, gain):
+    scaled = grad * gain
+    pull = scaled - jnp.mean(scaled, -1, keepdims=True)
+    pull = pull - unit * jnp.mean(scaled * unit, -1, keepdims=True)
+    return pull * inverse, jnp.sum(grad * unit, 0), jnp.sum(grad, 0)
+
+
+def whole_sequences(
+    tokens,
+    rand_blocks,
+    query_weight,
+    query_bias,
+    key_weight,
+    value_weight,
+    value_bias,
+    output_weight,
+    output_bias,
+    attn_gain,
+    attn_shift,
+    up_weight,
+    up_bias,
+    down_weight,
+    down_bias,
+    ffn_gain,
+    ffn_shift,
+    cotangent,
+):
+    seqs, rows, width = tokens.shape
+    n_dev = lax.axis_size("seq")
+    me = lax.axis_index("seq")
+    t = lax.axis_index("tp")
+    side, core = t // 2, t % 2
+    n_blocks = rows // BLOCK * n_dev
+    hidden = query_weight.shape[1]
+    units = up_weight.shape[1]
+    span = n_dev * BLOCK
+
+    gap = jnp.zeros((256 - hidden,), jnp.float32)
+    pack = jnp.concatenate([query_bias, gap, value_bias, gap, up_bias])[None]
+    x, q, k_own, v_own, k_far, v_far, wt, packs, ids = enter(
+        tokens, rand_blocks, query_weight, key_weight, value_weight, pack, n_dev
+    )
+    wq, wk, wv = (wt[m].reshape(4 * hidden, width) for m in range(3))
+    u_bias = packs[:, 0, 512:].reshape(4 * units)
+    attn_low, lse, cot, wo, w_up, w_down = attend_gather(
+        q, k_own, k_far, v_own, v_far, ids, cotangent, output_weight, up_weight, down_weight, n_dev
+    )
+    branch = plain_dot(attn_low, wo) + output_bias
+    unit_one, inverse_one = norm_parts(x.astype(jnp.float32) + branch)
+    normed = unit_one * attn_gain + attn_shift
+    normed_low = normed.astype(jnp.bfloat16)
+    pre_act = plain_dot(normed_low, w_up) + u_bias
+    cdf = 0.5 * (1.0 + lax.erf(pre_act * HALF_ROOT))
+    act_low = (pre_act * cdf).astype(jnp.bfloat16)
+    slope = (cdf + pre_act * (PDF_SCALE * jnp.exp(-0.5 * pre_act * pre_act))).astype(jnp.bfloat16)
+    ffn = plain_dot(act_low, w_down) + down_bias
+    unit_two, inverse_two = norm_parts(normed + ffn)
+    out_low = (unit_two * ffn_gain + ffn_shift).astype(jnp.bfloat16)
+
+    g_resid2, grad_ffngain, grad_ffnshift = norm_back(
+        cot.astype(jnp.float32), unit_two, inverse_two, ffn_gain
+    )
+    g_ffn = g_resid2.astype(jnp.bfloat16)
+    grad_downbias = jnp.sum(g_ffn.astype(jnp.float32), 0)
+    grad_down = rows_dot(act_low, g_ffn).astype(jnp.bfloat16)
+    g_pre = (back_dot(g_ffn, w_down) * slope.astype(jnp.float32)).astype(jnp.bfloat16)
+    grad_upbias = jnp.sum(g_pre.astype(jnp.float32), 0)
+    grad_up = rows_dot(normed_low, g_pre).astype(jnp.bfloat16)
+    g_normed = g_resid2 + back_dot(g_pre, w_up)
+    g_resid, grad_attngain, grad_attnshift = norm_back(g_normed, unit_one, inverse_one, attn_gain)
+    g_branch = g_resid.astype(jnp.bfloat16)
+    grad_obias = jnp.sum(g_branch.astype(jnp.float32), 0)
+    grad_o = rows_dot(attn_low, g_branch).astype(jnp.bfloat16)
+    g_attn = back_dot(g_branch, wo).astype(jnp.bfloat16)
+
+    dq, dk_own, dk_far, dv_own, dv_far = attend_back(
+        q, k_own, k_far, v_own, v_far, ids, lse, attn_low, g_attn, n_dev
+    )
+    dk = (dk_own + swap(dk_far, 1).astype(jnp.float32)).astype(jnp.bfloat16)
+    dv = (dv_own + swap(dv_far, 1).astype(jnp.float32)).astype(jnp.bfloat16)
+    grad_qbias = jnp.sum(dq.astype(jnp.float32), 0)
+    grad_vbias = jnp.sum(dv.astype(jnp.float32), 0)
+    grad_q = rows_dot(dq, x).astype(jnp.bfloat16)
+    grad_k = rows_dot(dk, x).astype(jnp.bfloat16)
+    grad_v = rows_dot(dv, x).astype(jnp.bfloat16)
+    input_grad = g_resid + plain_dot(dq, wq) + plain_dot(dk, wk) + plain_dot(dv, wv)
+    def absolute(vector):
+        parts = vector.reshape(4, -1)
+        return jnp.take(parts, jnp.arange(4) ^ (2 * side), 0).reshape(-1)
+
+    small = jnp.concatenate(
+        [
+            absolute(grad_qbias),
+            absolute(grad_vbias),
+            absolute(grad_upbias),
+            grad_obias,
+            grad_attngain,
+            grad_attnshift,
+            grad_downbias,
+            grad_ffngain,
+            grad_ffnshift,
+        ]
+    )
+    sums, layer_output, input_out, small_total = leave(
+        grad_down, grad_up, grad_o, grad_q, grad_k, grad_v, out_low,
+        input_grad.astype(jnp.bfloat16), small.reshape(-1, 128), n_dev,
+    )
+    small_total = small_total[5].reshape(-1)
+
+    def share(start, size):
+        whole = small_total[start : start + 4 * size].reshape(4, size)
+        return lax.dynamic_index_in_dim(whole, t, 0, False)
+
+    tail = 8 * hidden + 4 * units
+    rep = [small_total[tail + i * width : tail + (i + 1) * width] for i in range(6)]
+
+    sums = sums.astype(jnp.float32)
+    half = units // sums.shape[1]
+    g_down = sums[:half].reshape(units, width)
+    g_up = sums[half : half + width // sums.shape[1]].reshape(width, units)
+    g_o, g_q = sums[-2, :hidden], sums[-2, hidden:]
+    g_k, g_v = sums[-1, :hidden], sums[-1, hidden:]
+    return (
+        layer_output.reshape(seqs, rows, width),
+        input_out.astype(jnp.float32).reshape(seqs, rows, width),
+        g_q.T,
+        share(0, hidden),
+        g_k.T,
+        g_v.T,
+        share(4 * hidden, hidden),
+        g_o,
+        rep[0],
+        rep[1],
+        rep[2],
+        g_up,
+        share(8 * hidden, units),
+        g_down,
+        rep[3],
+        rep[4],
+        rep[5],
+    )
+
+
+def per_device(tokens, *rest):
+    seqs, rows, _ = tokens.shape
+    n_dev = lax.axis_size("seq")
+    if lax.axis_size("tp") == 4 and n_dev == 8 and seqs == 2 * n_dev and rows == 2 * BLOCK:
+        return whole_sequences(tokens, *rest)
+    return split_sequences(tokens, *rest)
+
+
 def solution(mesh):
     placed = (
         P(None, "seq", None),

time: 2490 us -> 423 us (0.17)
  waiting for transfers between devices: 992 us -> 0.01 us
  blocking collectives: 495 us -> 0 us
  local copies, waits for them, and re-layouts: 426 us -> 40.7 us
  Pallas kernels: 0 us -> 312 us
  other arithmetic: 293 us -> 15.8 us
  matrix products: 230 us -> 48.3 us
    psum x8 -> x0, waiting for transfers between devices: 864 us -> none  [the longest x2 237 us: head_sum_fwd(): return lax.psum(pieces, 'tp')]
    pallas_call x0 -> x4, Pallas kernels: none -> 312 us  [the longest x1 184 us: leave(): pl.pallas_call(partial(leave_kernel, n_dev), in_specs=[hbm] * 8 + [vmem],...]
    all_gather x2 -> x0, blocking collectives: 258 us -> none  [joined(): everything = jax.tree.map(lambda part: lax.all_gather(part, axis), shard)]
    psum x2 -> x0, blocking collectives: 237 us -> none  [the longest x1 201 us: per_device(): end_dout, end_delta = lax.psum((own_dout, own_delta), 'seq')]
    dot_general x12 -> x0, matrix products: 153 us -> none  [the longest x1 47.6 us: per_device(): jnp.einsum('sbhqk,sbhqd->sbhkd', grad_score, q_blocks, preferred_element_...]
    ppermute x4 -> x2, waiting for transfers between devices: 127 us -> 0.01 us  [swap(): return lax.ppermute(piece, 'tp', [(i, i ^ bits) for i in range(size)])]
    scatter-add x1 -> x0, other arithmetic: 90 us -> none  [per_device(): table_grad = jnp.zeros((seqs * per_dev * heads, block, 2 * hsize), jnp.fl...]
    reshape x18 -> x8, local copies, waits for them, and re-layouts: 64.9 us -> 3.13 us  [the longest x2 2.12 us: absolute(): return jnp.take(parts, jnp.arange(4) ^ 2 * side, 0).reshape(-1)]
  transfers between devices with their start and end apart: 15 -> 2, of which waited for: 11 -> 0; matrix products, arithmetic and copies ran while one was open for 15% -> 11% of each run, Pallas kernels for 0% -> 0%
where the time goes in v2:
time: 423 us; the launch traced here: 419 us
  Pallas kernels  312 us (74%)
  matrix products  48.3 us (11%)
  local copies, waits for them, and re-layouts  40.7 us (10%)
  other arithmetic  15.8 us (4%)
    pallas_call x1, Pallas kernels, leave(): pl.pallas_call(partial(leave_kernel, n_dev), in_specs=[hbm] * 8 + [vmem],...  184 us
    pallas_call x1, Pallas kernels, attend_gather(): pl.pallas_call(partial(attend_gather_kernel, n_dev), grid=(heads // 2,),...  76.8 us
    pallas_call x1, Pallas kernels, enter(): pl.pallas_call(partial(enter_kernel, n_dev), in_specs=[hbm, hbm, vmem, vm...  31 us
    dot_general x6, matrix products, rows_dot(): lax.dot_general(left, right, (((0,), (0,)), ((), ())), preferred_element_...  23.6 us
    unnamed x91, local copies, waits for them, and re-layouts  21.9 us
    pallas_call x1, Pallas kernels, attend_back(): pl.pallas_call(partial(attend_back_kernel, n_dev), grid=(heads // 2,), in...  20.7 us
    dot_general x6, matrix products, plain_dot(): return jnp.dot(left, right, preferred_element_type=jnp.float32)  14.4 us
    dot_general x3, matrix products, back_dot(): lax.dot_general(left, right, (((1,), (1,)), ((), ())), preferred_element_...  10.3 us
  transfers between devices with their start and end apart: 2, of which 0 were waited for; matrix products, arithmetic and copies ran while one was open for 11% of the time, Pallas kernels for 0%

profile of v2, /device:TPU:0, one launch (start us, length us, event | category | flops | bytes accessed | tf_op | source)
XLA Modules:
  0.0 419.1 jit_solution(6286385376970670026)
XLA Ops:
  4.6 31.0 %shard_map.305 = (bf16[512,768]{1,0:T(8,128)(2,1)S(1)}, bf16[512,768]{1,0:T(8,128)(2,1)S(1)}, bf16[512,768]{1,0:T(8,128)(2,1)S(1)}, bf16[512,768]{1,0:T(8,128)(2...) custom-call(bf16[16,128,768]{2,1,0:T(8,128)(2,1)} %tok.1, ...), custom_call_target="tpu_custom_call" | custom-call | tf_op jit(solution)/shard_map/pallas_call | solution.py:629
  36.8 76.8 %shard_map.306 = (bf16[512,768]{1,0:T(8,128)(2,1)S(1)}, f32[6,2,512]{2,1,0:T(2,128)S(1)}, bf16[512,768]{1,0:T(8,128)(2,1)S(1)}, bf16[768,768]{1,0:T(8,128)(2,1)}...) custom-call(bf16[512,768]{1,0:T(8,128)(2,1)S(1)} %get-tuple-element.43.q_ref, ...), custom_call_target="tpu_custom_call" | custom-call | tf_op jit(solution)/shard_map/pallas_call | solution.py:842
  113.6 2.5 fusion.25
  117.0 3.4 multiply_convert_fusion.1
  120.4 2.8 fusion.26
  124.0 2.3 fusion.11
  127.4 4.9 %convert_reduce_fusion = (f32[3072]{0:T(1024)S(1)}, bf16[512,3072]{1,0:T(8,128)(2,1)S(1)}) fusion(f32[512,3072]{1,0:T(8,128)S(1)} %get-tuple-element.103, f32[3072]{0:T(1024)S(1)} %bitcast.71, bf16[3072,768]{1,0:T(8,128)(2,1)S(1)} %bitcast.75, f32[512,768]{1,0:T(8,128)S(1)} %get-tuple-element.75), kind=kOutput, calls=%fused_computation.9 | convolution fusion | flops 2439902208 | bytes 15753216 | tf_op jit(solution)/shard_map/dot_general | solution.py:63
  132.3 3.7 multiply_reduce_fusion
  139.0 20.7 %shard_map.307 = (bf16[512,768]{1,0:T(8,128)(2,1)S(1)}, f32[512,768]{1,0:T(8,128)}, bf16[512,768]{1,0:T(8,128)(2,1)S(1)}, f32[512,768]{1,0:T(8,128)}, bf16[512,768]{1,0:T(8,128)(2,1)}) custom-call(bf16[512,768]{1,0:T(8,128)(2,1)S(1)} %get-tuple-element.43.q_ref, bf16[512,768]{1,0:T(8,128)(2,1)S(1)} %get-tuple-element.44.ko_ref, ...), custom_call_target="tpu_custom_call" | custom-call | flops 16106127360 | bytes 11796480 | tf_op jit(solution)/shard_map/pallas_call | solution.py:922
  160.3 3.4 convolution_convert_fusion.5.go
  163.7 6.8 %convolution_convert_fusion.1.gd = bf16[3072,768]{1,0:T(8,128)(2,1)} fusion(bf16[512,3072]{1,0:T(8,128)(2,1)} %copy-done.35, f32[512,768]{1,0:T(8,128)S(1)} %copy-done.15), kind=kOutput, calls=%fused_computation.14 | convolution fusion | flops 2418671616 | bytes 9437184 | tf_op jit(solution)/shard_map/dot_general | solution.py:57
  172.0 3.3 fusion.24
  175.2 1.9 fusion.27
  178.4 1.8 convolution_convert_fusion.4.gq
  180.3 6.9 %convolution_convert_fusion.gu = bf16[768,3072]{1,0:T(8,128)(2,1)} fusion(bf16[512,3072]{1,0:T(8,128)(2,1)} %copy-done.36, f32[512,768]{1,0:T(8,128)S(1)} %copy-done.9, f32[768]{0:T(1024)S(1)} %copy-done.34, f32[768]{0:T(1024)S(1)} %copy-done.24, f32[512]{0:T(512)S(1)} %copy-done.21, f32[512]{0:T(512)S(1)} %copy-done.18), kind=kOutput, calls=%fused_computation.13 | convolution fusion | flops 2420244480 | bytes 9447424 | tf_op jit(solution)/shard_map/dot_general | solution.py:57
  187.2 2.0 convert_reduce_fusion.4
  206.5 1.8 convolution_convert_fusion.2.gv
  208.3 2.1 fusion.18
  212.2 3.0 convolution_convert_fusion.3.gk
  215.2 183.6 %shard_map.308 = (bf16[6,384,768]{2,1,0:T(8,128)(2,1)}, bf16[8,2,128,768]{3,2,1,0:T(8,128)(2,1)}, bf16[8,2,128,768]{3,2,1,0:T(8,128)(2,1)}, f32[6,72,128]{2,1,0:T(8,128)}) custom-call(bf16[3072,768]{1,0:T(8,128)(2,1)} %convolution_convert_fusion.1.gd, bf16[768,3072]{1,0:T(8,128)(2,1)} %convolution_convert_fusion.gu, ...), custom_call_target="tpu_custom_call" | custom-call | tf_op jit(solution)/shard_map/pallas_call | solution.py:1201
  398.8 2.8 convert_element_type.112
  401.8 2.6 fusion.23
  409.3 3.6 bitcast_convert_fusion
  414.8 3.8 copy.53
  (140 shorter events, 40.0 us)
Async XLA Ops:
  0.7 3.6 copy-start.16
  0.7 3.8 copy-start.27
  0.7 3.8 copy-start.28
  0.7 3.8 copy-start.25
  4.6 31.1 %copy-start.3 = (bf16[192,768]{1,0:T(8,128)(2,1)S(1)}, bf16[192,768]{1,0:T(8,128)(2,1)}, u32[]{:S(2)}) copy-start(bf16[192,768]{1,0:T(8,128)(2,1)} %wo.1) | copy-start | bytes 884740
  36.8 76.8 %copy-start.31 = (f32[768]{0:T(1024)S(1)}, f32[768]{0:T(1024)}, u32[]{:S(2)}) copy-start(f32[768]{0:T(1024)} %param.28) | copy-start | bytes 9220
  113.6 3.0 copy-start.29
  116.1 19.9 %copy-start.8 = (f32[512,768]{1,0:T(8,128)}, f32[512,768]{1,0:T(8,128)S(1)}, u32[]{:S(2)}) copy-start(f32[512,768]{1,0:T(8,128)S(1)} %get-tuple-element.101) | copy-start | bytes 4718596
  116.1 19.9 %copy-start.17 = (f32[512]{0:T(512)}, f32[512]{0:T(512)S(1)}, u32[]{:S(2)}) copy-start(f32[512]{0:T(512)S(1)} %broadcast_multiply_fusion.5) | copy-start | bytes 6148
  116.2 4.2 %slice-start = ((s8[4718592]{0:T(1024)(128)(4,1)}), s8[4194304]{0:T(1024)(128)(4,1)S(1)}, s32[]{:S(2)}) async-start(s8[4718592]{0:T(1024)(128)(4,1)} %bitcast.74), calls=%async_computation | async-start | bytes 8388608
  116.5 19.6 %copy-start.20 = (f32[512]{0:T(512)}, f32[512]{0:T(512)S(1)}, u32[]{:S(2)}) copy-start(f32[512]{0:T(512)S(1)} %add_rsqrt_fusion.1) | copy-start | bytes 6148
  117.0 3.4 slice-start.1
  117.0 3.4 copy-start.32
  120.4 2.9 copy-start.35
  127.4 4.9 %copy-start.14 = (f32[512,768]{1,0:T(8,128)}, f32[512,768]{1,0:T(8,128)S(1)}, u32[]{:S(2)}) copy-start(f32[512,768]{1,0:T(8,128)S(1)} %get-tuple-element.75) | copy-start | bytes 4718596
  132.3 3.7 copy-start.36
  139.0 21.3 %copy-start.1 = (bf16[512,768]{1,0:T(8,128)(2,1)S(1)}, bf16[512,768]{1,0:T(8,128)(2,1)}, u32[]{:S(2)}) copy-start(bf16[512,768]{1,0:T(8,128)(2,1)} %copy-done) | copy-start | bytes 2359300
  159.8 27.4 %collective-permute-start.1 = (bf16[512,768]{1,0:T(8,128)(2,1)}, bf16[512,768]{1,0:T(8,128)(2,1)}, u32[]{:S(2)}, u32[]{:S(2)}) collective-permute-start(bf16[512,768]{1,0:T(8,128)(2,1)} %get-tuple-element.60), channel_id=1, source_target_pairs={{0,1},{1,0},{2,3},{3,2},{4,5},{5,4},{6,7},{7,6},{8,9},{9,8},{10,11... | collective-permute-start | bytes 2359304 | tf_op jit(solution)/shard_map/ppermute | solution.py:1239
  159.8 48.5 %collective-permute-start = (bf16[512,768]{1,0:T(8,128)(2,1)S(1)}, bf16[512,768]{1,0:T(8,128)(2,1)}, u32[]{:S(2)}, u32[]{:S(2)}) collective-permute-start(bf16[512,768]{1,0:T(8,128)(2,1)S(1)} %get-tuple-element.58), channel_id=1, source_target_pairs={{0,1},{1,0},{2,3},{3,2},{4,5},{5,4},{6,7},{7,6},{8,9},{9,8},{10,11... | collective-permute-start | bytes 2359304 | tf_op jit(solution)/shard_map/ppermute | solution.py:1239
  160.3 11.6 %copy-start.26 = (pred[4]{0:T(512)(128)(4,1)}, pred[4]{0:T(512)(128)(4,1)S(1)}, u32[]{:S(2)}) copy-start(pred[4]{0:T(512)(128)(4,1)S(1)} %compare_and_fusion) | copy-start | bytes 16
  160.3 3.4 copy-start.15
  180.3 6.9 %copy-start.13 = (f32[512,768]{1,0:T(8,128)S(1)}, f32[512,768]{1,0:T(8,128)}, u32[]{:S(2)}) copy-start(f32[512,768]{1,0:T(8,128)} %get-tuple-element.59) | copy-start | bytes 4718596
  398.8 3.1 copy-start.4
  406.5 2.7 copy-start.11
  (17 other events, 27.1 us)

commit v3 on v0

--- a/solution.py
+++ b/solution.py
@@ -1,7 +1,11 @@
+from functools import partial
+
 import jax
 import jax.numpy as jnp
 from jax import lax
 from jax.sharding import PartitionSpec as P
+from jax.experimental import pallas as pl
+from jax.experimental.pallas import tpu as pltpu
 
 HD = 64
 BLOCK = 64
@@ -126,7 +130,7 @@
     )
 
 
-def per_device(
+def split_sequences(
     tokens,
     rand_blocks,
     query_weight,
@@ -461,6 +465,915 @@
     )
 
 
+HALF_ROOT = 0.7071067811865476
+PDF_SCALE = 0.3989422804014327
+
+
+MESH = pl.DeviceIdType.MESH
+
+
+def place():
+    me, t = lax.axis_index("seq"), lax.axis_index("tp")
+    side, core = lax.div(t, 2), lax.rem(t, 2)
+    return me, t, side, core
+
+
+def tp_peer(side, core, bits):
+    there = 1 - side if bits & 2 else side
+    return there * 2 + (1 - core if bits & 1 else core)
+
+
+def greet(peers):
+    barrier = pltpu.get_barrier_semaphore()
+    for peer in peers:
+        pl.semaphore_signal(barrier, inc=1, device_id=peer, device_id_type=MESH)
+    pl.semaphore_wait(barrier, len(peers))
+
+
+def remote(src, dst, sends, recvs, at, peer):
+    return pltpu.make_async_remote_copy(
+        src_ref=src,
+        dst_ref=dst,
+        send_sem=sends.at[at],
+        recv_sem=recvs.at[at],
+        device_id=peer,
+        device_id_type=MESH,
+    )
+
+
+class Piece:
+    def __init__(self, at, bit, own, held, spots, sems):
+        me, t, side, core = spots
+        self.at, self.own, self.far = at, own, partial(held, 2 + core)
+        mate, self.half = flip(me, bit)
+        self.mate = (mate, t)
+        self.near, self.across = (me, tp_peer(side, core, 1)), (me, tp_peer(side, core, 2))
+        self.sems = sems
+
+    def move(self, n):
+        h = 1 - self.half if n == 3 else self.half
+        src = self.own(h) if n == 0 else self.far(h)
+        peer = (self.across, self.mate, self.near, self.near)[n]
+        return remote(src, self.far(h), *self.sems, (self.at, n), peer)
+
+    def start(self):
+        self.move(0).start()
+
+    def pass_on(self):
+        self.move(0).wait_recv()
+        self.move(1).start()
+        self.move(2).start()
+
+    def pass_side(self):
+        self.move(1).wait_recv()
+        self.move(3).start()
+
+    def arrive(self):
+        self.move(2).wait_recv()
+        self.move(3).wait_recv()
+
+    def sent(self):
+        for n in range(4):
+            self.move(n).wait_send()
+
+
+def enter_kernel(
+    n_dev, tok, cot, rand, wq, wk, wv, qb, vb, ub, wo, up, down,
+    x, q, ko, kf, vo, vf, attn, lse, ids, ubs, wt_out, cot_out, wo_out, up_out, down_out,
+    wt, qbs, vbs, ids_for,
+    tok_send, tok_recv, cot_send, cot_recv, p_send, p_recv, o_send, o_recv, s_send, s_recv, kv_send, kv_recv, local,
+):
+    spots = me, t, side, core = place()
+    near = (me, tp_peer(side, core, 1))
+    hidden, width = wq.shape
+    units = down.shape[0]
+    span = x.shape[0]
+    heads = hidden // HD
+    pairs = width // (2 * HD)
+    part = hidden // 2
+    n_part = units // 2 // part
+
+    holds = [(w, lambda j, m=m: wt.at[m, j]) for m, w in ((1, wk), (2, wv), (0, wq))]
+    holds += [
+        (wo, lambda j: wo_out.at[pl.ds(j * hidden, hidden), :]),
+        (up, lambda j: up_out.at[:, pl.ds(j * units, units)]),
+        (down, lambda j: down_out.at[pl.ds(j * units, units), :]),
+    ]
+    pieces = []
+    for n, (ref, block) in enumerate(holds):
+        for i in range(1 if n < 4 else n_part):
+            count = 1 if n < 4 else n_part
+
+            def rows(r, h, i=i, count=count):
+                return r.at[pl.ds((h * count + i) * part, part), :]
+
+            at = len(pieces)
+            pieces.append(
+                Piece(
+                    at, (1, 2)[at % 2],
+                    lambda h, ref=ref, rows=rows: rows(ref, h),
+                    lambda j, h, block=block, rows=rows: rows(block(j), h),
+                    spots, (p_send, p_recv),
+                )
+            )
+
+    def own_near(n):
+        return remote(holds[n][0], holds[n][1](core), o_send, o_recv, n, near)
+
+    def own_here(n):
+        return pltpu.make_async_copy(holds[n][0], holds[n][1](core), local.at[n])
+
+    def spread(src, dst, sends, recvs):
+        return [
+            remote(
+                src.at[2 * lax.rem(me + k, n_dev) + side, pl.ds(core * BLOCK, BLOCK), :],
+                dst.at[pl.ds(k * BLOCK, BLOCK), :],
+                sends, recvs, k - 1, (lax.rem(me + k, n_dev), t),
+            )
+            for k in range(1, n_dev)
+        ]
+
+    def kept(n):
+        src, dst = ((tok, x), (cot, cot_out))[n]
+        return pltpu.make_async_copy(
+            src.at[2 * me + side, pl.ds(core * BLOCK, BLOCK), :], dst.at[pl.ds(0, BLOCK), :], local.at[6 + n]
+        )
+
+    def shared(bits, which=(0, 1, 2, 3)):
+        slot = (bits & 2) + core
+        to = tp_peer(side, core, bits)
+        moves = (
+            (qb, qbs.at[slot]), (vb, vbs.at[slot]), (ub, ubs.at[slot]),
+            (ids_for.at[to], ids.at[pl.ds(slot * heads, heads)]),
+        )
+        return [
+            remote(*moves[n], s_send, s_recv, (bits - 1, n), (me, to)) for n in which
+        ]
+
+    greet(all_peers(n_dev, *spots) + [(me, tp_peer(side, core, 3))])
+    for move in spread(tok, x, tok_send, tok_recv):
+        move.start()
+    for piece in pieces[:3]:
+        piece.start()
+    kept(0).start()
+    for n in range(3):
+        own_near(n).start()
+        own_here(n).start()
+    qbs[core], vbs[core], ubs[core] = qb[...], vb[...], ub[...]
+    for bits in (1, 2, 3):
+        for move in shared(bits, (0, 1, 2)):
+            move.start()
+    for piece in pieces[3:]:
+        piece.start()
+    for n in range(3, 6):
+        own_near(n).start()
+        own_here(n).start()
+
+    lane = lax.broadcasted_iota(jnp.int32, (1, span), 1)
+    for y in range(2):
+        for c in range(2):
+            block = 2 * lax.rem(me - lane // BLOCK + n_dev, n_dev) + c
+            for h in range(heads):
+                for r in range(3):
+                    line = rand[h, r, pl.ds(2 * me + y, 1), :]
+                    row = jnp.zeros((1, span), jnp.int32)
+                    for b in range(c, 2 * n_dev, 2):
+                        row = jnp.where(block == b, line[:, b : b + 1], row)
+                    ids_for[2 * y + c, h, r : r + 1, :] = row
+    ids[pl.ds(core * heads, heads)] = ids_for[t]
+    for bits in (1, 2, 3):
+        shared(bits, (3,))[0].start()
+
+    for piece in pieces[:3]:
+        piece.pass_on()
+    for piece in pieces[:3]:
+        piece.pass_side()
+    for move in spread(tok, x, tok_send, tok_recv):
+        move.wait_recv()
+    kept(0).wait()
+    for move in spread(cot, cot_out, cot_send, cot_recv):
+        move.start()
+    kept(1).start()
+    for bits in (1, 2, 3):
+        for move in shared(bits):
+            move.wait_recv()
+
+    def bias_of(ref):
+        return jnp.concatenate([ref[j] for j in range(4)], 1)
+
+    def project(n, m):
+        own_near(n).wait_recv()
+        own_here(n).wait()
+        pieces[n].arrive()
+        return back_dot(x[...], wt[m].reshape(width, width))
+
+    def swap_kv(n):
+        src, dst = ((ko, kf), (vo, vf))[n]
+        return remote(src, dst, kv_send, kv_recv, n, near)
+
+    ko[...] = project(0, 1).astype(jnp.bfloat16)
+    swap_kv(0).start()
+    vo[...] = (project(1, 2) + bias_of(vbs)).astype(jnp.bfloat16)
+    swap_kv(1).start()
+    q[...] = (project(2, 0) + bias_of(qbs)).astype(jnp.bfloat16)
+    keep = pltpu.make_async_copy(wt, wt_out, local.at[8])
+    keep.start()
+    for n in (3, 4):
+        pieces[n].pass_on()
+    pieces[3].pass_side()
+    swap_kv(0).wait_recv()
+    swap_kv(1).wait_recv()
+
+    def pair(p, carry):
+        lanes = pl.ds(pl.multiple_of(p * 2 * HD, 2 * HD), 2 * HD)
+        attend_pair(n_dev, p, lanes, q, ko, kf, vo, vf, ids, attn, lse, me, core)
+        for k in range(5):
+
+            @pl.when(p == k)
+            def _():
+                pieces[5 + k].pass_on()
+                pieces[4 + k].pass_side()
+
+        return carry
+
+    lax.fori_loop(0, pairs, pair, 0)
+    for n in range(10, len(pieces)):
+        pieces[n].pass_on()
+        pieces[n - 1].pass_side()
+    pieces[-1].pass_side()
+    for n in range(3, len(pieces)):
+        pieces[n].arrive()
+    for move in spread(cot, cot_out, cot_send, cot_recv):
+        move.wait()
+    kept(1).wait()
+    keep.wait()
+    for move in spread(tok, x, tok_send, tok_recv):
+        move.wait_send()
+    for piece in pieces:
+        piece.sent()
+    for n in range(6):
+        own_near(n).wait_send()
+        if n > 2:
+            own_near(n).wait_recv()
+            own_here(n).wait()
+    for bits in (1, 2, 3):
+        for move in shared(bits):
+            move.wait_send()
+    for n in range(2):
+        swap_kv(n).wait_send()
+
+
+def enter(tok, cot, rand, wq, wk, wv, qb, vb, ub, wo, up, down, n_dev):
+    hidden, width = wq.shape
+    units = down.shape[0]
+    span = n_dev * BLOCK
+    heads = hidden // HD
+    pieces = 4 + 2 * (units // hidden)
+    vmem = pl.BlockSpec(memory_space=pltpu.VMEM)
+    hbm = pl.BlockSpec(memory_space=pl.ANY)
+    shape = lambda dtype, *dims: jax.ShapeDtypeStruct(dims, dtype)
+    low = partial(shape, jnp.bfloat16)
+    dma = pltpu.SemaphoreType.DMA
+    return pl.pallas_call(
+        partial(enter_kernel, n_dev),
+        in_specs=[hbm, hbm, vmem] + [hbm] * 3 + [vmem] * 3 + [hbm] * 3,
+        out_specs=[vmem] * 10 + [hbm] * 5,
+        out_shape=[low(span, width)] * 7
+        + [
+            shape(jnp.float32, 2 * heads, 2, span),
+            shape(jnp.int32, 4 * heads, 3, span),
+            shape(jnp.float32, 4, 1, units),
+            low(3, 4, hidden, width),
+            low(span, width),
+            low(width, width),
+            low(width, 4 * units),
+            low(4 * units, width),
+        ],
+        scratch_shapes=[
+            pltpu.VMEM((3, 4, hidden, width), jnp.bfloat16),
+            pltpu.VMEM((4, 1, hidden), jnp.float32),
+            pltpu.VMEM((4, 1, hidden), jnp.float32),
+            pltpu.VMEM((4, heads, 3, span), jnp.int32),
+            dma((n_dev - 1,)),
+            dma((n_dev - 1,)),
+            dma((n_dev - 1,)),
+            dma((n_dev - 1,)),
+            dma((pieces, 4)),
+            dma((pieces, 4)),
+            dma((6,)),
+            dma((6,)),
+            dma((3, 4)),
+            dma((3, 4)),
+            dma((2,)),
+            dma((2,)),
+            dma((9,)),
+        ],
+        compiler_params=pltpu.CompilerParams(
+            collective_id=0, has_side_effects=True, vmem_limit_bytes=56 * 2**20
+        ),
+    )(tok, cot, rand, wq, wk, wv, qb, vb, ub, wo, up, down)
+
+
+def list_bias(ids_ref, h, key_shift, me, core, n_dev, span):
+    n_blocks = 2 * n_dev
+    row = lax.broadcasted_iota(jnp.int32, (n_dev, span), 0)
+    lane = lax.broadcasted_iota(jnp.int32, (n_dev, span), 1)
+    wrap = lambda i: lax.rem(me - i + n_dev, n_dev)
+    k = 2 * wrap(row) + (1 - core if key_shift else core)
+    b = 2 * wrap(lane // BLOCK) + core
+    one = lambda flag: jnp.where(flag, 1.0, 0.0)
+    count = (
+        one(k == 0)
+        + one(k == n_blocks - 1)
+        + one((k == b - 1) & (b != 1))
+        + one(k == b)
+        + one((k == b + 1) & (b != n_blocks - 2))
+    )
+    for r in range(3):
+        count = count + one(ids_ref[h, r : r + 1, :] == k)
+    count = jnp.where((b == 0) | (b == n_blocks - 1), 1.0, count)
+    return jnp.where(count > 0.5, jnp.log(jnp.maximum(count, 1.0)), masked_score)
+
+
+def attend_pair(n_dev, p, lanes, q_ref, ko, kf, vo, vf, ids, attn, lse, me, core):
+    span = q_ref.shape[0]
+    blocks = span // BLOCK
+    lane = lax.broadcasted_iota(jnp.int32, (1, 2 * HD), 1) // HD
+    q = q_ref[:, lanes]
+    keys = (ko[:, lanes], kf[:, lanes])
+    values = (vo[:, lanes].T, vf[:, lanes].T)
+    outs = []
+    for h in range(2):
+        qh = (jnp.where(lane == h, q, 0.0) * 0.125).astype(jnp.bfloat16)
+        scores = []
+        for far in range(2):
+            bias = list_bias(ids, 2 * p + h, far == 1, me, core, n_dev, span)
+            raw = back_dot(keys[far], qh).reshape(blocks, BLOCK, span)
+            scores.append((raw + bias[:, None, :]).reshape(span, span))
+        top = jnp.maximum(*(jnp.max(s, 0, keepdims=True) for s in scores))
+        expo = [jnp.exp(s - top) for s in scores]
+        total = sum(jnp.sum(e, 0, keepdims=True) for e in expo)
+        rows = slice(h * HD, (h + 1) * HD)
+        acc = sum(plain_dot(v[rows], e.astype(jnp.bfloat16)) for v, e in zip(values, expo))
+        outs.append(acc / total)
+        lse[p, h : h + 1, :] = top + jnp.log(total)
+    attn[:, lanes] = jnp.concatenate(outs, 0).T.astype(jnp.bfloat16)
+
+
+def flip(index, bit):
+    value = lax.rem(lax.div(index, bit), 2)
+    return index + bit - 2 * bit * value, value
+
+
+class Reduction:
+    def __init__(self, parts, mine, spots, bufs, sems):
+        self.parts, self.mine = parts, mine
+        self.me, self.t, self.side, self.core = spots
+        self.b0, self.b1, self.acc, self.halves, self.got, self.f = bufs
+        self.send, self.recv, self.send0, self.recv0 = sems
+        self.near = (self.me, tp_peer(self.side, self.core, 1))
+        self.across = (self.me, tp_peer(self.side, self.core, 2))
+        self.mates = []
+        self.bits = []
+        for bit in (1, 2, 4):
+            mate, value = flip(self.me, bit)
+            self.mates.append((mate, self.t))
+            self.bits.append(value)
+
+    def span(self, ref, start, size):
+        return ref.at[pl.ds(pl.multiple_of(start, 16), size), :]
+
+    def rows(self, depth):
+        start, size, inner = 0, self.f.shape[1], 0
+        for level in range(depth):
+            size //= 2
+            start = start + self.bits[level] * size
+            inner = inner + (self.bits[level] * size if level else 0)
+        return start, inner, size
+
+    def first(self, ch):
+        moves = []
+        for y in range(2):
+            at = 0
+            for ref in self.parts(ch, 2 * y + 1 - self.core):
+                rows = pl.ds(at, ref.shape[0])
+                at += ref.shape[0]
+                n = len(moves)
+                moves.append(
+                    remote(ref, self.b0.at[ch, y, rows, :], self.send0, self.recv0, (ch, n), self.near)
+                )
+        return moves
+
+    def over_y(self, ch):
+        return remote(self.mine(ch, 1), self.b1.at[ch], self.send, self.recv, (ch, 0), self.across)
+
+    def halving(self, ch, level):
+        size = self.rows(level + 1)[2]
+        return remote(
+            self.halves.at[ch, pl.ds(size, size), :],
+            self.got.at[ch, pl.ds(size, size), :],
+            self.send, self.recv, (ch, 1 + level), self.mates[level],
+        )
+
+    def gather(self, ch, level):
+        start, _, size = self.rows(level + 1)
+        held = self.span(self.f.at[ch], start, size)
+        return remote(held, held, self.send, self.recv, (ch, 4 + level), self.mates[level])
+
+    def stage(self, ch, s):
+        full = jnp.float32
+        if s == 0:
+            for move in self.first(ch):
+                move.start()
+        elif s == 1:
+            for move in self.first(ch):
+                move.wait_recv()
+            out = self.mine(ch, 1)
+            out[...] = (out[...].astype(full) + self.b0[ch, 1].astype(full)).astype(jnp.bfloat16)
+            self.over_y(ch).start()
+        elif s == 2:
+            self.over_y(ch).wait_recv()
+            size = self.rows(1)[2]
+
+            def total(start):
+                terms = (self.mine(ch, 0), self.b0.at[ch, 0], self.b1.at[ch])
+                one, two, three = (self.span(ref, start, size)[...].astype(full) for ref in terms)
+                return one + two + three
+
+            self.halves[ch, pl.ds(size, size), :] = total((1 - self.bits[0]) * size).astype(jnp.bfloat16)
+            self.halving(ch, 0).start()
+            self.acc[ch] = total(self.bits[0] * size)
+        elif s <= 5:
+            level = s - 3
+            _, inner, size = self.rows(level + 1)
+            self.halving(ch, level).wait_recv()
+            total = self.span(self.acc.at[ch], inner, size)[...] + self.got[ch, pl.ds(size, size), :].astype(full)
+            if s == 5:
+                self.span(self.f.at[ch], self.rows(3)[0], size)[...] = total.astype(jnp.bfloat16)
+                self.gather(ch, 2).start()
+            else:
+                self.span(self.acc.at[ch], inner, size)[...] = total
+                small = size // 2
+                other = self.span(self.acc.at[ch], inner + (1 - self.bits[level + 1]) * small, small)
+                self.halves[ch, pl.ds(small, small), :] = other[...].astype(jnp.bfloat16)
+                self.halving(ch, level + 1).start()
+        elif s <= 7:
+            self.gather(ch, 8 - s).wait_recv()
+            self.gather(ch, 7 - s).start()
+        else:
+            self.gather(ch, 0).wait_recv()
+
+    def finish(self, ch):
+        for move in self.first(ch):
+            move.wait_send()
+        self.over_y(ch).wait_send()
+        for level in range(3):
+            self.halving(ch, level).wait_send()
+            self.gather(ch, level).wait_send()
+
+
+class Return:
+    def __init__(self, at, n_dev, src, dst, spots, sems):
+        self.at, self.n_dev, self.src, self.dst = at, n_dev, src, dst
+        self.me, self.t, self.side, self.core = spots
+        self.send, self.recv, self.local = sems
+        self.near = (self.me, tp_peer(self.side, self.core, 1))
+        self.across = (self.me, tp_peer(self.side, self.core, 2))
+
+    def block(self, s, side):
+        return self.dst.at[s, side, pl.ds(self.core * BLOCK, BLOCK), :]
+
+    def keep(self):
+        return pltpu.make_async_copy(
+            self.src.at[pl.ds(0, BLOCK), :], self.block(self.me, self.side), self.local.at[self.at]
+        )
+
+    def out(self, k):
+        to = lax.rem(self.me - k + self.n_dev, self.n_dev)
+        return remote(
+            self.src.at[pl.ds(k * BLOCK, BLOCK), :], self.block(self.me, self.side),
+            self.send, self.recv, (self.at, k - 1), (to, self.t),
+        )
+
+    def pass_on(self, n):
+        side = 1 - self.side if n == 2 else self.side
+        held = self.dst.at[:, side, pl.ds(self.core * BLOCK, BLOCK), :]
+        peer = self.across if n == 0 else self.near
+        return remote(held, held, self.send, self.recv, (self.at, self.n_dev - 1 + n), peer)
+
+    def stage(self, s):
+        if s == 0:
+            self.keep().start()
+            for k in range(1, self.n_dev):
+                self.out(k).start()
+        elif s == 1:
+            self.keep().wait()
+            for k in range(1, self.n_dev):
+                self.out(k).wait_recv()
+            self.pass_on(0).start()
+            self.pass_on(1).start()
+        elif s == 2:
+            self.pass_on(0).wait_recv()
+            self.pass_on(2).start()
+        else:
+            for k in range(1, self.n_dev):
+                self.out(k).wait_send()
+            self.pass_on(0).wait_send()
+            self.pass_on(1).wait()
+            self.pass_on(2).wait()
+
+
+class SmallSum:
+    def __init__(self, out, came, spots, sems):
+        self.out, self.came = out, came
+        me, t, side, core = spots
+        self.send, self.recv = sems
+        self.peers = [(me, tp_peer(side, core, 1)), (me, tp_peer(side, core, 2))]
+        self.peers += [(flip(me, bit)[0], t) for bit in (1, 2, 4)]
+
+    def move(self, n):
+        held = self.out.at[n]
+        return remote(held, self.came.at[n], self.send, self.recv, n, self.peers[n])
+
+    def stage(self, n):
+        if n:
+            self.move(n - 1).wait_recv()
+            self.out[n] = self.out[n - 1] + self.came[n - 1]
+        if n < len(self.peers):
+            self.move(n).start()
+
+    def finish(self):
+        for n in range(len(self.peers)):
+            self.move(n).wait_send()
+
+
+def all_peers(n_dev, me, t, side, core):
+    return [(lax.rem(me + k, n_dev), t) for k in range(1, n_dev)] + [
+        (me, tp_peer(side, core, bits)) for bits in (1, 2)
+    ]
+
+
+def tail_kernel(
+    n_dev, q, ko, kf, vo, vf, ids, lse, attn, gat, x, gres, early, gd, gu, go, low, wt_hbm,
+    f, out, iout, total,
+    load, p2, wt, b0, b1, acc, halves, got, came, dq, own, far, far_in, ig,
+    send, recv, send0, recv0, local, x_send, x_recv, r_send, r_recv, r_local, s_send, s_recv,
+):
+    spots = me, t, side, core = place()
+    units, hidden = gd.shape[0] // 4, go.shape[0] // 4
+    span, width = q.shape
+    rows = f.shape[1]
+    n_down = units // rows
+    n_ffn = n_down + gu.shape[0] // rows
+    count = f.shape[0]
+    pairs = width // (2 * HD)
+    near = (me, tp_peer(side, core, 1))
+
+    def parts(ch, block):
+        if ch < n_down:
+            return [gd.at[pl.ds(block * units + ch * rows, rows), :]]
+        if ch < n_ffn:
+            return [gu.at[pl.ds((ch - n_down) * rows, rows), pl.ds(block * units, units)]]
+        return [p2.at[ch - n_ffn, block]]
+
+    def mine(ch, y):
+        return load.at[ch, y] if ch < n_ffn else p2.at[ch - n_ffn, 2 * y + core]
+
+    red = Reduction(parts, mine, spots, (b0, b1, acc, halves, got, f), (send, recv, send0, recv0))
+    back = [
+        Return(n, n_dev, src, dst, spots, (r_send, r_recv, r_local))
+        for n, (src, dst) in enumerate(((low, out), (ig, iout)))
+    ]
+    tiny = SmallSum(total, came, spots, (s_send, s_recv))
+
+    def loads(ch):
+        return [
+            pltpu.make_async_copy(parts(ch, 2 * y + core)[0], mine(ch, y), local.at[2 * ch + y])
+            for y in range(2)
+        ]
+
+    def others():
+        pieces = [(wt_hbm, wt)] + [
+            (go.at[pl.ds(j * hidden, hidden), :], p2.at[0, j, pl.ds(0, hidden), :]) for j in range(4)
+        ]
+        return [
+            pltpu.make_async_copy(a, b, local.at[2 * n_ffn + n]) for n, (a, b) in enumerate(pieces)
+        ]
+
+    def swap_far(p, n):
+        return remote(far.at[n, p], far_in.at[n, p], x_send, x_recv, (p, n), near)
+
+    greet(all_peers(n_dev, *spots))
+    for ch in range(n_ffn):
+        red.stage(ch, 0)
+        for move in loads(ch):
+            move.start()
+    back[0].stage(0)
+    for move in others():
+        move.start()
+
+    def pair(p, carry):
+        lanes = pl.ds(pl.multiple_of(p * 2 * HD, 2 * HD), 2 * HD)
+        attend_pair_back(n_dev, p, lanes, q, ko, kf, vo, vf, ids, lse, attn, gat, dq, own, far, me, core)
+        for n in range(2):
+            swap_far(p, n).start()
+        for k in range(2):
+
+            @pl.when(p == k)
+            def _():
+                for ch in range(k * n_ffn // 2, (k + 1) * n_ffn // 2):
+                    for move in loads(ch):
+                        move.wait()
+                    red.stage(ch, 1)
+
+        return carry
+
+    lax.fori_loop(0, pairs, pair, 0)
+
+    for p in range(pairs):
+        for n in range(2):
+            swap_far(p, n).wait_recv()
+
+    def joined_low(n):
+        cat = jnp.concatenate([far_in[n, p] for p in range(pairs)], 1)
+        return (own[n] + cat.astype(jnp.float32)).astype(jnp.bfloat16)
+
+    def weight_grad(low_grad, ch, at):
+        grad = plain_dot(low_grad.T, x[...]).astype(jnp.bfloat16)
+        for j in range(4):
+            p2[ch, j, pl.ds(at, hidden), :] = grad[j * hidden : (j + 1) * hidden]
+
+    def column_sum(low_grad):
+        sums = jnp.sum(low_grad.astype(jnp.float32), 0, keepdims=True)
+        turned = jnp.concatenate([sums[:, width // 2 :], sums[:, : width // 2]], 1)
+        return jnp.where(side == 0, sums, turned)
+
+    red.stage(0, 2)
+    weight_grad(dq[...], 0, hidden)
+    for move in others():
+        move.wait()
+    red.stage(n_ffn, 0)
+    dk = joined_low(0)
+    weight_grad(dk, 1, 0)
+    dv = joined_low(1)
+    weight_grad(dv, 1, hidden)
+    red.stage(n_ffn + 1, 0)
+    total[0] = early[...]
+    total[0, 0:1, :] = column_sum(dq[...])
+    total[0, 1:2, :] = column_sum(dv)
+    tiny.stage(0)
+    red.stage(n_ffn, 1)
+    matrix = lambda m: wt[m].reshape(width, width)
+    into = gres[...] + plain_dot(dq[...], matrix(0))
+    into = into + plain_dot(dk, matrix(1))
+    ig[...] = (into + plain_dot(dv, matrix(2))).astype(jnp.bfloat16)
+    red.stage(n_ffn + 1, 1)
+    back[1].stage(0)
+    back[0].stage(1)
+
+    events = []
+    for ch in range(count):
+        for s in range(2, 9):
+            if (ch, s) != (0, 2):
+                events.append((17 + 12.6 * ch + (0, 0, 0, 8, 13, 18, 23, 28, 35)[s], red, (ch, s)))
+    for n in range(1, 6):
+        events.append(((36, 84, 88, 92, 98)[n - 1], tiny, (n,)))
+    events += [(55, back[1], (1,)), (96, back[0], (2,)), (114, back[1], (2,))]
+    for _, who, what in sorted(events, key=lambda e: e[0]):
+        who.stage(*what)
+    for b in back:
+        b.stage(3)
+    for ch in range(count):
+        red.finish(ch)
+    tiny.finish()
+    for p in range(pairs):
+        for n in range(2):
+            swap_far(p, n).wait_send()
+
+
+def attend_pair_back(n_dev, p, lanes, q_ref, ko, kf, vo, vf, ids, lse_ref, attn, gat, dq, own, far, me, core):
+    span = q_ref.shape[0]
+    blocks = span // BLOCK
+    lane = lax.broadcasted_iota(jnp.int32, (1, 2 * HD), 1) // HD
+    q, g = q_ref[:, lanes], gat[:, lanes]
+    weighted = (attn[:, lanes].astype(jnp.float32) * g.astype(jnp.float32)).T
+    parts = ((ko[:, lanes], vo[:, lanes]), (kf[:, lanes], vf[:, lanes]))
+    k_ts = [k.T for k, _ in parts]
+    dks = [None, None]
+    dvs = [None, None]
+    dq_ts = []
+    for h in range(2):
+        rows = slice(h * HD, (h + 1) * HD)
+        qh = (jnp.where(lane == h, q, 0.0) * 0.125).astype(jnp.bfloat16)
+        gh = jnp.where(lane == h, g, 0.0).astype(jnp.bfloat16)
+        delta = jnp.sum(weighted[rows], 0, keepdims=True)
+        lse = lse_ref[p, h : h + 1, :]
+        dq_t = None
+        for at, (k, v) in enumerate(parts):
+            bias = list_bias(ids, 2 * p + h, at == 1, me, core, n_dev, span)
+            raw = back_dot(k, qh).reshape(blocks, BLOCK, span)
+            raw = (raw + bias[:, None, :]).reshape(span, span)
+            prob = jnp.exp(raw - lse)
+            dprob = back_dot(v, gh)
+            dscore = (prob * (dprob - delta)).astype(jnp.bfloat16)
+            dv = plain_dot(prob.astype(jnp.bfloat16), gh)
+            dk = plain_dot(dscore, qh)
+            dvs[at] = dv if dvs[at] is None else dvs[at] + dv
+            dks[at] = dk if dks[at] is None else dks[at] + dk
+            piece = plain_dot(k_ts[at][rows], dscore)
+            dq_t = piece if dq_t is None else dq_t + piece
+        dq_ts.append(dq_t * 0.125)
+    dq[:, lanes] = jnp.concatenate(dq_ts, 0).T.astype(jnp.bfloat16)
+    for n, grads in enumerate((dks, dvs)):
+        own[n, :, lanes] = grads[0]
+        far[n, p] = grads[1].astype(jnp.bfloat16)
+
+
+def tail(q, ko, kf, vo, vf, ids, lse, attn, gat, x, gres, early, gd, gu, go, low, wt, n_dev):
+    span, width = q.shape
+    hidden = go.shape[0] // 4
+    rows = 2 * hidden
+    n_ffn = (gd.shape[0] // 4 + gu.shape[0]) // rows
+    count = n_ffn + 2
+    pairs = width // (2 * HD)
+    vmem = pl.BlockSpec(memory_space=pltpu.VMEM)
+    hbm = pl.BlockSpec(memory_space=pl.ANY)
+    dma = pltpu.SemaphoreType.DMA
+    landed = jax.ShapeDtypeStruct((n_dev, 2, 2 * BLOCK, width), jnp.bfloat16)
+    low_buf = lambda *shape: pltpu.VMEM(shape + (width,), jnp.bfloat16)
+    pair_buf = pltpu.VMEM((2, pairs, span, 2 * HD), jnp.bfloat16)
+    return pl.pallas_call(
+        partial(tail_kernel, n_dev),
+        in_specs=[vmem] * 12 + [hbm] * 5,
+        out_specs=[vmem, hbm, hbm, vmem],
+        out_shape=[
+            jax.ShapeDtypeStruct((count, rows, width), jnp.bfloat16),
+            landed,
+            landed,
+            jax.ShapeDtypeStruct((6,) + early.shape, jnp.float32),
+        ],
+        scratch_shapes=[
+            low_buf(n_ffn, 2, rows),
+            low_buf(2, 4, rows),
+            pltpu.VMEM(wt.shape, jnp.bfloat16),
+            low_buf(count, 2, rows),
+            low_buf(count, rows),
+            pltpu.VMEM((count, rows // 2, width), jnp.float32),
+            low_buf(count, rows),
+            low_buf(count, rows),
+            pltpu.VMEM((5,) + early.shape, jnp.float32),
+            low_buf(span),
+            pltpu.VMEM((2, span, width), jnp.float32),
+            pair_buf,
+            pair_buf,
+            low_buf(span),
+            dma((count, 7)),
+            dma((count, 7)),
+            dma((count, 2)),
+            dma((count, 2)),
+            dma((2 * n_ffn + 5,)),
+            dma((pairs, 2)),
+            dma((pairs, 2)),
+            dma((2, n_dev + 2)),
+            dma((2, n_dev + 2)),
+            dma((2,)),
+            dma((5,)),
+            dma((5,)),
+        ],
+        compiler_params=pltpu.CompilerParams(
+            collective_id=2, has_side_effects=True, vmem_limit_bytes=60 * 2**20
+        ),
+    )(q, ko, kf, vo, vf, ids, lse, attn, gat, x, gres, early, gd, gu, go, low, wt)
+
+
+def norm_parts(resid):
+    centre = resid - jnp.mean(resid, -1, keepdims=True)
+    inverse = lax.rsqrt(jnp.mean(centre * centre, -1, keepdims=True) + norm_eps)
+    return centre * inverse, inverse
+
+
+def norm_back(grad, unit, inverse, gain):
+    scaled = grad * gain
+    pull = scaled - jnp.mean(scaled, -1, keepdims=True)
+    pull = pull - unit * jnp.mean(scaled * unit, -1, keepdims=True)
+    return pull * inverse, jnp.sum(grad * unit, 0), jnp.sum(grad, 0)
+
+
+def whole_sequences(
+    tokens,
+    rand_blocks,
+    query_weight,
+    query_bias,
+    key_weight,
+    value_weight,
+    value_bias,
+    output_weight,
+    output_bias,
+    attn_gain,
+    attn_shift,
+    up_weight,
+    up_bias,
+    down_weight,
+    down_bias,
+    ffn_gain,
+    ffn_shift,
+    cotangent,
+):
+    seqs, rows, width = tokens.shape
+    n_dev = lax.axis_size("seq")
+    me = lax.axis_index("seq")
+    t = lax.axis_index("tp")
+    side, core = t // 2, t % 2
+    n_blocks = rows // BLOCK * n_dev
+    hidden = query_weight.shape[1]
+    units = up_weight.shape[1]
+    span = n_dev * BLOCK
+
+    (
+        x, q, k_own, k_far, v_own, v_far, attn_low, lse, ids, u_bias, wt, cot, wo, w_up, w_down,
+    ) = enter(
+        tokens, cotangent, rand_blocks.transpose(2, 3, 0, 1), query_weight.T, key_weight.T, value_weight.T,
+        query_bias[None], value_bias[None], up_bias[None], output_weight, up_weight, down_weight, n_dev,
+    )
+    u_bias = u_bias.reshape(4 * units)
+    branch = plain_dot(attn_low, wo) + output_bias
+    unit_one, inverse_one = norm_parts(x.astype(jnp.float32) + branch)
+    normed = unit_one * attn_gain + attn_shift
+    normed_low = normed.astype(jnp.bfloat16)
+    pre_act = plain_dot(normed_low, w_up) + u_bias
+    cdf = 0.5 * (1.0 + lax.erf(pre_act * HALF_ROOT))
+    act_low = (pre_act * cdf).astype(jnp.bfloat16)
+    slope = (cdf + pre_act * (PDF_SCALE * jnp.exp(-0.5 * pre_act * pre_act))).astype(jnp.bfloat16)
+    ffn = plain_dot(act_low, w_down) + down_bias
+    unit_two, inverse_two = norm_parts(normed + ffn)
+    out_low = (unit_two * ffn_gain + ffn_shift).astype(jnp.bfloat16)
+
+    g_resid2, grad_ffngain, grad_ffnshift = norm_back(
+        cot.astype(jnp.float32), unit_two, inverse_two, ffn_gain
+    )
+    g_ffn = g_resid2.astype(jnp.bfloat16)
+    grad_downbias = jnp.sum(g_ffn.astype(jnp.float32), 0)
+    grad_down = rows_dot(act_low, g_ffn).astype(jnp.bfloat16)
+    g_pre = (back_dot(g_ffn, w_down) * slope.astype(jnp.float32)).astype(jnp.bfloat16)
+    grad_upbias = jnp.sum(g_pre.astype(jnp.float32), 0)
+    grad_up = rows_dot(normed_low, g_pre).astype(jnp.bfloat16)
+    g_normed = g_resid2 + back_dot(g_pre, w_up)
+    g_resid, grad_attngain, grad_attnshift = norm_back(g_normed, unit_one, inverse_one, attn_gain)
+    g_branch = g_resid.astype(jnp.bfloat16)
+    grad_obias = jnp.sum(g_branch.astype(jnp.float32), 0)
+    grad_o = rows_dot(attn_low, g_branch).astype(jnp.bfloat16)
+    g_attn = back_dot(g_branch, wo).astype(jnp.bfloat16)
+
+    ups = grad_upbias.reshape(2, 2, units)
+    ups = jnp.where(side == 0, ups, ups[::-1]).reshape(4, width)
+    late = jnp.zeros((2, width), jnp.float32)
+    lines = [grad_obias, grad_attngain, grad_attnshift, grad_downbias, grad_ffngain, grad_ffnshift]
+    early = jnp.concatenate([late, ups, jnp.stack(lines), late, late], 0)
+    sums, layer_output, input_out, small = tail(
+        q, k_own, k_far, v_own, v_far, ids, lse, attn_low, g_attn, x, g_resid, early,
+        grad_down, grad_up, grad_o, out_low, wt, n_dev,
+    )
+    small = small[5]
+
+    def share(first, size):
+        whole = small[first : first + 4 * size // width].reshape(4, size)
+        return lax.dynamic_index_in_dim(whole, t, 0, False)
+
+    sums = sums.astype(jnp.float32)
+    half = units // sums.shape[1]
+    g_down = sums[:half].reshape(units, width)
+    g_up = sums[half : half + width // sums.shape[1]].reshape(width, units)
+    g_o, g_q = sums[-2, :hidden], sums[-2, hidden:]
+    g_k, g_v = sums[-1, :hidden], sums[-1, hidden:]
+    return (
+        layer_output.reshape(seqs, rows, width),
+        input_out.astype(jnp.float32).reshape(seqs, rows, width),
+        g_q.T,
+        share(0, hidden),
+        g_k.T,
+        g_v.T,
+        share(1, hidden),
+        g_o,
+        small[6],
+        small[7],
+        small[8],
+        g_up,
+        share(2, units),
+        g_down,
+        small[9],
+        small[10],
+        small[11],
+    )
+
+
+def per_device(tokens, *rest):
+    seqs, rows, _ = tokens.shape
+    n_dev = lax.axis_size("seq")
+    if lax.axis_size("tp") == 4 and n_dev == 8 and seqs == 2 * n_dev and rows == 2 * BLOCK:
+        return whole_sequences(tokens, *rest)
+    return split_sequences(tokens, *rest)
+
+
 def solution(mesh):
     placed = (
         P(None, "seq", None),

time: 2490 us -> 297 us (0.12)
  waiting for transfers between devices: 992 us -> 0 us
  blocking collectives: 495 us -> 0 us
  local copies, waits for them, and re-layouts: 426 us -> 15.8 us
  other arithmetic: 293 us -> 9.78 us
  Pallas kernels: 0 us -> 241 us
  matrix products: 230 us -> 29.7 us
    psum x8 -> x0, waiting for transfers between devices: 864 us -> none  [the longest x2 237 us: head_sum_fwd(): return lax.psum(pieces, 'tp')]
    all_gather x2 -> x0, blocking collectives: 258 us -> none  [joined(): everything = jax.tree.map(lambda part: lax.all_gather(part, axis), shard)]
    pallas_call x0 -> x2, Pallas kernels: none -> 241 us  [the longest x1 145 us: tail(): pl.pallas_call(partial(tail_kernel, n_dev), in_specs=[vmem] * 12 + [hbm]...]
    psum x2 -> x0, blocking collectives: 237 us -> none  [the longest x1 201 us: per_device(): end_dout, end_delta = lax.psum((own_dout, own_delta), 'seq')]
    dot_general x12 -> x0, matrix products: 153 us -> none  [the longest x1 47.6 us: per_device(): jnp.einsum('sbhqk,sbhqd->sbhkd', grad_score, q_blocks, preferred_element_...]
    ppermute x4 -> x0, waiting for transfers between devices: 127 us -> none  [the longest x2 117 us: with_halo(): before = lax.ppermute(last, axis, up)]
    scatter-add x1 -> x0, other arithmetic: 90 us -> none  [per_device(): table_grad = jnp.zeros((seqs * per_dev * heads, block, 2 * hsize), jnp.fl...]
    reshape x18 -> x4, local copies, waits for them, and re-layouts: 64.9 us -> 0.19 us  [the longest x2 0.15 us: share(): whole = small[first:first + 4 * size // width].reshape(4, size)]
  transfers between devices with their start and end apart: 15 -> 0, of which waited for: 11 -> 0; matrix products, arithmetic and copies ran while one was open for 15% -> 0% of each run, Pallas kernels for 0% -> 0%
where the time goes in v3:
time: 297 us
  Pallas kernels  241 us (81%)
  matrix products  29.7 us (10%)
  local copies, waits for them, and re-layouts  15.8 us (5%)
  other arithmetic  9.78 us (3%)
    pallas_call x1, Pallas kernels, tail(): pl.pallas_call(partial(tail_kernel, n_dev), in_specs=[vmem] * 12 + [hbm]...  145 us
    pallas_call x1, Pallas kernels, enter(): pl.pallas_call(partial(enter_kernel, n_dev), in_specs=[hbm, hbm, vmem] +...  95.7 us
    dot_general x3, matrix products, rows_dot(): lax.dot_general(left, right, (((0,), (0,)), ((), ())), preferred_element_...  11 us
    dot_general x3, matrix products, back_dot(): lax.dot_general(left, right, (((1,), (1,)), ((), ())), preferred_element_...  9.79 us
    dot_general x3, matrix products, plain_dot(): return jnp.dot(left, right, preferred_element_type=jnp.float32)  8.91 us

profile of v3, /device:TPU:0, one launch (start us, length us, event | category | flops | bytes accessed | tf_op | source)
XLA Modules:
  0.0 297.0 jit_solution(18377073733318346426)
XLA Ops:
  0.7 1.3 broadcast_in_dim.10.ub
  1.9 95.7 %shard_map.305 = (bf16[512,768]{1,0:T(8,128)(2,1)}, bf16[512,768]{1,0:T(8,128)(2,1)}, bf16[512,768]{1,0:T(8,128)(2,1)}, bf16[512,768]{1,0:T(8,128)(2,1)}, bf16[5...) custom-call(bf16[16,128,768]{2,1,0:T(8,128)(2,1)} %tok.1, ...), custom_call_target="tpu_custom_call" | custom-call | tf_op jit(solution)/shard_map/pallas_call | solution.py:737
  97.7 2.8 fusion.22
  101.3 3.4 %multiply_convert_fusion.1 = (bf16[512,3072]{1,0:T(8,128)(2,1)S(1)}, f32[512,3072]{1,0:T(8,128)S(1)}) fusion(f32[3072]{0:T(1024)S(1)} %bitcast.54, bf16[768,3072]{1,0:T(8,128)(2,1)S(1)} %copy-done.9, f32[512,768]{1,0:T(8,128)S(1)} %get-tuple-element.83, f32[768]{0:T(1024)S(1)} %copy-done.14, f32[768]{0:T(1024)S(1)} %copy-done.8, ...), kind=kOutput, calls=%fused_computation.8 | convolution fusion | flops 2427322368 | bytes 15751168 | tf_op jit(solution)/shard_map/dot_general | solution.py:53
  104.7 2.8 fusion.23
  107.8 0.8 copy-done.4
  108.6 1.8 fusion.11
  111.0 4.9 %convert_reduce_fusion = (f32[3072]{0:T(1024)S(1)}, bf16[512,3072]{1,0:T(8,128)(2,1)S(1)}) fusion(f32[512,3072]{1,0:T(8,128)S(1)} %get-tuple-element.85, f32[3072]{0:T(1024)S(1)} %bitcast.55, bf16[3072,768]{1,0:T(8,128)(2,1)S(1)} %bitcast.53, f32[512,768]{1,0:T(8,128)S(1)} %get-tuple-element.72), kind=kOutput, calls=%fused_computation.6 | convolution fusion | flops 2439902208 | bytes 15753216 | tf_op jit(solution)/shard_map/dot_general | solution.py:63
  116.0 3.1 %multiply_reduce_fusion = (f32[768]{0:T(1024)S(1)}, f32[512]{0:T(512)S(1)}, f32[512]{0:T(512)S(1)}, f32[768]{0:T(1024)S(1)}, f32[512,768]{1,0:T(8,128)S(1)}) fusion(f32[512,768]{1,0:T(8,128)S(1)} %get-tuple-element.83, f32[512]{0:T(512)S(1)} %add_rsqrt_fusion.1, f32[512]{0:T(512)S(1)} %broadcast_multiply_fusion.4, f32[768]{0:T(1024)S(1)} %copy-done.8, ...), kind=kOutput, calls=%fused_computation.25 | convolution fusion | flops 2419848704 | bytes 12600320 | tf_op jit(solution)/shard_map/dot_general | solution.py:63
  120.3 1.8 convolution_convert_fusion.2.go
  122.1 4.9 %convolution_convert_fusion.gu = bf16[768,3072]{1,0:T(8,128)(2,1)} fusion(bf16[512,3072]{1,0:T(8,128)(2,1)S(1)} %get-tuple-element.90, f32[512,768]{1,0:T(8,128)S(1)} %get-tuple-element.83, f32[768]{0:T(1024)S(1)} %copy-done.14, f32[768]{0:T(1024)S(1)} %copy-done.8, f32[512]{0:T(512)S(1)} %add_rsqrt_fusion.1, f32[512]{0:T(512)S(1)} %broadcast_multiply_fusion.4), kind=kOutput, calls=%fused_computation.10 | convolution fusion | flops 2420244480 | bytes 9447424 | tf_op jit(solution)/shard_map/dot_general | solution.py:57
  127.0 4.3 %convolution_convert_fusion.1.gd = bf16[3072,768]{1,0:T(8,128)(2,1)} fusion(bf16[512,3072]{1,0:T(8,128)(2,1)S(1)} %get-tuple-element.84, f32[512,768]{1,0:T(8,128)S(1)} %get-tuple-element.72), kind=kOutput, calls=%fused_computation.11 | convolution fusion | flops 2418671616 | bytes 9437184 | tf_op jit(solution)/shard_map/dot_general | solution.py:57
  131.4 1.3 concatenate.7.early
  132.7 1.7 convolution_convert_fusion.3.gat
  134.4 145.0 %shard_map.306 = (bf16[6,384,768]{2,1,0:T(8,128)(2,1)}, bf16[8,2,128,768]{3,2,1,0:T(8,128)(2,1)}, bf16[8,2,128,768]{3,2,1,0:T(8,128)(2,1)}, f32[6,16,768]{2,1,0:T(8,128)}) custom-call(bf16[512,768]{1,0:T(8,128)(2,1)} %get-tuple-element.36.q, bf16[512,768]{1,0:T(8,128)(2,1)} %get-tuple-element.37.ko, bf16[512,768]{1,0:T(8,128)(2,1)} %get-tuple-element.38.kf, ...), custom_call_target="tpu_custom_call" | custom-call | tf_op jit(solution)/shard_map/pallas_call | solution.py:1205
  279.4 2.6 convert_element_type.72
  282.1 1.4 slice_bitcast_fusion
  283.5 1.3 copy-done.3
  284.8 3.6 %bitcast_convert_fusion = f32[16,128,768]{2,1,0:T(8,128)} fusion(bf16[8,2,128,768]{3,2,1,0:T(8,128)(2,1)S(1)} %copy-done.3), kind=kLoop, calls=%fused_computation.12 | loop fusion | flops 1572864 | bytes 9437184 | tf_op jit(solution)/shard_map/reshape | solution.py:1350
  288.4 2.6 fusion.21
  291.0 1.6 slice_reduce_fusion
  293.9 0.7 slice.74
  294.7 0.6 dynamic-slice_reduce_fusion
  295.3 1.7 copy.36
  (59 shorter events, 4.2 us)
Async XLA Ops:
  1.9 95.7 %copy-start.12 = (f32[768]{0:T(1024)S(1)}, f32[768]{0:T(1024)}, u32[]{:S(2)}) copy-start(f32[768]{0:T(1024)} %param.26) | copy-start | bytes 9220
  97.7 3.2 %copy-start.9 = (bf16[768,3072]{1,0:T(8,128)(2,1)S(1)}, bf16[768,3072]{1,0:T(8,128)(2,1)}, u32[]{:S(2)}) copy-start(bf16[768,3072]{1,0:T(8,128)(2,1)} %get-tuple-element.47) | copy-start | bytes 14155780
  100.4 0.8 copy-start.8
  100.4 0.8 copy-start.11
  100.5 0.8 copy-start.14
  100.5 4.2 %slice-start = ((s8[4718592]{0:T(1024)(128)(4,1)}), s8[4194304]{0:T(1024)(128)(4,1)S(1)}, s32[]{:S(2)}) async-start(s8[4718592]{0:T(1024)(128)(4,1)} %bitcast.52), calls=%async_computation | async-start | bytes 8388608
  101.3 3.4 %slice-start.1 = ((s8[4718592]{0:T(1024)(128)(4,1)}), s8[524288]{0:T(1024)(128)(4,1)S(1)}, s32[]{:S(2)}) async-start(s8[4718592]{0:T(1024)(128)(4,1)} %bitcast.52), calls=%async_computation.1 | async-start | bytes 1048576
  101.3 3.4 %copy-start.13 = (f32[768]{0:T(1024)S(1)}, f32[768]{0:T(1024)}, u32[]{:S(2)}) copy-start(f32[768]{0:T(1024)} %param.32) | copy-start | bytes 9220
  107.5 1.1 copy-start.4
  107.5 1.1 copy-start.6
  107.5 1.1 copy-start.7
  119.1 1.1 copy-start.5
  119.7 13.0 %copy-start.1 = (f32[512,768]{1,0:T(8,128)}, f32[512,768]{1,0:T(8,128)S(1)}, u32[]{:S(2)}) copy-start(f32[512,768]{1,0:T(8,128)S(1)} %get-tuple-element.74.gres) | copy-start | bytes 4718596
  127.0 5.8 %copy-start.10 = (bf16[768,768]{1,0:T(8,128)(2,1)S(1)}, bf16[768,768]{1,0:T(8,128)(2,1)}, u32[]{:S(2)}) copy-start(bf16[768,768]{1,0:T(8,128)(2,1)} %get-tuple-element.46) | copy-start | bytes 3538948
  282.1 2.7 copy-start.3
  284.8 3.6 %copy-start = (bf16[6,384,768]{2,1,0:T(8,128)(2,1)S(1)}, bf16[6,384,768]{2,1,0:T(8,128)(2,1)}, u32[]{:S(2)}) copy-start(bf16[6,384,768]{2,1,0:T(8,128)(2,1)} %get-tuple-element.53) | copy-start | bytes 10616836
  288.4 6.9 %copy-start.2 = (bf16[8,2,128,768]{3,2,1,0:T(8,128)(2,1)S(1)}, bf16[8,2,128,768]{3,2,1,0:T(8,128)(2,1)}, u32[]{:S(2)}) copy-start(bf16[8,2,128,768]{3,2,1,0:T(8,128)(2,1)} %get-tuple-element.51) | copy-start | bytes 9437188

commit v4 on v3

--- a/solution.py
+++ b/solution.py
@@ -509,6 +509,7 @@
         self.mate = (mate, t)
         self.near, self.across = (me, tp_peer(side, core, 1)), (me, tp_peer(side, core, 2))
         self.sems = sems
+        self.then = []
 
     def move(self, n):
         h = 1 - self.half if n == 3 else self.half
@@ -521,6 +522,8 @@
 
     def pass_on(self):
         self.move(0).wait_recv()
+        for piece in self.then:
+            piece.start()
         self.move(1).start()
         self.move(2).start()
 
@@ -540,7 +543,7 @@
 def enter_kernel(
     n_dev, tok, cot, rand, wq, wk, wv, qb, vb, ub, wo, up, down,
     x, q, ko, kf, vo, vf, attn, lse, ids, ubs, wt_out, cot_out, wo_out, up_out, down_out,
-    wt, qbs, vbs, ids_for,
+    wt, qbs, vbs, ids_for, own_wo, own_up, own_down,
     tok_send, tok_recv, cot_send, cot_recv, p_send, p_recv, o_send, o_recv, s_send, s_recv, kv_send, kv_recv, local,
 ):
     spots = me, t, side, core = place()
@@ -552,6 +555,7 @@
     pairs = width // (2 * HD)
     part = hidden // 2
     n_part = units // 2 // part
+    own_buf = (own_wo, own_up, own_down)
 
     holds = [(w, lambda j, m=m: wt.at[m, j]) for m, w in ((1, wk), (2, wv), (0, wq))]
     holds += [
@@ -577,11 +581,19 @@
                 )
             )
 
+    ahead = 4
+    for piece, later in zip(pieces, pieces[ahead:]):
+        piece.then = [later]
+
     def own_near(n):
         return remote(holds[n][0], holds[n][1](core), o_send, o_recv, n, near)
 
     def own_here(n):
-        return pltpu.make_async_copy(holds[n][0], holds[n][1](core), local.at[n])
+        src = holds[n][0] if n < 3 else own_buf[n - 3]
+        return pltpu.make_async_copy(src, holds[n][1](core), local.at[n])
+
+    def own_in(n):
+        return pltpu.make_async_copy(holds[n][0], own_buf[n - 3], local.at[6 + n])
 
     def spread(src, dst, sends, recvs):
         return [
@@ -596,7 +608,7 @@
     def kept(n):
         src, dst = ((tok, x), (cot, cot_out))[n]
         return pltpu.make_async_copy(
-            src.at[2 * me + side, pl.ds(core * BLOCK, BLOCK), :], dst.at[pl.ds(0, BLOCK), :], local.at[6 + n]
+            src.at[2 * me + side, pl.ds(core * BLOCK, BLOCK), :], dst.at[pl.ds(0, BLOCK), :], local.at[12 + n]
         )
 
     def shared(bits, which=(0, 1, 2, 3)):
@@ -613,7 +625,7 @@
     greet(all_peers(n_dev, *spots) + [(me, tp_peer(side, core, 3))])
     for move in spread(tok, x, tok_send, tok_recv):
         move.start()
-    for piece in pieces[:3]:
+    for piece in pieces[:ahead]:
         piece.start()
     kept(0).start()
     for n in range(3):
@@ -623,11 +635,8 @@
     for bits in (1, 2, 3):
         for move in shared(bits, (0, 1, 2)):
             move.start()
-    for piece in pieces[3:]:
-        piece.start()
     for n in range(3, 6):
-        own_near(n).start()
-        own_here(n).start()
+        own_in(n).start()
 
     lane = lax.broadcasted_iota(jnp.int32, (1, span), 1)
     for y in range(2):
@@ -644,16 +653,23 @@
     for bits in (1, 2, 3):
         shared(bits, (3,))[0].start()
 
-    for piece in pieces[:3]:
-        piece.pass_on()
-    for piece in pieces[:3]:
-        piece.pass_side()
+    def advance(n):
+        pieces[n].pass_on()
+        if n:
+            pieces[n - 1].pass_side()
+
+    for n in range(4):
+        advance(n)
     for move in spread(tok, x, tok_send, tok_recv):
         move.wait_recv()
     kept(0).wait()
     for move in spread(cot, cot_out, cot_send, cot_recv):
         move.start()
     kept(1).start()
+    for n in range(3, 6):
+        own_near(n).start()
+        own_in(n).wait()
+        own_here(n).start()
     for bits in (1, 2, 3):
         for move in shared(bits):
             move.wait_recv()
@@ -675,31 +691,28 @@
     swap_kv(0).start()
     vo[...] = (project(1, 2) + bias_of(vbs)).astype(jnp.bfloat16)
     swap_kv(1).start()
+    advance(4)
     q[...] = (project(2, 0) + bias_of(qbs)).astype(jnp.bfloat16)
-    keep = pltpu.make_async_copy(wt, wt_out, local.at[8])
+    keep = pltpu.make_async_copy(wt, wt_out, local.at[14])
     keep.start()
-    for n in (3, 4):
-        pieces[n].pass_on()
-    pieces[3].pass_side()
+    advance(5)
     swap_kv(0).wait_recv()
     swap_kv(1).wait_recv()
 
     def pair(p, carry):
         lanes = pl.ds(pl.multiple_of(p * 2 * HD, 2 * HD), 2 * HD)
         attend_pair(n_dev, p, lanes, q, ko, kf, vo, vf, ids, attn, lse, me, core)
-        for k in range(5):
-
-            @pl.when(p == k)
+        for k in range(3):
+
+            @pl.when(p == 2 * k + 1)
             def _():
-                pieces[5 + k].pass_on()
-                pieces[4 + k].pass_side()
+                advance(6 + k)
 
         return carry
 
     lax.fori_loop(0, pairs, pair, 0)
-    for n in range(10, len(pieces)):
-        pieces[n].pass_on()
-        pieces[n - 1].pass_side()
+    for n in range(9, len(pieces)):
+        advance(n)
     pieces[-1].pass_side()
     for n in range(3, len(pieces)):
         pieces[n].arrive()
@@ -754,6 +767,9 @@
             pltpu.VMEM((4, 1, hidden), jnp.float32),
             pltpu.VMEM((4, 1, hidden), jnp.float32),
             pltpu.VMEM((4, heads, 3, span), jnp.int32),
+            pltpu.VMEM(wo.shape, jnp.bfloat16),
+            pltpu.VMEM(up.shape, jnp.bfloat16),
+            pltpu.VMEM(down.shape, jnp.bfloat16),
             dma((n_dev - 1,)),
             dma((n_dev - 1,)),
             dma((n_dev - 1,)),
@@ -766,7 +782,7 @@
             dma((3, 4)),
             dma((2,)),
             dma((2,)),
-            dma((9,)),
+            dma((15,)),
         ],
         compiler_params=pltpu.CompilerParams(
             collective_id=0, has_side_effects=True, vmem_limit_bytes=56 * 2**20
@@ -828,6 +844,7 @@
 class Reduction:
     def __init__(self, parts, mine, spots, bufs, sems):
         self.parts, self.mine = parts, mine
+        self.jobs, self.ahead = [], 3
         self.me, self.t, self.side, self.core = spots
         self.b0, self.b1, self.acc, self.halves, self.got, self.f = bufs
         self.send, self.recv, self.send0, self.recv0 = sems
@@ -867,6 +884,10 @@
     def over_y(self, ch):
         return remote(self.mine(ch, 1), self.b1.at[ch], self.send, self.recv, (ch, 0), self.across)
 
+    def next_y(self, job):
+        if job + self.ahead < len(self.jobs):
+            self.jobs[job + self.ahead]().start()
+
     def halving(self, ch, level):
         size = self.rows(level + 1)[2]
         return remote(
@@ -890,9 +911,11 @@
                 move.wait_recv()
             out = self.mine(ch, 1)
             out[...] = (out[...].astype(full) + self.b0[ch, 1].astype(full)).astype(jnp.bfloat16)
-            self.over_y(ch).start()
+            if ch < self.ahead:
+                self.over_y(ch).start()
         elif s == 2:
             self.over_y(ch).wait_recv()
+            self.next_y(ch)
             size = self.rows(1)[2]
 
             def total(start):
@@ -970,10 +993,10 @@
             self.keep().wait()
             for k in range(1, self.n_dev):
                 self.out(k).wait_recv()
-            self.pass_on(0).start()
             self.pass_on(1).start()
         elif s == 2:
             self.pass_on(0).wait_recv()
+            self.then()
             self.pass_on(2).start()
         else:
             for k in range(1, self.n_dev):
@@ -1034,10 +1057,10 @@
             return [gd.at[pl.ds(block * units + ch * rows, rows), :]]
         if ch < n_ffn:
             return [gu.at[pl.ds((ch - n_down) * rows, rows), pl.ds(block * units, units)]]
-        return [p2.at[ch - n_ffn, block]]
+        return [p2.at[block, pl.ds((ch - n_ffn) * rows, rows), :]]
 
     def mine(ch, y):
-        return load.at[ch, y] if ch < n_ffn else p2.at[ch - n_ffn, 2 * y + core]
+        return load.at[ch, y] if ch < n_ffn else parts(ch, 2 * y + core)[0]
 
     red = Reduction(parts, mine, spots, (b0, b1, acc, halves, got, f), (send, recv, send0, recv0))
     back = [
@@ -1054,7 +1077,7 @@
 
     def others():
         pieces = [(wt_hbm, wt)] + [
-            (go.at[pl.ds(j * hidden, hidden), :], p2.at[0, j, pl.ds(0, hidden), :]) for j in range(4)
+            (go.at[pl.ds(j * hidden, hidden), :], p2.at[j, pl.ds(0, hidden), :]) for j in range(4)
         ]
         return [
             pltpu.make_async_copy(a, b, local.at[2 * n_ffn + n]) for n, (a, b) in enumerate(pieces)
@@ -1063,11 +1086,23 @@
     def swap_far(p, n):
         return remote(far.at[n, p], far_in.at[n, p], x_send, x_recv, (p, n), near)
 
-    greet(all_peers(n_dev, *spots))
-    for ch in range(n_ffn):
+    red.jobs = [partial(red.over_y, ch) for ch in range(count)]
+    red.jobs += [partial(b.pass_on, 0) for b in back]
+    back[0].then, back[1].then = partial(red.next_y, count), partial(red.next_y, count + 1)
+
+    def begin(ch):
         red.stage(ch, 0)
         for move in loads(ch):
             move.start()
+
+    def second(ch):
+        for move in loads(ch):
+            move.wait()
+        red.stage(ch, 1)
+
+    greet(all_peers(n_dev, *spots))
+    for ch in range(n_ffn // 2):
+        begin(ch)
     back[0].stage(0)
     for move in others():
         move.start()
@@ -1082,9 +1117,9 @@
             @pl.when(p == k)
             def _():
                 for ch in range(k * n_ffn // 2, (k + 1) * n_ffn // 2):
-                    for move in loads(ch):
-                        move.wait()
-                    red.stage(ch, 1)
+                    second(ch)
+                for ch in range(n_ffn // 2, (1 - k) * n_ffn):
+                    begin(ch)
 
         return carry
 
@@ -1098,10 +1133,10 @@
         cat = jnp.concatenate([far_in[n, p] for p in range(pairs)], 1)
         return (own[n] + cat.astype(jnp.float32)).astype(jnp.bfloat16)
 
-    def weight_grad(low_grad, ch, at):
+    def weight_grad(low_grad, at):
         grad = plain_dot(low_grad.T, x[...]).astype(jnp.bfloat16)
         for j in range(4):
-            p2[ch, j, pl.ds(at, hidden), :] = grad[j * hidden : (j + 1) * hidden]
+            p2[j, pl.ds(at * hidden, hidden), :] = grad[j * hidden : (j + 1) * hidden]
 
     def column_sum(low_grad):
         sums = jnp.sum(low_grad.astype(jnp.float32), 0, keepdims=True)
@@ -1109,36 +1144,40 @@
         return jnp.where(side == 0, sums, turned)
 
     red.stage(0, 2)
-    weight_grad(dq[...], 0, hidden)
+    weight_grad(dq[...], 1)
     for move in others():
         move.wait()
     red.stage(n_ffn, 0)
     dk = joined_low(0)
-    weight_grad(dk, 1, 0)
+    weight_grad(dk, 2)
+    red.stage(n_ffn + 1, 0)
+    red.stage(1, 2)
     dv = joined_low(1)
-    weight_grad(dv, 1, hidden)
-    red.stage(n_ffn + 1, 0)
+    weight_grad(dv, 3)
+    for ch in range(n_ffn + 2, count):
+        red.stage(ch, 0)
+    red.stage(0, 3)
     total[0] = early[...]
     total[0, 0:1, :] = column_sum(dq[...])
     total[0, 1:2, :] = column_sum(dv)
     tiny.stage(0)
-    red.stage(n_ffn, 1)
     matrix = lambda m: wt[m].reshape(width, width)
     into = gres[...] + plain_dot(dq[...], matrix(0))
     into = into + plain_dot(dk, matrix(1))
     ig[...] = (into + plain_dot(dv, matrix(2))).astype(jnp.bfloat16)
-    red.stage(n_ffn + 1, 1)
     back[1].stage(0)
+    for ch in range(n_ffn, count):
+        red.stage(ch, 1)
     back[0].stage(1)
 
     events = []
+    done = [(0, 2), (0, 3), (1, 2)]
     for ch in range(count):
         for s in range(2, 9):
-            if (ch, s) != (0, 2):
-                events.append((17 + 12.6 * ch + (0, 0, 0, 8, 13, 18, 23, 28, 35)[s], red, (ch, s)))
-    for n in range(1, 6):
-        events.append(((36, 84, 88, 92, 98)[n - 1], tiny, (n,)))
-    events += [(55, back[1], (1,)), (96, back[0], (2,)), (114, back[1], (2,))]
+            if (ch, s) not in done:
+                events.append((10 + 8 * (ch + 1) + (0, 10, 18, 26, 34, 42, 51)[s - 2], red, (ch, s)))
+    events += [(33 + 7 * n, tiny, (n,)) for n in range(1, 6)]
+    events += [(58, back[1], (1,)), (106, back[0], (2,)), (123, back[1], (2,))]
     for _, who, what in sorted(events, key=lambda e: e[0]):
         who.stage(*what)
     for b in back:
@@ -1192,9 +1231,9 @@
 def tail(q, ko, kf, vo, vf, ids, lse, attn, gat, x, gres, early, gd, gu, go, low, wt, n_dev):
     span, width = q.shape
     hidden = go.shape[0] // 4
-    rows = 2 * hidden
+    rows = 256
     n_ffn = (gd.shape[0] // 4 + gu.shape[0]) // rows
-    count = n_ffn + 2
+    count = n_ffn + go.shape[0] // rows
     pairs = width // (2 * HD)
     vmem = pl.BlockSpec(memory_space=pltpu.VMEM)
     hbm = pl.BlockSpec(memory_space=pl.ANY)
@@ -1214,7 +1253,7 @@
         ],
         scratch_shapes=[
             low_buf(n_ffn, 2, rows),
-            low_buf(2, 4, rows),
+            low_buf(4, 4 * hidden),
             pltpu.VMEM(wt.shape, jnp.bfloat16),
             low_buf(count, 2, rows),
             low_buf(count, rows),
@@ -1343,8 +1382,8 @@
     half = units // sums.shape[1]
     g_down = sums[:half].reshape(units, width)
     g_up = sums[half : half + width // sums.shape[1]].reshape(width, units)
-    g_o, g_q = sums[-2, :hidden], sums[-2, hidden:]
-    g_k, g_v = sums[-1, :hidden], sums[-1, hidden:]
+    rest = sums[half + width // sums.shape[1] :].reshape(4, hidden, width)
+    g_o, g_q, g_k, g_v = rest
     return (
         layer_output.reshape(seqs, rows, width),
         input_out.astype(jnp.float32).reshape(seqs, rows, width),

time: 297 us -> 259 us (0.87)
  Pallas kernels: 241 us -> 203 us
    pallas_call x1, Pallas kernels: 95.7 us -> 68.8 us  [enter(): pl.pallas_call(partial(enter_kernel, n_dev), in_specs=[hbm, hbm, vmem] +...]
    pallas_call x1, Pallas kernels: 145 us -> 134 us  [tail(): pl.pallas_call(partial(tail_kernel, n_dev), in_specs=[vmem] * 12 + [hbm]...]
where the time goes in v4:
time: 259 us; the launch traced here: 258 us
  Pallas kernels  203 us (78%)
  matrix products  29.7 us (11%)
  local copies, waits for them, and re-layouts  17.8 us (7%)
  other arithmetic  7.14 us (3%)
    pallas_call x1, Pallas kernels, tail(): pl.pallas_call(partial(tail_kernel, n_dev), in_specs=[vmem] * 12 + [hbm]...  134 us
    pallas_call x1, Pallas kernels, enter(): pl.pallas_call(partial(enter_kernel, n_dev), in_specs=[hbm, hbm, vmem] +...  68.8 us
    dot_general x3, matrix products, rows_dot(): lax.dot_general(left, right, (((0,), (0,)), ((), ())), preferred_element_...  11 us
    dot_general x3, matrix products, back_dot(): lax.dot_general(left, right, (((1,), (1,)), ((), ())), preferred_element_...  9.79 us
    dot_general x3, matrix products, plain_dot(): return jnp.dot(left, right, preferred_element_type=jnp.float32)  8.91 us

profile of v4, /device:TPU:0, one launch (start us, length us, event | category | flops | bytes accessed | tf_op | source)
XLA Modules:
  0.0 258.3 jit_solution(4426618924691811039)
XLA Ops:
  0.7 1.3 broadcast_in_dim.10.ub
  1.9 68.8 %shard_map.305 = (bf16[512,768]{1,0:T(8,128)(2,1)}, bf16[512,768]{1,0:T(8,128)(2,1)}, bf16[512,768]{1,0:T(8,128)(2,1)}, bf16[512,768]{1,0:T(8,128)(2,1)}, bf16[5...) custom-call(bf16[16,128,768]{2,1,0:T(8,128)(2,1)} %tok.1, ...), custom_call_target="tpu_custom_call" | custom-call | tf_op jit(solution)/shard_map/pallas_call | solution.py:750
  70.7 2.8 %fusion.22 = (f32[512]{0:T(512)S(1)}, f32[512,768]{1,0:T(8,128)S(1)}) fusion(f32[768]{0:T(1024)S(1)} %copy-done.11, bf16[512,768]{1,0:T(8,128)(2,1)} %get-tuple-element.43.attn, bf16[768,768]{1,0:T(8,128)(2,1)} %get-tuple-element.46, bf16[512,768]{1,0:T(8,128)(2,1)} %get-tuple-element.45.x), kind=kOutput, calls=%fused_computation.71 | convolution fusion | flops 605552128 | bytes 4330496 | tf_op jit(solution)/shard_map/dot_general | solution.py:53
  74.3 3.4 %multiply_convert_fusion.1 = (bf16[512,3072]{1,0:T(8,128)(2,1)S(1)}, f32[512,3072]{1,0:T(8,128)S(1)}) fusion(f32[3072]{0:T(1024)S(1)} %bitcast.56, bf16[768,3072]{1,0:T(8,128)(2,1)S(1)} %copy-done.8, f32[512,768]{1,0:T(8,128)S(1)} %get-tuple-element.84, f32[768]{0:T(1024)S(1)} %copy-done.13, f32[768]{0:T(1024)S(1)} %copy-done.7, ...), kind=kOutput, calls=%fused_computation.8 | convolution fusion | flops 2427322368 | bytes 15751168 | tf_op jit(solution)/shard_map/dot_general | solution.py:53
  77.7 2.8 %fusion.23 = (f32[512]{0:T(512)S(1)}, f32[512,768]{1,0:T(8,128)S(1)}) fusion(f32[768]{0:T(1024)S(1)} %copy-done.12, bf16[512,3072]{1,0:T(8,128)(2,1)S(1)} %get-tuple-element.85, bf16[3072,768]{1,0:T(8,128)(2,1)S(1)} %bitcast.55, f32[768]{0:T(1024)S(1)} %copy-done.13, f32[768]{0:T(1024)S(1)} %copy-done.7, f32[512]{0:T(512)S(1)} %add_rsqrt_fusion.1, ...), kind=kOutput, calls=%fused_computation.72 | convolution fusion | flops 2418671104 | bytes 11025408 | tf_op jit(solution)/shard_map/dot_general | solution.py:53
  80.9 0.8 copy-done.3
  81.7 1.8 fusion.11
  84.0 4.9 %convert_reduce_fusion = (f32[3072]{0:T(1024)S(1)}, bf16[512,3072]{1,0:T(8,128)(2,1)S(1)}) fusion(f32[512,3072]{1,0:T(8,128)S(1)} %get-tuple-element.86, f32[3072]{0:T(1024)S(1)} %bitcast.57, bf16[3072,768]{1,0:T(8,128)(2,1)S(1)} %bitcast.55, f32[512,768]{1,0:T(8,128)S(1)} %get-tuple-element.72), kind=kOutput, calls=%fused_computation.6 | convolution fusion | flops 2439902208 | bytes 15753216 | tf_op jit(solution)/shard_map/dot_general | solution.py:63
  89.0 3.1 %multiply_reduce_fusion = (f32[768]{0:T(1024)S(1)}, f32[512]{0:T(512)S(1)}, f32[512]{0:T(512)S(1)}, f32[768]{0:T(1024)S(1)}, f32[512,768]{1,0:T(8,128)S(1)}) fusion(f32[512,768]{1,0:T(8,128)S(1)} %get-tuple-element.84, f32[512]{0:T(512)S(1)} %add_rsqrt_fusion.1, f32[512]{0:T(512)S(1)} %broadcast_multiply_fusion.4, f32[768]{0:T(1024)S(1)} %copy-done.7, ...), kind=kOutput, calls=%fused_computation.25 | convolution fusion | flops 2419848704 | bytes 12600320 | tf_op jit(solution)/shard_map/dot_general | solution.py:63
  92.7 0.6 copy-done.4
  93.3 1.8 convolution_convert_fusion.2.go
  95.1 4.9 %convolution_convert_fusion.gu = bf16[768,3072]{1,0:T(8,128)(2,1)} fusion(bf16[512,3072]{1,0:T(8,128)(2,1)S(1)} %get-tuple-element.91, f32[512,768]{1,0:T(8,128)S(1)} %get-tuple-element.84, f32[768]{0:T(1024)S(1)} %copy-done.13, f32[768]{0:T(1024)S(1)} %copy-done.7, f32[512]{0:T(512)S(1)} %add_rsqrt_fusion.1, f32[512]{0:T(512)S(1)} %broadcast_multiply_fusion.4), kind=kOutput, calls=%fused_computation.10 | convolution fusion | flops 2420244480 | bytes 9447424 | tf_op jit(solution)/shard_map/dot_general | solution.py:57
  100.0 4.3 %convolution_convert_fusion.1.gd = bf16[3072,768]{1,0:T(8,128)(2,1)} fusion(bf16[512,3072]{1,0:T(8,128)(2,1)S(1)} %get-tuple-element.85, f32[512,768]{1,0:T(8,128)S(1)} %get-tuple-element.72), kind=kOutput, calls=%fused_computation.11 | convolution fusion | flops 2418671616 | bytes 9437184 | tf_op jit(solution)/shard_map/dot_general | solution.py:57
  104.5 1.3 concatenate.7.early
  105.7 1.7 convolution_convert_fusion.3.gat
  107.4 133.9 %shard_map.306 = (bf16[9,256,768]{2,1,0:T(8,128)(2,1)}, bf16[8,2,128,768]{3,2,1,0:T(8,128)(2,1)}, bf16[8,2,128,768]{3,2,1,0:T(8,128)(2,1)}, f32[6,16,768]{2,1,0:T(8,128)}) custom-call(bf16[512,768]{1,0:T(8,128)(2,1)} %get-tuple-element.36.q, bf16[512,768]{1,0:T(8,128)(2,1)} %get-tuple-element.37.ko, bf16[512,768]{1,0:T(8,128)(2,1)} %get-tuple-element.38.kf, ...), custom_call_target="tpu_custom_call" | custom-call | tf_op jit(solution)/shard_map/pallas_call | solution.py:1244
  241.4 4.7 %fusion.21 = (f32[3,256,768]{2,1,0:T(8,128)}, f32[3,256,768]{2,1,0:T(8,128)}, f32[3,256,768]{2,1,0:T(8,128)S(1)}) fusion(bf16[9,256,768]{2,1,0:T(8,128)(2,1)} %get-tuple-element.53), kind=kLoop, calls=%fused_computation.70 | loop fusion | bytes 14155776 | tf_op jit(solution)/shard_map/slice | solution.py:1383
  246.0 1.4 slice_bitcast_fusion
  247.5 1.3 copy-done.2
  248.8 3.6 %bitcast_convert_fusion = f32[16,128,768]{2,1,0:T(8,128)} fusion(bf16[8,2,128,768]{3,2,1,0:T(8,128)(2,1)S(1)} %copy-done.2), kind=kLoop, calls=%fused_computation.12 | loop fusion | flops 1572864 | bytes 9437184 | tf_op jit(solution)/shard_map/reshape | solution.py:1389
  252.4 1.6 slice_reduce_fusion
  255.3 0.7 slice.62
  256.0 0.6 dynamic-slice_reduce_fusion
  256.7 1.7 copy.36
  (56 shorter events, 3.6 us)
Async XLA Ops:
  1.9 68.8 %copy-start.11 = (f32[768]{0:T(1024)S(1)}, f32[768]{0:T(1024)}, u32[]{:S(2)}) copy-start(f32[768]{0:T(1024)} %param.26) | copy-start | bytes 9220
  70.7 3.2 %copy-start.8 = (bf16[768,3072]{1,0:T(8,128)(2,1)S(1)}, bf16[768,3072]{1,0:T(8,128)(2,1)}, u32[]{:S(2)}) copy-start(bf16[768,3072]{1,0:T(8,128)(2,1)} %get-tuple-element.47) | copy-start | bytes 14155780
  73.5 0.8 copy-start.7
  73.5 0.8 copy-start.10
  73.5 0.8 copy-start.13
  73.5 4.2 %slice-start = ((s8[4718592]{0:T(1024)(128)(4,1)}), s8[4194304]{0:T(1024)(128)(4,1)S(1)}, s32[]{:S(2)}) async-start(s8[4718592]{0:T(1024)(128)(4,1)} %bitcast.54), calls=%async_computation | async-start | bytes 8388608
  74.3 3.4 %slice-start.1 = ((s8[4718592]{0:T(1024)(128)(4,1)}), s8[524288]{0:T(1024)(128)(4,1)S(1)}, s32[]{:S(2)}) async-start(s8[4718592]{0:T(1024)(128)(4,1)} %bitcast.54), calls=%async_computation.1 | async-start | bytes 1048576
  74.3 3.4 %copy-start.12 = (f32[768]{0:T(1024)S(1)}, f32[768]{0:T(1024)}, u32[]{:S(2)}) copy-start(f32[768]{0:T(1024)} %param.32) | copy-start | bytes 9220
  80.5 1.1 copy-start.3
  80.5 1.1 copy-start.5
  80.5 1.1 copy-start.6
  92.2 1.1 copy-start.4
  92.7 13.0 %copy-start = (f32[512,768]{1,0:T(8,128)}, f32[512,768]{1,0:T(8,128)S(1)}, u32[]{:S(2)}) copy-start(f32[512,768]{1,0:T(8,128)S(1)} %get-tuple-element.74.gres) | copy-start | bytes 4718596
  100.0 5.8 %copy-start.9 = (bf16[768,768]{1,0:T(8,128)(2,1)S(1)}, bf16[768,768]{1,0:T(8,128)(2,1)}, u32[]{:S(2)}) copy-start(bf16[768,768]{1,0:T(8,128)(2,1)} %get-tuple-element.46) | copy-start | bytes 3538948
  246.0 2.7 %copy-start.2 = (bf16[8,2,128,768]{3,2,1,0:T(8,128)(2,1)S(1)}, bf16[8,2,128,768]{3,2,1,0:T(8,128)(2,1)}, u32[]{:S(2)}) copy-start(bf16[8,2,128,768]{3,2,1,0:T(8,128)(2,1)} %get-tuple-element.52) | copy-start | bytes 9437188
  248.8 7.9 %copy-start.1 = (bf16[8,2,128,768]{3,2,1,0:T(8,128)(2,1)S(1)}, bf16[8,2,128,768]{3,2,1,0:T(8,128)(2,1)}, u32[]{:S(2)}) copy-start(bf16[8,2,128,768]{3,2,1,0:T(8,128)(2,1)} %get-tuple-element.51) | copy-start | bytes 9437188

commit v5 on v4

--- a/solution.py
+++ b/solution.py
@@ -842,8 +842,8 @@
 
 
 class Reduction:
-    def __init__(self, parts, mine, spots, bufs, sems):
-        self.parts, self.mine = parts, mine
+    def __init__(self, away, mine, spots, bufs, sems):
+        self.away, self.mine = away, mine
         self.jobs, self.ahead = [], 3
         self.me, self.t, self.side, self.core = spots
         self.b0, self.b1, self.acc, self.halves, self.got, self.f = bufs
@@ -869,17 +869,10 @@
         return start, inner, size
 
     def first(self, ch):
-        moves = []
-        for y in range(2):
-            at = 0
-            for ref in self.parts(ch, 2 * y + 1 - self.core):
-                rows = pl.ds(at, ref.shape[0])
-                at += ref.shape[0]
-                n = len(moves)
-                moves.append(
-                    remote(ref, self.b0.at[ch, y, rows, :], self.send0, self.recv0, (ch, n), self.near)
-                )
-        return moves
+        return [
+            remote(self.away(ch, y), self.b0.at[ch, y], self.send0, self.recv0, (ch, y), self.near)
+            for y in range(2)
+        ]
 
     def over_y(self, ch):
         return remote(self.mine(ch, 1), self.b1.at[ch], self.send, self.recv, (ch, 0), self.across)
@@ -908,7 +901,7 @@
                 move.start()
         elif s == 1:
             for move in self.first(ch):
-                move.wait_recv()
+                move.wait()
             out = self.mine(ch, 1)
             out[...] = (out[...].astype(full) + self.b0[ch, 1].astype(full)).astype(jnp.bfloat16)
             if ch < self.ahead:
@@ -947,8 +940,6 @@
             self.gather(ch, 0).wait_recv()
 
     def finish(self, ch):
-        for move in self.first(ch):
-            move.wait_send()
         self.over_y(ch).wait_send()
         for level in range(3):
             self.halving(ch, level).wait_send()
@@ -1037,51 +1028,54 @@
 
 
 def tail_kernel(
-    n_dev, q, ko, kf, vo, vf, ids, lse, attn, gat, x, gres, early, gd, gu, go, low, wt_hbm,
+    n_dev, q, ko, kf, vo, vf, ids, lse, attn, gat, x, gres, early, normed, g_ffn, act, g_pre, low, wt_hbm,
     f, out, iout, total,
     load, p2, wt, b0, b1, acc, halves, got, came, dq, own, far, far_in, ig,
     send, recv, send0, recv0, local, x_send, x_recv, r_send, r_recv, r_local, s_send, s_recv,
 ):
     spots = me, t, side, core = place()
-    units, hidden = gd.shape[0] // 4, go.shape[0] // 4
     span, width = q.shape
+    units, hidden = act.shape[1] // 4, width // 4
     rows = f.shape[1]
     n_down = units // rows
-    n_ffn = n_down + gu.shape[0] // rows
+    n_ffn = n_down + width // rows
     count = f.shape[0]
     pairs = width // (2 * HD)
     near = (me, tp_peer(side, core, 1))
 
-    def parts(ch, block):
-        if ch < n_down:
-            return [gd.at[pl.ds(block * units + ch * rows, rows), :]]
-        if ch < n_ffn:
-            return [gu.at[pl.ds((ch - n_down) * rows, rows), pl.ds(block * units, units)]]
-        return [p2.at[block, pl.ds((ch - n_ffn) * rows, rows), :]]
+    def own_rows(ch, block):
+        return p2.at[block, pl.ds((ch - n_ffn) * rows, rows), :]
+
+    def away(ch, y):
+        return halves.at[2 * (ch % 4) + y] if ch < n_ffn else own_rows(ch, 2 * y + 1 - core)
 
     def mine(ch, y):
-        return load.at[ch, y] if ch < n_ffn else parts(ch, 2 * y + core)[0]
-
-    red = Reduction(parts, mine, spots, (b0, b1, acc, halves, got, f), (send, recv, send0, recv0))
+        return load.at[ch, y] if ch < n_ffn else own_rows(ch, 2 * y + core)
+
+    red = Reduction(away, mine, spots, (b0, b1, acc, halves, got, f), (send, recv, send0, recv0))
     back = [
         Return(n, n_dev, src, dst, spots, (r_send, r_recv, r_local))
         for n, (src, dst) in enumerate(((low, out), (ig, iout)))
     ]
     tiny = SmallSum(total, came, spots, (s_send, s_recv))
 
-    def loads(ch):
-        return [
-            pltpu.make_async_copy(parts(ch, 2 * y + core)[0], mine(ch, y), local.at[2 * ch + y])
-            for y in range(2)
-        ]
-
-    def others():
-        pieces = [(wt_hbm, wt)] + [
-            (go.at[pl.ds(j * hidden, hidden), :], p2.at[j, pl.ds(0, hidden), :]) for j in range(4)
-        ]
-        return [
-            pltpu.make_async_copy(a, b, local.at[2 * n_ffn + n]) for n, (a, b) in enumerate(pieces)
-        ]
+    def loads(n):
+        src = (act, g_pre)[n]
+        for j in range(4):
+            dst = (p2.at[j, pl.ds(0, span), :], wt.at[pl.ds(j * span, span), :])[n]
+            yield pltpu.make_async_copy(src.at[:, pl.ds(j * units, units)], dst, local.at[4 * n + j])
+        yield pltpu.make_async_copy((g_ffn, normed)[n], (ig, dq)[n], local.at[9 + n])
+
+    def weights_in():
+        return pltpu.make_async_copy(wt_hbm, wt, local.at[8])
+
+    def ffn_grad(ch, block):
+        if ch < n_down:
+            left, right = p2[block, 0:span, ch * rows : (ch + 1) * rows], ig[...]
+        else:
+            left = dq[:, (ch - n_down) * rows : (ch - n_down + 1) * rows]
+            right = wt[pl.ds(pl.multiple_of(block * span, span), span), :]
+        return plain_dot(left.T, right).astype(jnp.bfloat16)
 
     def swap_far(p, n):
         return remote(far.at[n, p], far_in.at[n, p], x_send, x_recv, (p, n), near)
@@ -1091,21 +1085,25 @@
     back[0].then, back[1].then = partial(red.next_y, count), partial(red.next_y, count + 1)
 
     def begin(ch):
+        for y in range(2):
+            away(ch, y)[...] = ffn_grad(ch, 2 * y + 1 - core)
         red.stage(ch, 0)
-        for move in loads(ch):
+        for y in range(2):
+            load[ch, y] = ffn_grad(ch, 2 * y + core)
+
+    for n in range(2):
+        for move in loads(n):
             move.start()
-
-    def second(ch):
-        for move in loads(ch):
+    greet(all_peers(n_dev, *spots))
+    back[0].stage(0)
+    for n in range(2):
+        for move in loads(n):
             move.wait()
-        red.stage(ch, 1)
-
-    greet(all_peers(n_dev, *spots))
-    for ch in range(n_ffn // 2):
-        begin(ch)
-    back[0].stage(0)
-    for move in others():
-        move.start()
+        for ch in (range(n_down), range(n_down, n_ffn))[n]:
+            if ch >= 4:
+                red.stage(ch - 4, 1)
+            begin(ch)
+    weights_in().start()
 
     def pair(p, carry):
         lanes = pl.ds(pl.multiple_of(p * 2 * HD, 2 * HD), 2 * HD)
@@ -1116,10 +1114,8 @@
 
             @pl.when(p == k)
             def _():
-                for ch in range(k * n_ffn // 2, (k + 1) * n_ffn // 2):
-                    second(ch)
-                for ch in range(n_ffn // 2, (1 - k) * n_ffn):
-                    begin(ch)
+                for ch in range(n_ffn - 4 + 2 * k, n_ffn - 2 + 2 * k):
+                    red.stage(ch, 1)
 
         return carry
 
@@ -1133,8 +1129,8 @@
         cat = jnp.concatenate([far_in[n, p] for p in range(pairs)], 1)
         return (own[n] + cat.astype(jnp.float32)).astype(jnp.bfloat16)
 
-    def weight_grad(low_grad, at):
-        grad = plain_dot(low_grad.T, x[...]).astype(jnp.bfloat16)
+    def weight_grad(left, right, at):
+        grad = plain_dot(left.T, right).astype(jnp.bfloat16)
         for j in range(4):
             p2[j, pl.ds(at * hidden, hidden), :] = grad[j * hidden : (j + 1) * hidden]
 
@@ -1144,16 +1140,15 @@
         return jnp.where(side == 0, sums, turned)
 
     red.stage(0, 2)
-    weight_grad(dq[...], 1)
-    for move in others():
-        move.wait()
+    weight_grad(attn[...], gres[...].astype(jnp.bfloat16), 0)
+    weight_grad(dq[...], x[...], 1)
     red.stage(n_ffn, 0)
     dk = joined_low(0)
-    weight_grad(dk, 2)
+    weight_grad(dk, x[...], 2)
     red.stage(n_ffn + 1, 0)
     red.stage(1, 2)
     dv = joined_low(1)
-    weight_grad(dv, 3)
+    weight_grad(dv, x[...], 3)
     for ch in range(n_ffn + 2, count):
         red.stage(ch, 0)
     red.stage(0, 3)
@@ -1161,7 +1156,8 @@
     total[0, 0:1, :] = column_sum(dq[...])
     total[0, 1:2, :] = column_sum(dv)
     tiny.stage(0)
-    matrix = lambda m: wt[m].reshape(width, width)
+    weights_in().wait()
+    matrix = lambda m: wt[m * width : (m + 1) * width]
     into = gres[...] + plain_dot(dq[...], matrix(0))
     into = into + plain_dot(dk, matrix(1))
     ig[...] = (into + plain_dot(dv, matrix(2))).astype(jnp.bfloat16)
@@ -1177,7 +1173,7 @@
             if (ch, s) not in done:
                 events.append((10 + 8 * (ch + 1) + (0, 10, 18, 26, 34, 42, 51)[s - 2], red, (ch, s)))
     events += [(33 + 7 * n, tiny, (n,)) for n in range(1, 6)]
-    events += [(58, back[1], (1,)), (106, back[0], (2,)), (123, back[1], (2,))]
+    events += [(68, back[1], (1,)), (106, back[0], (2,)), (123, back[1], (2,))]
     for _, who, what in sorted(events, key=lambda e: e[0]):
         who.stage(*what)
     for b in back:
@@ -1228,12 +1224,11 @@
         far[n, p] = grads[1].astype(jnp.bfloat16)
 
 
-def tail(q, ko, kf, vo, vf, ids, lse, attn, gat, x, gres, early, gd, gu, go, low, wt, n_dev):
+def tail(q, ko, kf, vo, vf, ids, lse, attn, gat, x, gres, early, normed, g_ffn, act, g_pre, low, wt, n_dev):
     span, width = q.shape
-    hidden = go.shape[0] // 4
     rows = 256
-    n_ffn = (gd.shape[0] // 4 + gu.shape[0]) // rows
-    count = n_ffn + go.shape[0] // rows
+    n_ffn = (act.shape[1] // 4 + width) // rows
+    count = n_ffn + width // rows
     pairs = width // (2 * HD)
     vmem = pl.BlockSpec(memory_space=pltpu.VMEM)
     hbm = pl.BlockSpec(memory_space=pl.ANY)
@@ -1243,7 +1238,7 @@
     pair_buf = pltpu.VMEM((2, pairs, span, 2 * HD), jnp.bfloat16)
     return pl.pallas_call(
         partial(tail_kernel, n_dev),
-        in_specs=[vmem] * 12 + [hbm] * 5,
+        in_specs=[vmem] * 12 + [hbm] * 6,
         out_specs=[vmem, hbm, hbm, vmem],
         out_shape=[
             jax.ShapeDtypeStruct((count, rows, width), jnp.bfloat16),
@@ -1253,7 +1248,7 @@
         ],
         scratch_shapes=[
             low_buf(n_ffn, 2, rows),
-            low_buf(4, 4 * hidden),
+            low_buf(4, width),
             pltpu.VMEM(wt.shape, jnp.bfloat16),
             low_buf(count, 2, rows),
             low_buf(count, rows),
@@ -1270,7 +1265,7 @@
             dma((count, 7)),
             dma((count, 2)),
             dma((count, 2)),
-            dma((2 * n_ffn + 5,)),
+            dma((11,)),
             dma((pairs, 2)),
             dma((pairs, 2)),
             dma((2, n_dev + 2)),
@@ -1282,7 +1277,7 @@
         compiler_params=pltpu.CompilerParams(
             collective_id=2, has_side_effects=True, vmem_limit_bytes=60 * 2**20
         ),
-    )(q, ko, kf, vo, vf, ids, lse, attn, gat, x, gres, early, gd, gu, go, low, wt)
+    )(q, ko, kf, vo, vf, ids, lse, attn, gat, x, gres, early, normed, g_ffn, act, g_pre, low, wt)
 
 
 def norm_parts(resid):
@@ -1352,15 +1347,12 @@
     )
     g_ffn = g_resid2.astype(jnp.bfloat16)
     grad_downbias = jnp.sum(g_ffn.astype(jnp.float32), 0)
-    grad_down = rows_dot(act_low, g_ffn).astype(jnp.bfloat16)
     g_pre = (back_dot(g_ffn, w_down) * slope.astype(jnp.float32)).astype(jnp.bfloat16)
     grad_upbias = jnp.sum(g_pre.astype(jnp.float32), 0)
-    grad_up = rows_dot(normed_low, g_pre).astype(jnp.bfloat16)
     g_normed = g_resid2 + back_dot(g_pre, w_up)
     g_resid, grad_attngain, grad_attnshift = norm_back(g_normed, unit_one, inverse_one, attn_gain)
     g_branch = g_resid.astype(jnp.bfloat16)
     grad_obias = jnp.sum(g_branch.astype(jnp.float32), 0)
-    grad_o = rows_dot(attn_low, g_branch).astype(jnp.bfloat16)
     g_attn = back_dot(g_branch, wo).astype(jnp.bfloat16)
 
     ups = grad_upbias.reshape(2, 2, units)
@@ -1370,7 +1362,7 @@
     early = jnp.concatenate([late, ups, jnp.stack(lines), late, late], 0)
     sums, layer_output, input_out, small = tail(
         q, k_own, k_far, v_own, v_far, ids, lse, attn_low, g_attn, x, g_resid, early,
-        grad_down, grad_up, grad_o, out_low, wt, n_dev,
+        normed_low, g_ffn, act_low, g_pre, out_low, wt.reshape(3 * width, width), n_dev,
     )
     small = small[5]
 

time: 259 us -> 250 us (0.965)
  matrix products: 29.7 us -> 19.2 us
    dot_general x3 -> x0, matrix products: 11 us -> none  [rows_dot(): lax.dot_general(left, right, (((0,), (0,)), ((), ())), preferred_element_...]
where the time goes in v5:
time: 250 us; the launch traced here: 249 us
  Pallas kernels  204 us (82%)
  matrix products  19.2 us (8%)
  local copies, waits for them, and re-layouts  17.4 us (7%)
  other arithmetic  7.49 us (3%)
    pallas_call x1, Pallas kernels, tail(): pl.pallas_call(partial(tail_kernel, n_dev), in_specs=[vmem] * 12 + [hbm]...  135 us
    pallas_call x1, Pallas kernels, enter(): pl.pallas_call(partial(enter_kernel, n_dev), in_specs=[hbm, hbm, vmem] +...  68.7 us
    dot_general x3, matrix products, back_dot(): lax.dot_general(left, right, (((1,), (1,)), ((), ())), preferred_element_...  9.94 us
    dot_general x3, matrix products, plain_dot(): return jnp.dot(left, right, preferred_element_type=jnp.float32)  9.22 us

profile of v5, /device:TPU:0, one launch (start us, length us, event | category | flops | bytes accessed | tf_op | source)
XLA Modules:
  0.0 249.3 jit_solution(1230976411258280143)
XLA Ops:
  0.7 1.3 broadcast_in_dim.10.ub
  1.9 68.7 %shard_map.305 = (bf16[512,768]{1,0:T(8,128)(2,1)}, bf16[512,768]{1,0:T(8,128)(2,1)}, bf16[512,768]{1,0:T(8,128)(2,1)}, bf16[512,768]{1,0:T(8,128)(2,1)}, bf16[5...) custom-call(bf16[16,128,768]{2,1,0:T(8,128)(2,1)} %tok.1, ...), custom_call_target="tpu_custom_call" | custom-call | tf_op jit(solution)/shard_map/pallas_call | solution.py:750
  70.7 2.8 %fusion.17 = (f32[512]{0:T(512)S(1)}, f32[512,768]{1,0:T(8,128)S(1)}) fusion(f32[768]{0:T(1024)S(1)} %copy-done.15, bf16[512,768]{1,0:T(8,128)(2,1)} %get-tuple-element.43.attn, bf16[768,768]{1,0:T(8,128)(2,1)} %get-tuple-element.46, bf16[512,768]{1,0:T(8,128)(2,1)} %get-tuple-element.45.x), kind=kOutput, calls=%fused_computation.65 | convolution fusion | flops 605552128 | bytes 4330496 | tf_op jit(solution)/shard_map/dot_general | solution.py:53
  74.5 3.7 %multiply_convert_fusion.1 = (bf16[512,3072]{1,0:T(8,128)(2,1)S(1)}, f32[512,3072]{1,0:T(8,128)S(1)}) fusion(f32[3072]{0:T(1024)S(1)} %bitcast.57, bf16[512,768]{1,0:T(8,128)(2,1)S(1)} %fusion.12.normed, bf16[768,3072]{1,0:T(8,128)(2,1)S(1)} %copy-done.12), kind=kOutput, calls=%fused_computation.8 | convolution fusion | flops 2425356288 | bytes 14954496 | tf_op jit(solution)/shard_map/dot_general | solution.py:53
  78.2 2.8 %fusion.18 = (f32[512]{0:T(512)S(1)}, f32[512,768]{1,0:T(8,128)S(1)}) fusion(f32[768]{0:T(1024)S(1)} %copy-done.16, bf16[512,3072]{1,0:T(8,128)(2,1)S(1)} %get-tuple-element.85.act, bf16[3072,768]{1,0:T(8,128)(2,1)S(1)} %bitcast.56, f32[768]{0:T(1024)S(1)} %copy-done.10, f32[768]{0:T(1024)S(1)} %copy-done.9, f32[512]{0:T(512)S(1)} %add_rsqrt_fusion.1, ...), kind=kOutput, calls=%fused_computation.66 | convolution fusion | flops 2418671104 | bytes 11025408 | tf_op jit(solution)/shard_map/dot_general | solution.py:53
  81.4 0.8 copy-done.7
  82.2 0.8 fusion.11
  83.0 1.7 convert_reduce_fusion.2
  84.6 4.9 %convert_reduce_fusion = (f32[3072]{0:T(1024)S(1)}, bf16[512,3072]{1,0:T(8,128)(2,1)S(1)}) fusion(f32[512,3072]{1,0:T(8,128)S(1)} %get-tuple-element.86, f32[3072]{0:T(1024)S(1)} %bitcast.58, bf16[512,768]{1,0:T(8,128)(2,1)S(1)} %get-tuple-element.72.g_ffn, bf16[3072,768]{1,0:T(8,128)(2,1)S(1)} %bitcast.56), kind=kOutput, calls=%fused_computation.6 | convolution fusion | flops 2439508992 | bytes 14966784 | tf_op jit(solution)/shard_map/dot_general | solution.py:63
  89.5 3.4 %multiply_reduce_fusion = (f32[768]{0:T(1024)S(1)}, f32[512]{0:T(512)S(1)}, f32[512]{0:T(512)S(1)}, f32[768]{0:T(1024)S(1)}, f32[512,768]{1,0:T(8,128)S(1)}) fusion(f32[512,768]{1,0:T(8,128)S(1)} %get-tuple-element.84, f32[512]{0:T(512)S(1)} %add_rsqrt_fusion.1, f32[512]{0:T(512)S(1)} %broadcast_multiply_fusion.4, f32[768]{0:T(1024)S(1)} %copy-done.9, ...), kind=kOutput, calls=%fused_computation.23 | convolution fusion | flops 2422994432 | bytes 13398016 | tf_op jit(solution)/shard_map/dot_general | solution.py:63
  92.9 0.5 convert_reduce_fusion.3
  93.6 1.5 concatenate.7.early
  95.1 1.7 convolution_convert_fusion.gat
  96.8 135.5 %shard_map.306 = (bf16[9,256,768]{2,1,0:T(8,128)(2,1)}, bf16[8,2,128,768]{3,2,1,0:T(8,128)(2,1)}, bf16[8,2,128,768]{3,2,1,0:T(8,128)(2,1)}, f32[6,16,768]{2,1,0:T(8,128)}) custom-call(bf16[512,768]{1,0:T(8,128)(2,1)} %get-tuple-element.36.q, bf16[512,768]{1,0:T(8,128)(2,1)} %get-tuple-element.37.ko, bf16[512,768]{1,0:T(8,128)(2,1)} %get-tuple-element.38.kf, ...), custom_call_target="tpu_custom_call" | custom-call | tf_op jit(solution)/shard_map/pallas_call | solution.py:1239
  232.3 4.7 %fusion.16 = (f32[3,256,768]{2,1,0:T(8,128)}, f32[3,256,768]{2,1,0:T(8,128)}, f32[3,256,768]{2,1,0:T(8,128)S(1)}) fusion(bf16[9,256,768]{2,1,0:T(8,128)(2,1)} %get-tuple-element.53), kind=kLoop, calls=%fused_computation.64 | loop fusion | bytes 14155776 | tf_op jit(solution)/shard_map/slice | solution.py:1375
  237.0 1.4 slice_bitcast_fusion
  238.4 1.3 copy-done.6
  239.7 3.6 %bitcast_convert_fusion = f32[16,128,768]{2,1,0:T(8,128)} fusion(bf16[8,2,128,768]{3,2,1,0:T(8,128)(2,1)S(1)} %copy-done.6), kind=kLoop, calls=%fused_computation.10 | loop fusion | flops 1572864 | bytes 9437184 | tf_op jit(solution)/shard_map/reshape | solution.py:1381
  243.3 1.6 slice_reduce_fusion
  245.0 0.6 constant_dynamic-slice_fusion.1
  245.7 0.6 constant_dynamic-slice_fusion
  246.3 0.7 slice.62
  247.0 0.6 dynamic-slice_reduce_fusion
  247.6 1.7 copy.36
  (60 shorter events, 1.6 us)
Async XLA Ops:
  1.9 68.7 %copy-start.15 = (f32[768]{0:T(1024)S(1)}, f32[768]{0:T(1024)}, u32[]{:S(2)}) copy-start(f32[768]{0:T(1024)} %param.26) | copy-start | bytes 9220
  70.7 3.8 %copy-start.12 = (bf16[768,3072]{1,0:T(8,128)(2,1)S(1)}, bf16[768,3072]{1,0:T(8,128)(2,1)}, u32[]{:S(2)}) copy-start(bf16[768,3072]{1,0:T(8,128)(2,1)} %get-tuple-element.47) | copy-start | bytes 14155780
  73.4 0.7 copy-start.9
  73.4 0.7 copy-start.10
  73.8 0.7 copy-start.14
  74.1 4.1 %slice-start = ((s8[4718592]{0:T(1024)(128)(4,1)}), s8[4194304]{0:T(1024)(128)(4,1)S(1)}, s32[]{:S(2)}) async-start(s8[4718592]{0:T(1024)(128)(4,1)} %bitcast.55), calls=%async_computation | async-start | bytes 8388608
  74.5 3.7 %copy-start.1 = (bf16[512,768]{1,0:T(8,128)(2,1)}, bf16[512,768]{1,0:T(8,128)(2,1)S(1)}, u32[]{:S(2)}) copy-start(bf16[512,768]{1,0:T(8,128)(2,1)S(1)} %fusion.12.normed) | copy-start | bytes 2359300
  74.5 3.7 %slice-start.1 = ((s8[4718592]{0:T(1024)(128)(4,1)}), s8[524288]{0:T(1024)(128)(4,1)S(1)}, s32[]{:S(2)}) async-start(s8[4718592]{0:T(1024)(128)(4,1)} %bitcast.55), calls=%async_computation.1 | async-start | bytes 1048576
  74.5 3.7 %copy-start.16 = (f32[768]{0:T(1024)S(1)}, f32[768]{0:T(1024)}, u32[]{:S(2)}) copy-start(f32[768]{0:T(1024)} %param.32) | copy-start | bytes 9220
  78.2 2.9 %copy-start.3 = (bf16[512,3072]{1,0:T(8,128)(2,1)}, bf16[512,3072]{1,0:T(8,128)(2,1)S(1)}, u32[]{:S(2)}) copy-start(bf16[512,3072]{1,0:T(8,128)(2,1)S(1)} %get-tuple-element.85.act) | copy-start | bytes 9437188
  81.1 1.1 copy-start.7
  81.1 1.1 copy-start.8
  81.4 1.6 copy-start.11
  84.6 4.9 %copy-start.2 = (bf16[512,768]{1,0:T(8,128)(2,1)}, bf16[512,768]{1,0:T(8,128)(2,1)S(1)}, u32[]{:S(2)}) copy-start(bf16[512,768]{1,0:T(8,128)(2,1)S(1)} %get-tuple-element.72.g_ffn) | copy-start | bytes 2359300
  89.5 3.4 %copy-start.4 = (bf16[512,3072]{1,0:T(8,128)(2,1)}, bf16[512,3072]{1,0:T(8,128)(2,1)S(1)}, u32[]{:S(2)}) copy-start(bf16[512,3072]{1,0:T(8,128)(2,1)S(1)} %get-tuple-element.91.g_pre) | copy-start | bytes 9437188
  92.9 2.2 copy-start.13
  93.5 3.4 %copy-start = (f32[512,768]{1,0:T(8,128)}, f32[512,768]{1,0:T(8,128)S(1)}, u32[]{:S(2)}) copy-start(f32[512,768]{1,0:T(8,128)S(1)} %get-tuple-element.74.gres) | copy-start | bytes 4718596
  237.0 2.7 %copy-start.6 = (bf16[8,2,128,768]{3,2,1,0:T(8,128)(2,1)S(1)}, bf16[8,2,128,768]{3,2,1,0:T(8,128)(2,1)}, u32[]{:S(2)}) copy-start(bf16[8,2,128,768]{3,2,1,0:T(8,128)(2,1)} %get-tuple-element.52) | copy-start | bytes 9437188
  239.7 7.9 %copy-start.5 = (bf16[8,2,128,768]{3,2,1,0:T(8,128)(2,1)S(1)}, bf16[8,2,128,768]{3,2,1,0:T(8,128)(2,1)}, u32[]{:S(2)}) copy-start(bf16[8,2,128,768]{3,2,1,0:T(8,128)(2,1)} %get-tuple-element.51) | copy-start | bytes 9437188

commit v6 on v5

--- a/solution.py
+++ b/solution.py
@@ -615,7 +615,7 @@
         slot = (bits & 2) + core
         to = tp_peer(side, core, bits)
         moves = (
-            (qb, qbs.at[slot]), (vb, vbs.at[slot]), (ub, ubs.at[slot]),
+            (qbs.at[core], qbs.at[slot]), (vbs.at[core], vbs.at[slot]), (ubs.at[core], ubs.at[slot]),
             (ids_for.at[to], ids.at[pl.ds(slot * heads, heads)]),
         )
         return [
@@ -631,7 +631,8 @@
     for n in range(3):
         own_near(n).start()
         own_here(n).start()
-    qbs[core], vbs[core], ubs[core] = qb[...], vb[...], ub[...]
+    for ref, rows in ((qb, qbs), (vb, vbs), (ub, ubs)):
+        rows[core] = ref[...].reshape(1, ref.shape[0])
     for bits in (1, 2, 3):
         for move in shared(bits, (0, 1, 2)):
             move.start()
@@ -1327,7 +1328,7 @@
         x, q, k_own, k_far, v_own, v_far, attn_low, lse, ids, u_bias, wt, cot, wo, w_up, w_down,
     ) = enter(
         tokens, cotangent, rand_blocks.transpose(2, 3, 0, 1), query_weight.T, key_weight.T, value_weight.T,
-        query_bias[None], value_bias[None], up_bias[None], output_weight, up_weight, down_weight, n_dev,
+        query_bias, value_bias, up_bias, output_weight, up_weight, down_weight, n_dev,
     )
     u_bias = u_bias.reshape(4 * units)
     branch = plain_dot(attn_low, wo) + output_bias

time: 250 us -> 248 us (level)
  no operation moved by 1% of the time
where the time goes in v6:
time: 248 us
  Pallas kernels  204 us (82%)
  matrix products  19.2 us (8%)
  local copies, waits for them, and re-layouts  16.1 us (6%)
  other arithmetic  7.49 us (3%)
    pallas_call x1, Pallas kernels, tail(): pl.pallas_call(partial(tail_kernel, n_dev), in_specs=[vmem] * 12 + [hbm]...  135 us
    pallas_call x1, Pallas kernels, enter(): pl.pallas_call(partial(enter_kernel, n_dev), in_specs=[hbm, hbm, vmem] +...  68.8 us
    dot_general x3, matrix products, back_dot(): lax.dot_general(left, right, (((1,), (1,)), ((), ())), preferred_element_...  9.94 us
    dot_general x3, matrix products, plain_dot(): return jnp.dot(left, right, preferred_element_type=jnp.float32)  9.23 us

profile of v6, /device:TPU:0, one launch (start us, length us, event | category | flops | bytes accessed | tf_op | source)
XLA Modules:
  0.0 248.0 jit_solution(10608721530931362970)
XLA Ops:
  0.7 68.8 %shard_map.305 = (bf16[512,768]{1,0:T(8,128)(2,1)}, bf16[512,768]{1,0:T(8,128)(2,1)}, bf16[512,768]{1,0:T(8,128)(2,1)}, bf16[512,768]{1,0:T(8,128)(2,1)}, bf16[5...) custom-call(bf16[16,128,768]{2,1,0:T(8,128)(2,1)} %tok.1, ...), custom_call_target="tpu_custom_call" | custom-call | tf_op jit(solution)/shard_map/pallas_call | solution.py:751
  69.5 2.8 %fusion.17 = (f32[512]{0:T(512)S(1)}, f32[512,768]{1,0:T(8,128)S(1)}) fusion(f32[768]{0:T(1024)S(1)} %copy-done.15, bf16[512,768]{1,0:T(8,128)(2,1)} %get-tuple-element.43.attn, bf16[768,768]{1,0:T(8,128)(2,1)} %get-tuple-element.46, bf16[512,768]{1,0:T(8,128)(2,1)} %get-tuple-element.45.x), kind=kOutput, calls=%fused_computation.65 | convolution fusion | flops 605552128 | bytes 4330496 | tf_op jit(solution)/shard_map/dot_general | solution.py:53
  72.6 0.3 copy-done.9
  73.3 3.7 %multiply_convert_fusion.1 = (bf16[512,3072]{1,0:T(8,128)(2,1)S(1)}, f32[512,3072]{1,0:T(8,128)S(1)}) fusion(f32[3072]{0:T(1024)S(1)} %bitcast.53, bf16[512,768]{1,0:T(8,128)(2,1)S(1)} %fusion.12.normed, bf16[768,3072]{1,0:T(8,128)(2,1)S(1)} %copy-done.12), kind=kOutput, calls=%fused_computation.8 | convolution fusion | flops 2425356288 | bytes 14954496 | tf_op jit(solution)/shard_map/dot_general | solution.py:53
  77.0 2.8 %fusion.18 = (f32[512]{0:T(512)S(1)}, f32[512,768]{1,0:T(8,128)S(1)}) fusion(f32[768]{0:T(1024)S(1)} %copy-done.16, bf16[512,3072]{1,0:T(8,128)(2,1)S(1)} %get-tuple-element.85.act, bf16[3072,768]{1,0:T(8,128)(2,1)S(1)} %bitcast.52, f32[768]{0:T(1024)S(1)} %copy-done.10, f32[768]{0:T(1024)S(1)} %copy-done.9, f32[512]{0:T(512)S(1)} %add_rsqrt_fusion.1, ...), kind=kOutput, calls=%fused_computation.66 | convolution fusion | flops 2418671104 | bytes 11025408 | tf_op jit(solution)/shard_map/dot_general | solution.py:53
  80.2 0.8 copy-done.7
  81.0 0.8 fusion.11
  81.8 1.7 convert_reduce_fusion.2
  83.4 4.9 %convert_reduce_fusion = (f32[3072]{0:T(1024)S(1)}, bf16[512,3072]{1,0:T(8,128)(2,1)S(1)}) fusion(f32[512,3072]{1,0:T(8,128)S(1)} %get-tuple-element.86, f32[3072]{0:T(1024)S(1)} %bitcast.54, bf16[512,768]{1,0:T(8,128)(2,1)S(1)} %get-tuple-element.72.g_ffn, bf16[3072,768]{1,0:T(8,128)(2,1)S(1)} %bitcast.52), kind=kOutput, calls=%fused_computation.6 | convolution fusion | flops 2439508992 | bytes 14966784 | tf_op jit(solution)/shard_map/dot_general | solution.py:63
  88.3 3.4 %multiply_reduce_fusion = (f32[768]{0:T(1024)S(1)}, f32[512]{0:T(512)S(1)}, f32[512]{0:T(512)S(1)}, f32[768]{0:T(1024)S(1)}, f32[512,768]{1,0:T(8,128)S(1)}) fusion(f32[512,768]{1,0:T(8,128)S(1)} %get-tuple-element.84, f32[512]{0:T(512)S(1)} %add_rsqrt_fusion.1, f32[512]{0:T(512)S(1)} %broadcast_multiply_fusion.4, f32[768]{0:T(1024)S(1)} %copy-done.9, ...), kind=kOutput, calls=%fused_computation.23 | convolution fusion | flops 2422994432 | bytes 13398016 | tf_op jit(solution)/shard_map/dot_general | solution.py:63
  91.7 0.5 convert_reduce_fusion.3
  92.4 1.5 concatenate.7.early
  93.9 1.7 convolution_convert_fusion.gat
  95.6 135.5 %shard_map.306 = (bf16[9,256,768]{2,1,0:T(8,128)(2,1)}, bf16[8,2,128,768]{3,2,1,0:T(8,128)(2,1)}, bf16[8,2,128,768]{3,2,1,0:T(8,128)(2,1)}, f32[6,16,768]{2,1,0:T(8,128)}) custom-call(bf16[512,768]{1,0:T(8,128)(2,1)} %get-tuple-element.36.q, bf16[512,768]{1,0:T(8,128)(2,1)} %get-tuple-element.37.ko, bf16[512,768]{1,0:T(8,128)(2,1)} %get-tuple-element.38.kf, ...), custom_call_target="tpu_custom_call" | custom-call | tf_op jit(solution)/shard_map/pallas_call | solution.py:1240
  231.1 4.7 %fusion.16 = (f32[3,256,768]{2,1,0:T(8,128)}, f32[3,256,768]{2,1,0:T(8,128)}, f32[3,256,768]{2,1,0:T(8,128)S(1)}) fusion(bf16[9,256,768]{2,1,0:T(8,128)(2,1)} %get-tuple-element.53), kind=kLoop, calls=%fused_computation.64 | loop fusion | bytes 14155776 | tf_op jit(solution)/shard_map/slice | solution.py:1376
  235.8 1.4 slice_bitcast_fusion
  237.2 1.3 copy-done.6
  238.5 3.6 %bitcast_convert_fusion = f32[16,128,768]{2,1,0:T(8,128)} fusion(bf16[8,2,128,768]{3,2,1,0:T(8,128)(2,1)S(1)} %copy-done.6), kind=kLoop, calls=%fused_computation.10 | loop fusion | flops 1572864 | bytes 9437184 | tf_op jit(solution)/shard_map/reshape | solution.py:1382
  242.1 1.6 slice_reduce_fusion
  243.8 0.6 constant_dynamic-slice_fusion.1
  244.5 0.6 constant_dynamic-slice_fusion
  245.0 0.7 slice.62
  245.8 0.6 dynamic-slice_reduce_fusion
  246.4 1.7 copy.36
  (59 shorter events, 1.3 us)
Async XLA Ops:
  0.7 68.8 %copy-start.15 = (f32[768]{0:T(1024)S(1)}, f32[768]{0:T(1024)}, u32[]{:S(2)}) copy-start(f32[768]{0:T(1024)} %param.26) | copy-start | bytes 9220
  69.4 3.8 %copy-start.12 = (bf16[768,3072]{1,0:T(8,128)(2,1)S(1)}, bf16[768,3072]{1,0:T(8,128)(2,1)}, u32[]{:S(2)}) copy-start(bf16[768,3072]{1,0:T(8,128)(2,1)} %get-tuple-element.47) | copy-start | bytes 14155780
  72.2 0.7 copy-start.9
  72.2 0.7 copy-start.10
  72.5 0.7 copy-start.14
  72.9 4.1 %slice-start = ((s8[4718592]{0:T(1024)(128)(4,1)}), s8[4194304]{0:T(1024)(128)(4,1)S(1)}, s32[]{:S(2)}) async-start(s8[4718592]{0:T(1024)(128)(4,1)} %bitcast.51), calls=%async_computation | async-start | bytes 8388608
  73.2 3.7 %copy-start.1 = (bf16[512,768]{1,0:T(8,128)(2,1)}, bf16[512,768]{1,0:T(8,128)(2,1)S(1)}, u32[]{:S(2)}) copy-start(bf16[512,768]{1,0:T(8,128)(2,1)S(1)} %fusion.12.normed) | copy-start | bytes 2359300
  73.3 3.7 %slice-start.1 = ((s8[4718592]{0:T(1024)(128)(4,1)}), s8[524288]{0:T(1024)(128)(4,1)S(1)}, s32[]{:S(2)}) async-start(s8[4718592]{0:T(1024)(128)(4,1)} %bitcast.51), calls=%async_computation.1 | async-start | bytes 1048576
  73.3 3.7 %copy-start.16 = (f32[768]{0:T(1024)S(1)}, f32[768]{0:T(1024)}, u32[]{:S(2)}) copy-start(f32[768]{0:T(1024)} %param.32) | copy-start | bytes 9220
  77.0 2.9 %copy-start.3 = (bf16[512,3072]{1,0:T(8,128)(2,1)}, bf16[512,3072]{1,0:T(8,128)(2,1)S(1)}, u32[]{:S(2)}) copy-start(bf16[512,3072]{1,0:T(8,128)(2,1)S(1)} %get-tuple-element.85.act) | copy-start | bytes 9437188
  79.8 1.1 copy-start.7
  79.8 1.1 copy-start.8
  80.2 1.6 copy-start.11
  83.4 4.9 %copy-start.2 = (bf16[512,768]{1,0:T(8,128)(2,1)}, bf16[512,768]{1,0:T(8,128)(2,1)S(1)}, u32[]{:S(2)}) copy-start(bf16[512,768]{1,0:T(8,128)(2,1)S(1)} %get-tuple-element.72.g_ffn) | copy-start | bytes 2359300
  88.3 3.4 %copy-start.4 = (bf16[512,3072]{1,0:T(8,128)(2,1)}, bf16[512,3072]{1,0:T(8,128)(2,1)S(1)}, u32[]{:S(2)}) copy-start(bf16[512,3072]{1,0:T(8,128)(2,1)S(1)} %get-tuple-element.91.g_pre) | copy-start | bytes 9437188
  91.7 2.2 copy-start.13
  92.2 3.4 %copy-start = (f32[512,768]{1,0:T(8,128)}, f32[512,768]{1,0:T(8,128)S(1)}, u32[]{:S(2)}) copy-start(f32[512,768]{1,0:T(8,128)S(1)} %get-tuple-element.74.gres) | copy-start | bytes 4718596
  235.8 2.7 %copy-start.6 = (bf16[8,2,128,768]{3,2,1,0:T(8,128)(2,1)S(1)}, bf16[8,2,128,768]{3,2,1,0:T(8,128)(2,1)}, u32[]{:S(2)}) copy-start(bf16[8,2,128,768]{3,2,1,0:T(8,128)(2,1)} %get-tuple-element.52) | copy-start | bytes 9437188
  238.5 7.9 %copy-start.5 = (bf16[8,2,128,768]{3,2,1,0:T(8,128)(2,1)S(1)}, bf16[8,2,128,768]{3,2,1,0:T(8,128)(2,1)}, u32[]{:S(2)}) copy-start(bf16[8,2,128,768]{3,2,1,0:T(8,128)(2,1)} %get-tuple-element.51) | copy-start | bytes 9437188
